TPU v7x, 512 devices: a whole 4x4x16 slice. The times are simulated.
512 devices in a mesh: grp: 16 (over z_lo, core), xy: 32 (over x, y, z_hi).
Axes of the slice: x: 4, y: 4, z: 16 (z_hi: 2, z_lo: 8; z = z_hi * 8 + z_lo), core: 2. Of those that a mesh axis runs over, the one named last changes fastest.
Arguments:
- activations: bfloat16 [64, 512, 32, 128], P(None, ('grp', 'xy')), may hold values from -6 to 6
- cotangent: bfloat16 [64, 64, 32, 128], P(None, 'grp', 'xy'), may hold values from -6 to 6
- weight: bfloat16 [9, 64, 64], replicated, may hold values from -0.25 to 0.25
- conv_bias: float32 [64], replicated, may hold values from -3 to 3
- blur_taps: float32 [9], replicated, may hold values from 0.1 to 1
Outputs:
- grad_input: bfloat16 [64, 512, 32, 128], P(None, ('grp', 'xy'))
- grad_weight: float32 [9, 64, 64], replicated
- grad_bias: float32 [64], replicated
All inputs are finite; a program needn't handle non-finite values.
Results may differ from a plain program's by a relative error of at most 0.0052.
Values may be sent and summed in bfloat16 or wider, within the bound.
No kernel may reach another device: no remote copies, remote signals or barrier semaphores. Data moves between devices by JAX's collectives and lax.ppermute only.
A program may use at most 64 MiB of HBM per device.

v0:
```python
import jax
import jax.numpy as jnp
from jax import lax
from jax.sharding import PartitionSpec as P

R = 8


def passed_along(value, axis, steps):
    count = lax.axis_size(axis)
    leading, last = (max(0, -steps), min(count, count - steps))
    return lax.ppermute(value, axis, [(source, source + steps) for source in range(leading, last)])


def tap_weights(planes, centers, blur_taps):
    tap_count = blur_taps.shape[0]
    taps_index = planes[:, None] - centers[None, :] + tap_count // 2
    onehot = taps_index[:, :, None] == jnp.arange(tap_count, dtype=jnp.int32)[None, None, :]
    return jnp.sum(jnp.where(onehot, blur_taps[None, None, :], 0.0), axis=2)


def forward_taps(volume, weight):
    channels, planes, rows, cols = volume.shape
    padded = jnp.pad(volume, ((0, 0), (0, 0), (1, 1), (1, 1)))
    summed = jnp.zeros((channels, planes * rows * cols), jnp.float32)
    for offset in range(9):
        row_off = offset // 3
        col_off = offset % 3
        shifted = padded[:, :, row_off : row_off + rows, col_off : col_off + cols].reshape(
            channels, -1
        )
        summed = summed + jnp.dot(weight[offset], shifted, preferred_element_type=jnp.float32)
    return summed


def backward_taps(volume, grad_hidden, weight):
    channels, planes, rows, cols = volume.shape
    padded_in = jnp.pad(volume, ((0, 0), (0, 0), (1, 1), (1, 1)))
    padded_grad = jnp.pad(grad_hidden, ((0, 0), (0, 0), (1, 1), (1, 1)))
    grad_flat = grad_hidden.reshape(channels, -1)
    summed = jnp.zeros((channels, planes * rows * cols), jnp.float32)
    grad_list = []
    for offset in range(9):
        row_off = offset // 3
        col_off = offset % 3
        shifted_in = padded_in[:, :, row_off : row_off + rows, col_off : col_off + cols].reshape(
            channels, -1
        )
        grad_list.append(
            lax.dot_general(
                grad_flat, shifted_in, (((1,), (1,)), ((), ())), preferred_element_type=jnp.float32
            )
        )
        shifted_grad = padded_grad[
            :, :, 2 - row_off : 2 - row_off + rows, 2 - col_off : 2 - col_off + cols
        ].reshape(channels, -1)
        summed = summed + jnp.dot(
            weight[offset].T, shifted_grad, preferred_element_type=jnp.float32
        )
    return (jnp.stack(grad_list, 0), summed)


def layer_backward(volume, g_out, weight, conv_bias):
    channels = volume.shape[0]
    hidden = forward_taps(volume, weight) + conv_bias[:, None]
    sigmoid_h = jax.nn.sigmoid(hidden)
    slope_h = sigmoid_h * (1.0 + hidden * (1.0 - sigmoid_h))
    grad_flat = g_out.reshape(channels, -1).astype(jnp.float32)
    grad_hidden = (grad_flat * slope_h).astype(jnp.bfloat16)
    grad_w, grad_conv = backward_taps(volume, grad_hidden.reshape(volume.shape), weight)
    grad_bias = jnp.sum(grad_hidden.astype(jnp.float32), axis=1)
    grad_input = (grad_flat + grad_conv).reshape(volume.shape).astype(jnp.bfloat16)
    return (grad_input, grad_w, grad_bias)


def on_device(activations, cotangent, weight, conv_bias, blur_taps):
    channels, slab_planes, rows, cols = activations.shape
    xy_count = lax.axis_size("xy")
    coarse_count = cotangent.shape[1]
    earlier = passed_along(cotangent[:, coarse_count - 1 :], "grp", 1)
    extended = jnp.concatenate([earlier, cotangent], axis=1)
    centers = R * (jnp.arange(coarse_count + 1, dtype=jnp.int32) - 1) + R // 2
    group_planes = jnp.arange(coarse_count * R, dtype=jnp.int32)
    mixing = tap_weights(group_planes, centers, blur_taps)
    dense_field = jnp.einsum(
        "ze,ceyx->czyx", mixing, extended.astype(jnp.float32), precision=lax.Precision.HIGHEST
    ).astype(jnp.bfloat16)
    g_out = lax.all_to_all(dense_field, "xy", split_axis=1, concat_axis=2, tiled=True)
    grad_input, grad_w, grad_bias = layer_backward(activations, g_out, weight, conv_bias)
    grad_w, grad_bias = lax.psum((grad_w, grad_bias), ("grp", "xy"))
    factor = float(slab_planes * rows * cols * lax.axis_size("grp") * xy_count) ** (-0.5)
    return (grad_input, grad_w * factor, grad_bias * factor)


def solution(mesh):
    in_specs = (P(None, ("grp", "xy"), None, None), P(None, "grp", "xy", None), P(), P(), P())
    out_specs = (P(None, ("grp", "xy"), None, None), P(), P())
    return jax.shard_map(
        on_device, mesh=mesh, in_specs=in_specs, out_specs=out_specs, check_vma=False
    )
```

profile of v0, /device:TPU:1, one launch (start us, length us, event | category | flops | bytes accessed | tf_op | source)
XLA Modules:
  0.0 650.0 jit_solution(4405214585588789270)
XLA Ops:
  7.2 0.9 slice.124
  8.0 4.9 collective-permute-start
  13.0 0.1 subtract_add_fusion
  13.1 5.8 pad_slice_fusion.12
  18.9 0.0 copy-done.16
  18.9 0.0 copy-start
  18.9 0.1 select_reduce_fusion
  19.0 0.0 collective-permute-done
  19.0 0.0 copy-done.15
  19.0 0.6 fusion.9
  19.6 0.0 copy-start.12
  19.7 1.0 copy.18
  20.7 19.5 %all-to-all-start = ((bf16[64,32,1,128]{3,0,2,1:T(8,128)(2,1)}), bf16[64,32,1,128]{3,0,2,1:T(8,128)(2,1)}, u32[]{:S(2)}, u32[]{:S(2)}) async-start(bf16[64,32,1,128]{3,0,2,1:T(8,128)(2,1)} %copy.18), calls=%async_computation | async-start | bytes 1048576 | tf_op jit(solution)/shard_map/all_to_all | solution.py:88
  40.2 0.0 all-reduce.4.cloned.1.call-start
  40.2 0.0 copy-done.12
  40.3 1.3 convolution_bitcast_fusion.3
  41.6 1.3 convolution_bitcast_fusion.2
  42.8 1.3 convolution_bitcast_fusion.1
  44.1 1.3 convolution_bitcast_fusion
  45.4 0.3 fusion.55
  45.7 0.7 copy-done.4
  46.5 0.3 convolution_add_fusion.2
  46.8 0.3 convolution_add_fusion.1
  47.1 0.0 copy-done
  47.1 1.3 fusion.7
  48.4 13.5 %all-to-all-done = bf16[64,32,1,128]{3,0,2,1:T(8,128)(2,1)} async-done(((bf16[64,32,1,128]{3,0,2,1:T(8,128)(2,1)}), bf16[64,32,1,128]{3,0,2,1:T(8,128)(2,1)}, u32[]{:S(2)}, u32[]{:S(2)}) %all-to-all-start) | async-done | bytes 524320 | tf_op jit(solution)/shard_map/all_to_all | solution.py:88
  61.9 1.5 copy.19
  63.4 0.0 copy-done.17
  63.4 0.0 copy-done.11
  63.4 0.0 copy-done.13
  63.4 3.4 convert_reduce_fusion
  66.9 0.0 copy-start.5
  66.9 0.4 fusion.19
  67.3 0.8 copy-done.5
  68.1 0.4 fusion.18
  68.5 0.0 copy-done.3
  68.5 0.4 fusion.17
  68.9 0.3 copy-done.1
  69.2 0.4 fusion.16
  69.6 0.0 copy-start.14
  69.6 0.7 copy-done.14
  70.3 115.2 %psum.15 = f32[64]{0:T(128)S(1)} all-reduce(f32[64]{0:T(128)S(1)} %get-tuple-element.28), channel_id=1, replica_groups=mesh['grp'=16,'xy'=32] {'grp','xy'}, use_global_device_ids=true, to_apply=%region_3.4 | all-reduce | flops 64 | bytes 512 | tf_op jit(solution)/shard_map/psum | solution.py:90
  185.5 0.5 broadcast_multiply_fusion.1
  186.0 2.2 fusion.15
  188.2 0.0 copy-done.9
  188.2 1.0 fusion.14
  189.2 1.0 fusion.13
  190.2 1.0 fusion.12
  191.3 1.0 fusion.11
  192.3 0.0 all-reduce.4.cloned.1.call-update
  192.3 0.1 copy.31
  192.4 1.6 pad_slice_fusion
  194.0 0.3 fusion.35
  194.3 0.3 convolution_add_fusion.10
  194.7 0.3 convolution_add_fusion.9
  195.0 0.3 convolution_add_fusion.8
  195.4 0.3 convolution_add_fusion.7
  195.7 0.3 convolution_add_fusion.6
  196.1 0.3 convolution_add_fusion.5
  196.5 0.3 convolution_add_fusion.4
  196.8 0.9 fusion.10
  197.7 0.9 copy.40
  198.6 442.9 %all-reduce.4.cloned.1.call-done = f32[9,64,64]{2,1,0:T(8,128)} async-done(((f32[9,64,64]{2,1,0:T(8,128)}), f32[9,64,64]{2,1,0:T(8,128)}) %all-reduce.4.cloned.1.call-update) | async-done | bytes 147472 | tf_op jit(solution)/shard_map/psum | solution.py:90
  641.5 1.7 broadcast_multiply_fusion
  (20 shorter events, 0.0 us)
Async XLA Ops:
  8.0 11.0 %collective-permute-start = (bf16[64,1,1,128]{3,1,0,2:T(2,128)(2,1)S(1)}, bf16[64,1,1,128]{3,1,0,2:T(2,128)(2,1)S(1)}, u32[]{:S(2)}, u32[]{:S(2)}) collective-permute-start(bf16[64,1,1,128]{3,1,0,2:T(2,128)(2,1)S(1)} %slice.124), channel_id=1, source_target_pairs={{0,32},{32,64},{64,96},{96,128},{128,160},{160,192},{192,224},{224... | collective-permute-start | bytes 49160 | tf_op jit(solution)/shard_map/ppermute | solution.py:12
  13.1 5.8 copy-start.16
  13.1 5.9 copy-start.15
  18.9 27.9 %copy-start.2 = (bf16[64,1,32,128]{3,2,1,0:T(8,128)(2,1)}, bf16[64,1,32,128]{3,2,1,0:T(8,128)(2,1)S(1)}, u32[]{:S(2)}) copy-start(bf16[64,1,32,128]{3,2,1,0:T(8,128)(2,1)S(1)} %get-tuple-element.22) | copy-start | bytes 1572868
  18.9 28.2 %copy-start = (bf16[64,1,32,128]{3,2,1,0:T(8,128)(2,1)}, bf16[64,1,32,128]{3,2,1,0:T(8,128)(2,1)S(1)}, u32[]{:S(2)}) copy-start(bf16[64,1,32,128]{3,2,1,0:T(8,128)(2,1)S(1)} %get-tuple-element.20) | copy-start | bytes 1572868
  19.6 20.6 %copy-start.12 = (bf16[9,64,64]{2,1,0:T(8,128)(2,1)S(1)}, bf16[9,64,64]{2,1,0:T(8,128)(2,1)}, u32[]{:S(2)}) copy-start(bf16[9,64,64]{2,1,0:T(8,128)(2,1)} %param.7) | copy-start | bytes 221188
  20.7 41.2 %all-to-all-start = ((bf16[64,32,1,128]{3,0,2,1:T(8,128)(2,1)}), bf16[64,32,1,128]{3,0,2,1:T(8,128)(2,1)}, u32[]{:S(2)}, u32[]{:S(2)}) async-start(bf16[64,32,1,128]{3,0,2,1:T(8,128)(2,1)} %copy.18), calls=%async_computation | async-start | bytes 1048576 | tf_op jit(solution)/shard_map/all_to_all | solution.py:88
  40.2 601.3 %all-reduce.4.cloned.1.call-start = ((), (), s32[]{:S(2)}) async-start(), calls=%async_computation.1 | async-start | bytes 589824 | tf_op jit(solution)/shard_map/psum | solution.py:90
  44.1 1.3 copy-start.6
  45.4 1.0 copy-start.4
  48.4 15.0 %copy-start.17 = (f32[64]{0:T(128)S(1)}, f32[64]{0:T(128)}, u32[]{:S(2)}) copy-start(f32[64]{0:T(128)} %param.8) | copy-start | bytes 772
  61.9 1.5 copy-start.11
  61.9 1.5 copy-start.13
  63.4 3.5 copy-start.7
  66.9 2.0 copy-start.8
  66.9 1.2 copy-start.5
  66.9 1.6 copy-start.3
  68.1 1.1 copy-start.1
  69.6 0.7 copy-start.14
  185.5 2.7 copy-start.9
  190.2 2.0 copy-start.10
Sparse Core Ops, SparseCore 0:
  192.4 449.0 all-reduce.3
where the time goes:
time: 651 us; the launch traced here: 650 us
  waiting for transfers between devices  456 us (70%)
  blocking collectives  115 us (18%)
  starting transfers between devices  24.5 us (4%)
  matrix products  22.8 us (4%)
  between operations  14.4 us (2%)
  local copies, waits for them, and re-layouts  14.3 us (2%)
    psum x1, waiting for transfers between devices, on_device(): grad_w, grad_bias = lax.psum((grad_w, grad_bias), ('grp', 'xy'))  443 us
    psum x1, blocking collectives, on_device(): grad_w, grad_bias = lax.psum((grad_w, grad_bias), ('grp', 'xy'))  115 us
    all_to_all x1, starting transfers between devices, on_device(): lax.all_to_all(dense_field, 'xy', split_axis=1, concat_axis=2, tiled=True)  19.5 us
    all_to_all x1, waiting for transfers between devices, on_device(): lax.all_to_all(dense_field, 'xy', split_axis=1, concat_axis=2, tiled=True)  13.5 us
  transfers between devices with their start and end apart: 3, of which 2 were waited for; matrix products, arithmetic and copies ran while one was open for 3% of the time, Pallas kernels for 0%

commit v1 on v0

v1 whole, which is shorter than its diff:
```python
import jax
import jax.numpy as jnp
from jax import lax
from jax.experimental import pallas as pl
from jax.experimental.pallas import tpu as pltpu
from jax.sharding import Mesh
from jax.sharding import PartitionSpec as P

R = 8
C = 64
Y = 32
X = 128
AXES = ("zl", "core", "x", "y", "zh")
SIZES = (8, 2, 4, 4, 2)
GROUP = ("zl", "core")
PLANE = ("x", "y", "zh")
FLAT = ("core", "x", "y")
COLUMN = ("zl", "zh")
N_FLAT = 32
N_COLUMN = 16
PIECE = 8
WIDE = 256
VMEM_LIMIT = 48 * 1024 * 1024


def shifted(row, step):
    if step == 0:
        return row
    lane = lax.broadcasted_iota(jnp.int32, row.shape, 1)
    edge = 0 if step < 0 else X - 1
    return jnp.where(lane == edge, 0.0, pltpu.roll(row, (-step) % X, 1))


def forward_kernel(act_ref, mix_ref, bias_ref, slope_ref, turned_ref, stack, hidden):
    column = lax.broadcasted_iota(jnp.int32, (X, WIDE - 3 * C), 1)
    ones = jnp.where(column == 0, 1.0, 0.0).astype(jnp.bfloat16)

    def spread(y, carry):
        row = act_ref[y].astype(jnp.float32)
        at = pl.ds(pl.multiple_of(y * X, X), X)
        whole = jnp.concatenate([shifted(row, b - 1) for b in range(3)], axis=0)
        stack[:, at] = whole.astype(jnp.bfloat16)
        turned_ref[at, : 3 * C] = whole.T.astype(jnp.bfloat16)
        turned_ref[at, 3 * C :] = ones
        return carry

    lax.fori_loop(0, Y, spread, 0)
    hidden[...] = jnp.broadcast_to(bias_ref[...], hidden.shape)

    def taps(j, carry):
        at = pl.multiple_of(j * 2 * X, 2 * X)
        part = jnp.dot(
            mix_ref[...], stack[:, pl.ds(at, 2 * X)], preferred_element_type=jnp.float32
        )
        for a in range(3):
            place = pl.ds(pl.multiple_of(at + (2 - a) * X, X), 2 * X)
            hidden[:, place] += part[a * C : (a + 1) * C]
        return carry

    lax.fori_loop(0, Y // 2, taps, 0)

    def slopes(y, carry):
        h = hidden[:, pl.ds(pl.multiple_of((y + 1) * X, X), X)]
        s = jax.nn.sigmoid(h)
        slope_ref[y] = s * (1.0 + h * (1.0 - s))
        return carry

    lax.fori_loop(0, Y, slopes, 0)


def weight_kernel(g_ref, slope_ref, turned_ref, grad_ref, sums_ref, stack):
    zero = jnp.zeros((C, X), jnp.bfloat16)
    stack[0:C, (Y - 1) * X :] = zero
    stack[2 * C :, 0:X] = zero
    for y in range(Y):
        grad = (g_ref[y].astype(jnp.float32) * slope_ref[y]).astype(jnp.bfloat16)
        grad_ref[y] = grad
        for a in range(3):
            row = y + a - 1
            if 0 <= row < Y:
                stack[a * C : (a + 1) * C, row * X : (row + 1) * X] = grad
    total = jnp.zeros((3 * C, WIDE), jnp.float32)
    for j in range(Y // 2):
        at = slice(j * 2 * X, (j + 1) * 2 * X)
        total += jnp.dot(stack[:, at], turned_ref[at, :], preferred_element_type=jnp.float32)
    sums_ref[: 3 * C // PIECE] = total.reshape(3 * C // PIECE, PIECE, WIDE)
    bias = total[C : 2 * C, 3 * C : 3 * C + 1]
    diagonal = lax.broadcasted_iota(jnp.int32, (C, WIDE), 0) == lax.broadcasted_iota(
        jnp.int32, (C, WIDE), 1
    )
    row = jnp.sum(jnp.where(diagonal, bias, 0.0), axis=0, keepdims=True)
    first = lax.broadcasted_iota(jnp.int32, (PIECE, WIDE), 0) == 0
    sums_ref[3 * C // PIECE] = jnp.where(first, row, 0.0)
    sums_ref[3 * C // PIECE + 1 :] = jnp.zeros(
        (N_FLAT - 3 * C // PIECE - 1, PIECE, WIDE), jnp.float32
    )


def input_kernel(grad_ref, g_ref, mix_ref, out_ref, stack, total):
    total[...] = jnp.zeros_like(total)

    def spread(y, carry):
        row = grad_ref[y].astype(jnp.float32)
        at = pl.ds(pl.multiple_of(y * X, X), X)
        whole = jnp.concatenate([shifted(row, 1 - b) for b in range(3)], axis=0)
        stack[:, at] = whole.astype(jnp.bfloat16)
        return carry

    lax.fori_loop(0, Y, spread, 0)

    def taps(j, carry):
        at = pl.multiple_of(j * 2 * X, 2 * X)
        part = jnp.dot(
            mix_ref[...], stack[:, pl.ds(at, 2 * X)], preferred_element_type=jnp.float32
        )
        for a in range(3):
            place = pl.ds(pl.multiple_of(at + a * X, X), 2 * X)
            total[:, place] += part[a * C : (a + 1) * C]
        return carry

    lax.fori_loop(0, Y // 2, taps, 0)

    def finish(y, carry):
        conv = total[:, pl.ds(pl.multiple_of((y + 1) * X, X), X)]
        out_ref[y] = (g_ref[y].astype(jnp.float32) + conv).astype(jnp.bfloat16)
        return carry

    lax.fori_loop(0, Y, finish, 0)


def spread_sum_kernel(parts_ref, out_ref):
    total = jnp.sum(parts_ref[...], axis=0)
    for copy in range(out_ref.shape[0]):
        out_ref[copy] = total


def scaled_sum_kernel(factor, parts_ref, out_ref):
    total = jnp.sum(parts_ref[...], axis=0) * factor
    for copy in range(out_ref.shape[0]):
        out_ref[copy] = total


def call(kernel, outs, scratch, flops, moved, *args):
    return pl.pallas_call(
        kernel,
        out_shape=outs,
        in_specs=[pl.BlockSpec(memory_space=pltpu.VMEM)] * len(args),
        out_specs=jax.tree.map(lambda _: pl.BlockSpec(memory_space=pltpu.VMEM), outs),
        scratch_shapes=scratch,
        compiler_params=pltpu.CompilerParams(vmem_limit_bytes=VMEM_LIMIT),
        cost_estimate=pl.CostEstimate(flops=flops, bytes_accessed=moved, transcendentals=0),
    )(*args)


def on_device(activations, cotangent, weight, conv_bias, blur_taps):
    shape = jax.ShapeDtypeStruct
    bf16, f32 = jnp.bfloat16, jnp.float32
    groups = 16
    coarse = cotangent[:, :, 0, :].transpose(1, 0, 2)
    hops = [(g, g + 1) for g in range(groups - 1)]
    earlier = lax.ppermute(coarse[3:], GROUP, hops)
    before = jnp.concatenate([earlier, coarse[:3]], axis=0)
    first = (jnp.arange(R) == 0)[None, :, None, None]
    field = blur_taps[:R][None, :, None, None] * coarse.astype(f32)[:, None]
    field = field + jnp.where(first, blur_taps[R] * before.astype(f32)[:, None], 0.0)
    field = field.astype(bf16).reshape(Y, C, X)
    g_out = lax.all_to_all(field, PLANE, 0, 0, tiled=True)

    taps = weight.reshape(3, 3, C, C)
    forward_mix = taps.transpose(0, 2, 1, 3).reshape(3 * C, 3 * C)
    backward_mix = taps.transpose(0, 3, 1, 2).reshape(3 * C, 3 * C)
    act = activations[:, 0].transpose(1, 0, 2)
    flops = 2 * Y * X * 9 * C * C
    slope, turned = call(
        forward_kernel,
        (shape((Y, C, X), f32), shape((Y * X, WIDE), bf16)),
        [pltpu.VMEM((3 * C, Y * X), bf16), pltpu.VMEM((C, (Y + 2) * X), f32)],
        flops,
        4 << 20,
        act,
        forward_mix,
        conv_bias[:, None],
    )
    grad, sums = call(
        weight_kernel,
        (shape((Y, C, X), bf16), shape((N_FLAT, PIECE, WIDE), f32)),
        [pltpu.VMEM((3 * C, Y * X), bf16)],
        flops,
        4 << 20,
        g_out,
        slope,
        turned,
    )
    out = call(
        input_kernel,
        shape((Y, C, X), bf16),
        [pltpu.VMEM((3 * C, Y * X), bf16), pltpu.VMEM((C, (Y + 2) * X), f32)],
        flops,
        2 << 20,
        grad,
        g_out,
        backward_mix,
    )
    grad_input = out.transpose(1, 0, 2)[:, None]

    parts = lax.all_to_all(sums, FLAT, 0, 0, tiled=True)
    sent = call(
        spread_sum_kernel, shape((N_COLUMN, PIECE, WIDE), f32), [], 1 << 16, 1 << 18, parts
    )
    parts = lax.all_to_all(sent, COLUMN, 0, 0, tiled=True)
    factor = float(512 * Y * X) ** -0.5
    sent = call(
        lambda a, b: scaled_sum_kernel(factor, a, b),
        shape((N_FLAT, PIECE, WIDE), f32),
        [],
        1 << 16,
        1 << 18,
        parts,
    )
    whole = lax.all_to_all(sent, FLAT, 0, 0, tiled=True).reshape(N_FLAT * PIECE, WIDE)
    grad_w = whole[: 3 * C, : 3 * C].reshape(3, C, 3, C).transpose(0, 2, 1, 3)
    return grad_input, grad_w.reshape(9, C, C), whole[3 * C, :C]


def solution(mesh):
    fine = Mesh(mesh.devices.reshape(SIZES), AXES)
    in_specs = (P(None, AXES, None, None), P(None, GROUP, PLANE, None), P(), P(), P())
    out_specs = (P(None, AXES, None, None), P(), P())
    return jax.shard_map(
        on_device, mesh=fine, in_specs=in_specs, out_specs=out_specs, check_vma=False
    )
```

time: 651 us -> 118 us (0.18)
  waiting for transfers between devices: 456 us -> 13.4 us
  blocking collectives: 115 us -> 46.5 us
  matrix products: 22.8 us -> 0 us
  Pallas kernels: 0 us -> 17.3 us
  between operations: 14.4 us -> 0.8 us
  local copies, waits for them, and re-layouts: 14.3 us -> 7.77 us
    psum x1 -> x0, waiting for transfers between devices: 443 us -> none  [on_device(): grad_w, grad_bias = lax.psum((grad_w, grad_bias), ('grp', 'xy'))]
    psum x1 -> x0, blocking collectives: 115 us -> none  [on_device(): grad_w, grad_bias = lax.psum((grad_w, grad_bias), ('grp', 'xy'))]
    all_to_all x0 -> x2, blocking collectives: none -> 46.5 us  [the longest x1 34.1 us: on_device(): parts = lax.all_to_all(sent, COLUMN, 0, 0, tiled=True)]
    dot_general x28 -> x0, matrix products: 22.8 us -> none  [the longest x9 10.8 us: forward_taps(): jnp.dot(weight[offset], shifted, preferred_element_type=jnp.float32)]
    pallas_call x0 -> x5, Pallas kernels: none -> 17.3 us  [call(): pl.pallas_call(kernel, out_shape=outs, in_specs=[pl.BlockSpec(memory_spac...]
    slice x3 -> x4, local copies, waits for them, and re-layouts: 8.27 us -> 1.26 us  [the longest x1 1.24 us: on_device(): blur_taps[R] * before.astype(f32)[:, None]]
    all_to_all x1 -> x2, starting transfers between devices: 19.5 us -> 24.1 us  [the longest x1 17.6 us: on_device(): g_out = lax.all_to_all(field, PLANE, 0, 0, tiled=True)]
    all_to_all x1 -> x2, waiting for transfers between devices: 13.5 us -> 11.6 us  [the longest x1 10.2 us: on_device(): g_out = lax.all_to_all(field, PLANE, 0, 0, tiled=True)]
  transfers between devices with their start and end apart: 3 -> 3, of which waited for: 2 -> 3; matrix products, arithmetic and copies ran while one was open for 3% -> 4% of each run, Pallas kernels for 0% -> 14%
where the time goes in v1:
time: 118 us; the launch traced here: 117 us
  blocking collectives  46.5 us (39%)
  starting transfers between devices  29.1 us (25%)
  Pallas kernels  17.3 us (15%)
  waiting for transfers between devices  13.4 us (11%)
  local copies, waits for them, and re-layouts  7.77 us (7%)
  other arithmetic  2.6 us (2%)
    all_to_all x1, blocking collectives, on_device(): parts = lax.all_to_all(sent, COLUMN, 0, 0, tiled=True)  34.1 us
    all_to_all x1, starting transfers between devices, on_device(): g_out = lax.all_to_all(field, PLANE, 0, 0, tiled=True)  17.6 us
    pallas_call x5, Pallas kernels, call(): pl.pallas_call(kernel, out_shape=outs, in_specs=[pl.BlockSpec(memory_spac...  17.3 us
    all_to_all x1, blocking collectives, on_device(): parts = lax.all_to_all(sums, FLAT, 0, 0, tiled=True)  12.4 us
    all_to_all x1, waiting for transfers between devices, on_device(): g_out = lax.all_to_all(field, PLANE, 0, 0, tiled=True)  10.2 us
    all_to_all x1, starting transfers between devices, on_device(): lax.all_to_all(sent, FLAT, 0, 0, tiled=True).reshape(N_FLAT * PIECE, WIDE)  6.53 us
    ppermute x1, starting transfers between devices, on_device(): earlier = lax.ppermute(coarse[3:], GROUP, hops)  4.94 us
    unnamed x12, local copies, waits for them, and re-layouts  3.55 us
  transfers between devices with their start and end apart: 3, of which 3 were waited for; matrix products, arithmetic and copies ran while one was open for 4% of the time, Pallas kernels for 14%

profile of v1, /device:TPU:1, one launch (start us, length us, event | category | flops | bytes accessed | tf_op | source)
XLA Modules:
  0.0 117.4 jit_solution(5544467086158961948)
XLA Ops:
  0.6 0.0 copy-start.2
  0.6 0.0 copy-start.3
  0.7 0.0 copy-start.4
  0.7 0.9 fusion.2
  1.6 4.9 %collective-permute-start = (bf16[1,64,128]{2,1,0:T(8,128)(2,1)S(1)}, bf16[1,64,128]{2,1,0:T(8,128)(2,1)S(1)}, u32[]{:S(2)}, u32[]{:S(2)}) collective-permute-start(bf16[1,64,128]{2,1,0:T(8,128)(2,1)S(1)} %slice.24), channel_id=1, source_target_pairs={{0,32},{32,64},{64,96},{96,128},{128,160},{160,192},{192,224},{224... | collective-permute-start | bytes 49160 | tf_op jit(solution)/shard_map/ppermute | solution.py:161
  6.6 1.2 %slice.19 = f32[1]{0:T(128)} slice(f32[9]{0:T(128)} %param.9), slice={[8:9]} | slice | bytes 8 | tf_op jit(solution)/shard_map/slice | solution.py:165
  7.8 0.7 mul.31
  8.5 0.1 mul.32
  8.6 0.1 broadcast_in_dim.37
  8.6 1.8 %collective-permute-done = bf16[1,64,128]{2,1,0:T(8,128)(2,1)S(1)} collective-permute-done((bf16[1,64,128]{2,1,0:T(8,128)(2,1)S(1)}, bf16[1,64,128]{2,1,0:T(8,128)(2,1)S(1)}, u32[]{:S(2)}, u32[]{:S(2)}) %collective-permute-start) | collective-permute-done | bytes 16416 | tf_op jit(solution)/shard_map/ppermute | solution.py:161
  10.4 0.7 convert_multiply_fusion
  11.1 1.0 fusion.1
  12.1 17.6 %all-to-all-start = ((bf16[32,64,128]{2,1,0:T(8,128)(2,1)}), bf16[32,64,128]{2,1,0:T(8,128)(2,1)S(1)}, u32[]{:S(2)}, u32[]{:S(2)}) async-start(bf16[32,64,128]{2,1,0:T(8,128)(2,1)} %fusion.1), calls=%async_computation | async-start | bytes 1048576 | tf_op jit(solution)/shard_map/all_to_all | solution.py:167
  29.7 0.0 copy-done.2
  29.7 0.1 copy.44
  29.9 0.2 reshape.53.mix_ref
  30.0 0.0 copy-done.3
  30.0 0.2 copy.43
  30.3 0.0 copy-done.4
  30.3 0.1 copy.34.bias_ref
  30.4 9.9 %shard_map.76 = (f32[32,64,128]{2,1,0:T(8,128)S(1)}, bf16[4096,256]{1,0:T(8,128)(2,1)S(1)}) custom-call(bf16[32,64,128]{2,1,0:T(8,128)(2,1)S(1)} %bitcast.38, bf16[192,192]{1,0:T(8,128)(2,1)S(1)} %reshape.53.mix_ref, f32[64,1]{1,0:T(8,128)S(1)} %copy.34.bias_ref), custom_call_target="tpu_custom_call" | custom-call | flops 301989888 | bytes 4194304 | tf_op jit(solution)/shard_map/pallas_call | solution.py:144
  40.3 0.0 copy-start
  40.3 1.0 copy-done
  41.3 10.2 %all-to-all-done.g_ref = bf16[32,64,128]{2,1,0:T(8,128)(2,1)S(1)} async-done(((bf16[32,64,128]{2,1,0:T(8,128)(2,1)}), bf16[32,64,128]{2,1,0:T(8,128)(2,1)S(1)}, u32[]{:S(2)}, u32[]{:S(2)}) %all-to-all-start) | async-done | bytes 524320 | tf_op jit(solution)/shard_map/all_to_all | solution.py:167
  51.5 0.0 copy-start.1
  51.5 1.2 %copy-done.1 = f32[32,64,128]{2,1,0:T(8,128)S(1)} copy-done((f32[32,64,128]{2,1,0:T(8,128)S(1)}, f32[32,64,128]{2,1,0:T(8,128)}, u32[]{:S(2)}) %copy-start.1) | copy-done | bytes 1048600
  52.7 0.7 shard_map.77
  53.4 12.4 %all_to_all.20.parts_ref = f32[32,8,256]{2,1,0:T(8,128)S(1)} all-to-all(f32[32,8,256]{2,1,0:T(8,128)S(1)} %get-tuple-element.10), channel_id=1, replica_groups=mesh['zl'=8,'core'=2,'x'=4,'y'=4,'zh'=2] {'core','x','y'}, dimensions={0} | all-to-all | bytes 524288 | tf_op jit(solution)/shard_map/all_to_all | solution.py:206
  65.8 34.1 %all_to_all.21.a = f32[16,8,256]{2,1,0:T(8,128)S(1)} all-to-all(f32[16,8,256]{2,1,0:T(8,128)S(1)} %shard_map.79), channel_id=1, replica_groups=mesh['zl'=8,'core'=2,'x'=4,'y'=4,'zh'=2] {'zl','zh'}, dimensions={0} | all-to-all | bytes 262144 | tf_op jit(solution)/shard_map/all_to_all | solution.py:210
  99.9 0.7 shard_map.80
  100.6 6.5 %all-to-all-start.3 = ((f32[32,8,256]{2,1,0:T(8,128)}), f32[32,8,256]{2,1,0:T(8,128)S(1)}, u32[]{:S(2)}, u32[]{:S(2)}) async-start(f32[32,8,256]{2,1,0:T(8,128)} %shard_map.80), calls=%async_computation.3 | async-start | bytes 524288 | tf_op jit(solution)/shard_map/all_to_all | solution.py:220
  107.1 0.2 copy.35
  107.3 0.2 reshape.54.mix_ref
  107.5 6.0 %shard_map.78 = bf16[32,64,128]{2,1,0:T(8,128)(2,1)S(1)} custom-call(bf16[32,64,128]{2,1,0:T(8,128)(2,1)S(1)} %get-tuple-element.9.grad_ref, bf16[32,64,128]{2,1,0:T(8,128)(2,1)S(1)} %all-to-all-done.g_ref, bf16[192,192]{1,0:T(8,128)(2,1)S(1)} %reshape.54.mix_ref), custom_call_target="tpu_custom_call" | custom-call | flops 301989888 | bytes 2097152 | tf_op jit(solution)/shard_map/pallas_call | solution.py:144
  113.4 1.1 copy.37
  114.6 1.4 %all-to-all-done.3 = f32[32,8,256]{2,1,0:T(8,128)S(1)} async-done(((f32[32,8,256]{2,1,0:T(8,128)}), f32[32,8,256]{2,1,0:T(8,128)S(1)}, u32[]{:S(2)}, u32[]{:S(2)}) %all-to-all-start.3) | async-done | bytes 262176 | tf_op jit(solution)/shard_map/all_to_all | solution.py:220
  116.0 0.5 slice_bitcast_fusion
  116.5 0.2 reshape.56
  116.7 0.7 copy.36
  (6 shorter events, 0.1 us)
Async XLA Ops:
  0.6 29.1 %copy-start.2 = (bf16[9,64,64]{2,1,0:T(8,128)(2,1)S(1)}, bf16[9,64,64]{2,1,0:T(8,128)(2,1)}, u32[]{:S(2)}) copy-start(bf16[9,64,64]{2,1,0:T(8,128)(2,1)} %param.7) | copy-start | bytes 221188
  0.6 29.4 %copy-start.3 = (bf16[64,1,32,128]{3,2,1,0:T(8,128)(2,1)S(1)}, bf16[64,1,32,128]{3,2,1,0:T(8,128)(2,1)}, u32[]{:S(2)}) copy-start(bf16[64,1,32,128]{3,2,1,0:T(8,128)(2,1)} %param.5) | copy-start | bytes 1572868
  0.7 29.6 %copy-start.4 = (f32[64]{0:T(128)S(1)}, f32[64]{0:T(128)}, u32[]{:S(2)}) copy-start(f32[64]{0:T(128)} %param.8) | copy-start | bytes 772
  1.6 8.8 %collective-permute-start = (bf16[1,64,128]{2,1,0:T(8,128)(2,1)S(1)}, bf16[1,64,128]{2,1,0:T(8,128)(2,1)S(1)}, u32[]{:S(2)}, u32[]{:S(2)}) collective-permute-start(bf16[1,64,128]{2,1,0:T(8,128)(2,1)S(1)} %slice.24), channel_id=1, source_target_pairs={{0,32},{32,64},{64,96},{96,128},{128,160},{160,192},{192,224},{224... | collective-permute-start | bytes 49160 | tf_op jit(solution)/shard_map/ppermute | solution.py:161
  12.1 39.3 %all-to-all-start = ((bf16[32,64,128]{2,1,0:T(8,128)(2,1)}), bf16[32,64,128]{2,1,0:T(8,128)(2,1)S(1)}, u32[]{:S(2)}, u32[]{:S(2)}) async-start(bf16[32,64,128]{2,1,0:T(8,128)(2,1)} %fusion.1), calls=%async_computation | async-start | bytes 1048576 | tf_op jit(solution)/shard_map/all_to_all | solution.py:167
  40.3 1.0 copy-start
  51.5 1.2 %copy-start.1 = (f32[32,64,128]{2,1,0:T(8,128)S(1)}, f32[32,64,128]{2,1,0:T(8,128)}, u32[]{:S(2)}) copy-start(f32[32,64,128]{2,1,0:T(8,128)} %copy-done) | copy-start | bytes 3145732
  100.6 15.4 %all-to-all-start.3 = ((f32[32,8,256]{2,1,0:T(8,128)}), f32[32,8,256]{2,1,0:T(8,128)S(1)}, u32[]{:S(2)}, u32[]{:S(2)}) async-start(f32[32,8,256]{2,1,0:T(8,128)} %shard_map.80), calls=%async_computation.3 | async-start | bytes 524288 | tf_op jit(solution)/shard_map/all_to_all | solution.py:220

commit v2 on v1

--- a/solution.py
+++ b/solution.py
@@ -14,9 +14,12 @@
 SIZES = (8, 2, 4, 4, 2)
 GROUP = ("zl", "core")
 PLANE = ("x", "y", "zh")
+CROSS = ("x", "y")
+N_CROSS = 16
 FLAT = ("core", "x", "y")
 COLUMN = ("zl", "zh")
 N_FLAT = 32
+N_GROUP = 16
 N_COLUMN = 16
 PIECE = 8
 WIDE = 256
@@ -128,6 +131,30 @@
     lax.fori_loop(0, Y, finish, 0)
 
 
+def blur_kernel(half_ref, taps_ref, own_ref, other_ref, halo_own_ref, halo_other_ref, out_ref):
+    half = half_ref[0]
+    spill = jnp.where(half == 0, taps_ref[R], 0.0)
+    sides = ((half, own_ref, halo_own_ref), (1 - half, other_ref, halo_other_ref))
+    for slot, rows_ref, halo_ref in sides:
+        before = halo_ref[0].astype(jnp.float32)
+        for k in range(4):
+            row = rows_ref[k].astype(jnp.float32)
+            for pair in range(4):
+                value = taps_ref[2 * pair + half] * row
+                if pair == 0:
+                    value = value + spill * before
+                out_ref[4 * k + pair, slot] = value.astype(jnp.bfloat16)
+            before = row
+
+
+def unpack_kernel(whole_ref, weight_ref, bias_ref):
+    for a in range(3):
+        rows = whole_ref[a * C : (a + 1) * C]
+        for b in range(3):
+            weight_ref[3 * a + b] = rows[:, b * C : (b + 1) * C]
+    bias_ref[...] = whole_ref[3 * C : 3 * C + 1, :C]
+
+
 def spread_sum_kernel(parts_ref, out_ref):
     total = jnp.sum(parts_ref[...], axis=0)
     for copy in range(out_ref.shape[0]):
@@ -140,11 +167,12 @@
         out_ref[copy] = total
 
 
-def call(kernel, outs, scratch, flops, moved, *args):
+def call(kernel, outs, scratch, flops, moved, *args, scalars=0):
     return pl.pallas_call(
         kernel,
         out_shape=outs,
-        in_specs=[pl.BlockSpec(memory_space=pltpu.VMEM)] * len(args),
+        in_specs=[pl.BlockSpec(memory_space=pltpu.SMEM)] * scalars
+        + [pl.BlockSpec(memory_space=pltpu.VMEM)] * (len(args) - scalars),
         out_specs=jax.tree.map(lambda _: pl.BlockSpec(memory_space=pltpu.VMEM), outs),
         scratch_shapes=scratch,
         compiler_params=pltpu.CompilerParams(vmem_limit_bytes=VMEM_LIMIT),
@@ -155,16 +183,31 @@
 def on_device(activations, cotangent, weight, conv_bias, blur_taps):
     shape = jax.ShapeDtypeStruct
     bf16, f32 = jnp.bfloat16, jnp.float32
-    groups = 16
     coarse = cotangent[:, :, 0, :].transpose(1, 0, 2)
-    hops = [(g, g + 1) for g in range(groups - 1)]
-    earlier = lax.ppermute(coarse[3:], GROUP, hops)
-    before = jnp.concatenate([earlier, coarse[:3]], axis=0)
-    first = (jnp.arange(R) == 0)[None, :, None, None]
-    field = blur_taps[:R][None, :, None, None] * coarse.astype(f32)[:, None]
-    field = field + jnp.where(first, blur_taps[R] * before.astype(f32)[:, None], 0.0)
-    field = field.astype(bf16).reshape(Y, C, X)
-    g_out = lax.all_to_all(field, PLANE, 0, 0, tiled=True)
+    other = lax.ppermute(coarse, "zh", [(0, 1), (1, 0)])
+    halos = []
+    for side in range(2):
+        pairs = []
+        for group in range(N_GROUP - 1):
+            for cross in range(N_CROSS):
+                source = (group * N_CROSS + cross) * 2 + side
+                pairs.append((source, ((group + 1) * N_CROSS + cross) * 2))
+        halos.append(lax.ppermute(coarse[3:], AXES, pairs))
+    half = lax.axis_index("zh").astype(jnp.int32)
+    field = call(
+        blur_kernel,
+        shape((N_CROSS, 2, C, X), bf16),
+        [],
+        1 << 20,
+        1 << 20,
+        half[None],
+        blur_taps,
+        coarse,
+        other,
+        *halos,
+        scalars=2,
+    )
+    g_out = lax.all_to_all(field, CROSS, 0, 0, tiled=True).reshape(Y, C, X)
 
     taps = weight.reshape(3, 3, C, C)
     forward_mix = taps.transpose(0, 2, 1, 3).reshape(3 * C, 3 * C)
@@ -208,6 +251,7 @@
         spread_sum_kernel, shape((N_COLUMN, PIECE, WIDE), f32), [], 1 << 16, 1 << 18, parts
     )
     parts = lax.all_to_all(sent, COLUMN, 0, 0, tiled=True)
+    parts, grad_input = lax.optimization_barrier((parts, grad_input))
     factor = float(512 * Y * X) ** -0.5
     sent = call(
         lambda a, b: scaled_sum_kernel(factor, a, b),
@@ -218,8 +262,10 @@
         parts,
     )
     whole = lax.all_to_all(sent, FLAT, 0, 0, tiled=True).reshape(N_FLAT * PIECE, WIDE)
-    grad_w = whole[: 3 * C, : 3 * C].reshape(3, C, 3, C).transpose(0, 2, 1, 3)
-    return grad_input, grad_w.reshape(9, C, C), whole[3 * C, :C]
+    grad_w, grad_b = call(
+        unpack_kernel, (shape((9, C, C), f32), shape((1, C), f32)), [], 1, 1 << 18, whole
+    )
+    return grad_input, grad_w, grad_b.reshape(C)
 
 
 def solution(mesh):

time: 118 us -> 110 us (0.932)
  blocking collectives: 46.5 us -> 15.7 us
  waiting for transfers between devices: 13.4 us -> 27.2 us
  starting transfers between devices: 29.1 us -> 38.7 us
  Pallas kernels: 17.3 us -> 20.2 us
  other arithmetic: 2.6 us -> 0 us
    all_to_all x1 -> x0, blocking collectives: 34.1 us -> none  [on_device(): parts = lax.all_to_all(sent, COLUMN, 0, 0, tiled=True)]
    ppermute x1 -> x3, starting transfers between devices: 4.94 us -> 21.1 us  [the longest x1 16.3 us: on_device(): other = lax.ppermute(coarse, 'zh', [(0, 1), (1, 0)])]
    ppermute x1 -> x3, waiting for transfers between devices: 1.79 us -> 12.5 us  [the longest x2 12.5 us: on_device(): halos.append(lax.ppermute(coarse[3:], AXES, pairs))]
    all_to_all x1 -> x2, starting transfers between devices: 17.6 us -> 11.1 us  [the longest x1 6.75 us: on_device(): g_out = lax.all_to_all(field, CROSS, 0, 0, tiled=True).reshape(Y, C, X)]
    all_to_all x1, waiting for transfers between devices: 1.4 us -> 7.7 us  [on_device(): lax.all_to_all(sent, FLAT, 0, 0, tiled=True).reshape(N_FLAT * PIECE, WIDE)]
    all_to_all x1, blocking collectives: 12.4 us -> 15.7 us  [on_device(): parts = lax.all_to_all(sums, FLAT, 0, 0, tiled=True)]
    all_to_all x1 -> x2, waiting for transfers between devices: 10.2 us -> 7 us  [the longest x1 7 us: on_device(): parts = lax.all_to_all(sent, COLUMN, 0, 0, tiled=True)]
    pallas_call x5 -> x7, Pallas kernels: 17.3 us -> 20.2 us  [call(): pl.pallas_call(kernel, out_shape=outs, in_specs=[pl.BlockSpec(memory_spac...]
  transfers between devices with their start and end apart: 3 -> 6, of which waited for: 3 -> 3; matrix products, arithmetic and copies ran while one was open for 4% -> 3% of each run, Pallas kernels for 14% -> 15%
where the time goes in v2:
time: 110 us; the launch traced here: 109 us
  starting transfers between devices  38.7 us (35%)
  waiting for transfers between devices  27.2 us (25%)
  Pallas kernels  20.2 us (18%)
  blocking collectives  15.7 us (14%)
  local copies, waits for them, and re-layouts  6.71 us (6%)
    pallas_call x7, Pallas kernels, call(): pl.pallas_call(kernel, out_shape=outs, in_specs=[pl.BlockSpec(memory_spac...  20.2 us
    ppermute x1, starting transfers between devices, on_device(): other = lax.ppermute(coarse, 'zh', [(0, 1), (1, 0)])  16.3 us
    all_to_all x1, blocking collectives, on_device(): parts = lax.all_to_all(sums, FLAT, 0, 0, tiled=True)  15.7 us
    ppermute x2, waiting for transfers between devices, on_device(): halos.append(lax.ppermute(coarse[3:], AXES, pairs))  12.5 us
    all_to_all x1, waiting for transfers between devices, on_device(): lax.all_to_all(sent, FLAT, 0, 0, tiled=True).reshape(N_FLAT * PIECE, WIDE)  7.7 us
    all_to_all x1, waiting for transfers between devices, on_device(): parts = lax.all_to_all(sent, COLUMN, 0, 0, tiled=True)  7 us
    all_to_all x1, starting transfers between devices, on_device(): g_out = lax.all_to_all(field, CROSS, 0, 0, tiled=True).reshape(Y, C, X)  6.75 us
    all_to_all x1, starting transfers between devices, on_device(): lax.all_to_all(sent, FLAT, 0, 0, tiled=True).reshape(N_FLAT * PIECE, WIDE)  6.53 us
  transfers between devices with their start and end apart: 6, of which 3 were waited for; matrix products, arithmetic and copies ran while one was open for 3% of the time, Pallas kernels for 15%

profile of v2, /device:TPU:1, one launch (start us, length us, event | category | flops | bytes accessed | tf_op | source)
XLA Modules:
  0.0 109.3 jit_solution(2914509530652787652)
XLA Ops:
  0.6 0.0 copy-start.5
  0.6 0.9 copy.25
  1.5 16.3 %collective-permute-start = (bf16[4,64,128]{2,1,0:T(8,128)(2,1)S(1)}, bf16[4,64,128]{2,1,0:T(8,128)(2,1)S(1)}, u32[]{:S(2)}, u32[]{:S(2)}) collective-permute-start(bf16[4,64,128]{2,1,0:T(8,128)(2,1)S(1)} %bitcast.28), channel_id=1, source_target_pairs={{0,1},{1,0},{2,3},{3,2},{4,5},{5,4},{6,7},{7,6},{8,9},{9,8},{10,11... | collective-permute-start | bytes 196616 | tf_op jit(solution)/shard_map/ppermute | solution.py:187
  17.8 3.5 %collective-permute-start.1 = (bf16[1,64,128]{2,1,0:T(8,128)(2,1)S(1)}, bf16[1,64,128]{2,1,0:T(8,128)(2,1)S(1)}, u32[]{:S(2)}, u32[]{:S(2)}) collective-permute-start(bf16[1,64,128]{2,1,0:T(8,128)(2,1)S(1)} %slice.5), channel_id=1, source_target_pairs={{0,32},{2,34},{4,36},{6,38},{8,40},{10,42},{12,44},{14,46},{16,48}... | collective-permute-start | bytes 49160 | tf_op jit(solution)/shard_map/ppermute | solution.py:195
  21.3 1.3 %collective-permute-start.2 = (bf16[1,64,128]{2,1,0:T(8,128)(2,1)S(1)}, bf16[1,64,128]{2,1,0:T(8,128)(2,1)S(1)}, u32[]{:S(2)}, u32[]{:S(2)}) collective-permute-start(bf16[1,64,128]{2,1,0:T(8,128)(2,1)S(1)} %slice.5), channel_id=1, source_target_pairs={{1,32},{3,34},{5,36},{7,38},{9,40},{11,42},{13,44},{15,46},{17,48}... | collective-permute-start | bytes 49160 | tf_op jit(solution)/shard_map/ppermute | solution.py:195
  22.6 0.0 collective-permute-done.1.halo_own_ref
  22.6 12.5 %collective-permute-done.2.halo_other_ref = bf16[1,64,128]{2,1,0:T(8,128)(2,1)S(1)} collective-permute-done((bf16[1,64,128]{2,1,0:T(8,128)(2,1)S(1)}, bf16[1,64,128]{2,1,0:T(8,128)(2,1)S(1)}, u32[]{:S(2)}, u32[]{:S(2)}) %collective-permute-start.2) | collective-permute-done | bytes 16416 | tf_op jit(solution)/shard_map/ppermute | solution.py:195
  35.1 0.0 collective-permute-done.other_ref
  35.1 0.0 copy-start.2
  35.1 0.7 copy-done.2
  35.7 0.0 copy-start.4
  35.7 1.4 %shard_map.76 = bf16[16,2,64,128]{3,2,1,0:T(8,128)(2,1)} custom-call(s32[1]{0:T(128)} %bitcast.half_ref, f32[9]{0:T(128)S(1)} %copy-done.2, bf16[4,64,128]{2,1,0:T(8,128)(2,1)S(1)} %bitcast.30, bf16[4,64,128]{2,1,0:T(8,128)(2,1)S(1)} %collective-permute-done.other_ref, bf16[1,64,128]{2,1,0:T(8,128)(2,1)S(1)} %collective-permute-done.1.halo_own_ref, ...), custom_call_target="tpu_custom_call" | custom-call | flops 1048576 | bytes 1048576 | tf_op jit(solution)/shard_map/pallas_call | solution.py:171
  37.2 6.8 %all-to-all-start = ((bf16[16,2,64,128]{3,2,1,0:T(8,128)(2,1)}), bf16[16,2,64,128]{3,2,1,0:T(8,128)(2,1)S(1)}, u32[]{:S(2)}, u32[]{:S(2)}) async-start(bf16[16,2,64,128]{3,2,1,0:T(8,128)(2,1)} %shard_map.76), calls=%async_computation | async-start | bytes 1048576 | tf_op jit(solution)/shard_map/all_to_all | solution.py:210
  43.9 1.0 copy.24
  45.0 0.2 reshape.26.mix_ref
  45.1 0.0 copy-done.4
  45.1 0.2 copy.23
  45.3 0.0 copy-done.5
  45.4 0.1 copy.17.bias_ref
  45.5 9.9 %shard_map.77 = (f32[32,64,128]{2,1,0:T(8,128)S(1)}, bf16[4096,256]{1,0:T(8,128)(2,1)S(1)}) custom-call(bf16[32,64,128]{2,1,0:T(8,128)(2,1)S(1)} %bitcast.27, bf16[192,192]{1,0:T(8,128)(2,1)S(1)} %reshape.26.mix_ref, f32[64,1]{1,0:T(8,128)S(1)} %copy.17.bias_ref), custom_call_target="tpu_custom_call" | custom-call | flops 301989888 | bytes 4194304 | tf_op jit(solution)/shard_map/pallas_call | solution.py:171
  55.4 0.0 copy-start
  55.4 1.0 copy-done
  56.4 0.0 all-to-all-done
  56.4 0.0 copy-start.1
  56.4 1.2 %copy-done.1 = f32[32,64,128]{2,1,0:T(8,128)S(1)} copy-done((f32[32,64,128]{2,1,0:T(8,128)S(1)}, f32[32,64,128]{2,1,0:T(8,128)}, u32[]{:S(2)}) %copy-start.1) | copy-done | bytes 1048600
  57.6 0.0 copy-start.3
  57.6 0.7 shard_map.78
  58.3 15.7 %all_to_all.20.parts_ref = f32[32,8,256]{2,1,0:T(8,128)S(1)} all-to-all(f32[32,8,256]{2,1,0:T(8,128)S(1)} %get-tuple-element.13), channel_id=1, replica_groups=mesh['zl'=8,'core'=2,'x'=4,'y'=4,'zh'=2] {'core','x','y'}, dimensions={0} | all-to-all | bytes 524288 | tf_op jit(solution)/shard_map/all_to_all | solution.py:249
  74.0 0.7 shard_map.79
  74.7 4.4 %all-to-all-start.2 = ((f32[16,8,256]{2,1,0:T(8,128)}), f32[16,8,256]{2,1,0:T(8,128)S(1)}, u32[]{:S(2)}, u32[]{:S(2)}) async-start(f32[16,8,256]{2,1,0:T(8,128)} %shard_map.79), calls=%async_computation.2 | async-start | bytes 262144 | tf_op jit(solution)/shard_map/all_to_all | solution.py:253
  79.1 0.0 copy-done.3
  79.1 0.2 copy.18
  79.3 0.2 reshape.27.mix_ref
  79.4 5.9 %shard_map.80 = bf16[32,64,128]{2,1,0:T(8,128)(2,1)S(1)} custom-call(bf16[32,64,128]{2,1,0:T(8,128)(2,1)S(1)} %get-tuple-element.14.grad_ref, bf16[32,64,128]{2,1,0:T(8,128)(2,1)S(1)} %bitcast.24, bf16[192,192]{1,0:T(8,128)(2,1)S(1)} %reshape.27.mix_ref), custom_call_target="tpu_custom_call" | custom-call | flops 301989888 | bytes 2097152 | tf_op jit(solution)/shard_map/pallas_call | solution.py:171
  85.4 7.0 %all-to-all-done.2.a = f32[16,8,256]{2,1,0:T(8,128)S(1)} async-done(((f32[16,8,256]{2,1,0:T(8,128)}), f32[16,8,256]{2,1,0:T(8,128)S(1)}, u32[]{:S(2)}, u32[]{:S(2)}) %all-to-all-start.2) | async-done | bytes 131104 | tf_op jit(solution)/shard_map/all_to_all | solution.py:253
  92.4 0.7 shard_map.81
  93.1 6.5 %all-to-all-start.3 = ((f32[32,8,256]{2,1,0:T(8,128)}), f32[32,8,256]{2,1,0:T(8,128)S(1)}, u32[]{:S(2)}, u32[]{:S(2)}) async-start(f32[32,8,256]{2,1,0:T(8,128)} %shard_map.81), calls=%async_computation.3 | async-start | bytes 524288 | tf_op jit(solution)/shard_map/all_to_all | solution.py:264
  99.6 1.1 %copy.19 = bf16[64,1,32,128]{3,2,1,0:T(8,128)(2,1)} copy(bf16[64,1,32,128]{3,0,2,1:T(8,128)(2,1)S(1)} %bitcast.25) | data formatting | bytes 1048576
  100.8 7.7 %all-to-all-done.3 = f32[32,8,256]{2,1,0:T(8,128)S(1)} async-done(((f32[32,8,256]{2,1,0:T(8,128)}), f32[32,8,256]{2,1,0:T(8,128)S(1)}, u32[]{:S(2)}, u32[]{:S(2)}) %all-to-all-start.3) | async-done | bytes 262176 | tf_op jit(solution)/shard_map/all_to_all | solution.py:264
  108.5 0.8 shard_map.82
  (1 shorter events, 0.0 us)
Async XLA Ops:
  0.6 44.7 %copy-start.5 = (f32[64]{0:T(128)S(1)}, f32[64]{0:T(128)}, u32[]{:S(2)}) copy-start(f32[64]{0:T(128)} %param.8) | copy-start | bytes 772
  1.5 33.6 %collective-permute-start = (bf16[4,64,128]{2,1,0:T(8,128)(2,1)S(1)}, bf16[4,64,128]{2,1,0:T(8,128)(2,1)S(1)}, u32[]{:S(2)}, u32[]{:S(2)}) collective-permute-start(bf16[4,64,128]{2,1,0:T(8,128)(2,1)S(1)} %bitcast.28), channel_id=1, source_target_pairs={{0,1},{1,0},{2,3},{3,2},{4,5},{5,4},{6,7},{7,6},{8,9},{9,8},{10,11... | collective-permute-start | bytes 196616 | tf_op jit(solution)/shard_map/ppermute | solution.py:187
  17.8 4.8 %collective-permute-start.1 = (bf16[1,64,128]{2,1,0:T(8,128)(2,1)S(1)}, bf16[1,64,128]{2,1,0:T(8,128)(2,1)S(1)}, u32[]{:S(2)}, u32[]{:S(2)}) collective-permute-start(bf16[1,64,128]{2,1,0:T(8,128)(2,1)S(1)} %slice.5), channel_id=1, source_target_pairs={{0,32},{2,34},{4,36},{6,38},{8,40},{10,42},{12,44},{14,46},{16,48}... | collective-permute-start | bytes 49160 | tf_op jit(solution)/shard_map/ppermute | solution.py:195
  21.3 13.8 %collective-permute-start.2 = (bf16[1,64,128]{2,1,0:T(8,128)(2,1)S(1)}, bf16[1,64,128]{2,1,0:T(8,128)(2,1)S(1)}, u32[]{:S(2)}, u32[]{:S(2)}) collective-permute-start(bf16[1,64,128]{2,1,0:T(8,128)(2,1)S(1)} %slice.5), channel_id=1, source_target_pairs={{1,32},{3,34},{5,36},{7,38},{9,40},{11,42},{13,44},{15,46},{17,48}... | collective-permute-start | bytes 49160 | tf_op jit(solution)/shard_map/ppermute | solution.py:195
  35.1 0.7 copy-start.2
  35.7 9.4 %copy-start.4 = (bf16[64,1,32,128]{3,2,1,0:T(8,128)(2,1)S(1)}, bf16[64,1,32,128]{3,2,1,0:T(8,128)(2,1)}, u32[]{:S(2)}) copy-start(bf16[64,1,32,128]{3,2,1,0:T(8,128)(2,1)} %param.5) | copy-start | bytes 1572868
  37.2 19.2 %all-to-all-start = ((bf16[16,2,64,128]{3,2,1,0:T(8,128)(2,1)}), bf16[16,2,64,128]{3,2,1,0:T(8,128)(2,1)S(1)}, u32[]{:S(2)}, u32[]{:S(2)}) async-start(bf16[16,2,64,128]{3,2,1,0:T(8,128)(2,1)} %shard_map.76), calls=%async_computation | async-start | bytes 1048576 | tf_op jit(solution)/shard_map/all_to_all | solution.py:210
  55.4 1.0 copy-start
  56.4 1.2 %copy-start.1 = (f32[32,64,128]{2,1,0:T(8,128)S(1)}, f32[32,64,128]{2,1,0:T(8,128)}, u32[]{:S(2)}) copy-start(f32[32,64,128]{2,1,0:T(8,128)} %copy-done) | copy-start | bytes 3145732
  57.6 21.5 %copy-start.3 = (bf16[9,64,64]{2,1,0:T(8,128)(2,1)S(1)}, bf16[9,64,64]{2,1,0:T(8,128)(2,1)}, u32[]{:S(2)}) copy-start(bf16[9,64,64]{2,1,0:T(8,128)(2,1)} %param.7) | copy-start | bytes 221188
  74.7 17.7 %all-to-all-start.2 = ((f32[16,8,256]{2,1,0:T(8,128)}), f32[16,8,256]{2,1,0:T(8,128)S(1)}, u32[]{:S(2)}, u32[]{:S(2)}) async-start(f32[16,8,256]{2,1,0:T(8,128)} %shard_map.79), calls=%async_computation.2 | async-start | bytes 262144 | tf_op jit(solution)/shard_map/all_to_all | solution.py:253
  93.1 15.4 %all-to-all-start.3 = ((f32[32,8,256]{2,1,0:T(8,128)}), f32[32,8,256]{2,1,0:T(8,128)S(1)}, u32[]{:S(2)}, u32[]{:S(2)}) async-start(f32[32,8,256]{2,1,0:T(8,128)} %shard_map.81), calls=%async_computation.3 | async-start | bytes 524288 | tf_op jit(solution)/shard_map/all_to_all | solution.py:264

commit v3 on v2

--- a/solution.py
+++ b/solution.py
@@ -23,7 +23,7 @@
 N_COLUMN = 16
 PIECE = 8
 WIDE = 256
-VMEM_LIMIT = 48 * 1024 * 1024
+VMEM_LIMIT = 16 * 1024 * 1024
 
 
 def shifted(row, step):
@@ -34,41 +34,65 @@
     return jnp.where(lane == edge, 0.0, pltpu.roll(row, (-step) % X, 1))
 
 
-def forward_kernel(act_ref, mix_ref, bias_ref, slope_ref, turned_ref, stack, hidden):
+def forward_kernel(
+    half_ref,
+    taps_ref,
+    bias_ref,
+    act_far,
+    weight_far,
+    slope_ref,
+    turned_ref,
+    coef_ref,
+    stack,
+    hidden,
+    act_ref,
+    weight_ref,
+    sems,
+):
+    copies = [
+        pltpu.make_async_copy(act_far, act_ref, sems.at[0]),
+        pltpu.make_async_copy(weight_far, weight_ref, sems.at[1]),
+    ]
+    for copy in copies:
+        copy.start()
+    half = half_ref[0]
+    for pair in range(4):
+        coef_ref[pair : pair + 1] = jnp.full((1, X), taps_ref[2 * pair + half], jnp.float32)
+    spill = jnp.where(half == 0, taps_ref[R], 0.0)
+    coef_ref[4:] = jnp.full((4, X), spill, jnp.float32)
     column = lax.broadcasted_iota(jnp.int32, (X, WIDE - 3 * C), 1)
     ones = jnp.where(column == 0, 1.0, 0.0).astype(jnp.bfloat16)
-
-    def spread(y, carry):
-        row = act_ref[y].astype(jnp.float32)
-        at = pl.ds(pl.multiple_of(y * X, X), X)
+    for copy in copies:
+        copy.wait()
+    for y in range(Y):
+        if y % 16 == 0:
+            rows = jnp.swapaxes(act_ref[:, y : y + 16].astype(jnp.float32), 0, 1)
+        row = rows[y % 16]
+        at = slice(y * X, (y + 1) * X)
         whole = jnp.concatenate([shifted(row, b - 1) for b in range(3)], axis=0)
         stack[:, at] = whole.astype(jnp.bfloat16)
         turned_ref[at, : 3 * C] = whole.T.astype(jnp.bfloat16)
         turned_ref[at, 3 * C :] = ones
-        return carry
-
-    lax.fori_loop(0, Y, spread, 0)
-    hidden[...] = jnp.broadcast_to(bias_ref[...], hidden.shape)
-
-    def taps(j, carry):
-        at = pl.multiple_of(j * 2 * X, 2 * X)
-        part = jnp.dot(
-            mix_ref[...], stack[:, pl.ds(at, 2 * X)], preferred_element_type=jnp.float32
-        )
+    square = (C, C)
+    diagonal = lax.broadcasted_iota(jnp.int32, square, 0) == lax.broadcasted_iota(
+        jnp.int32, square, 1
+    )
+    bias = jnp.sum(jnp.where(diagonal, bias_ref[...], 0.0), axis=1, keepdims=True)
+    hidden[...] = jnp.broadcast_to(bias, hidden.shape)
+    mix = jnp.concatenate(
+        [jnp.concatenate([weight_ref[3 * a + b] for b in range(3)], axis=1) for a in range(3)],
+        axis=0,
+    )
+    for j in range(Y // 2):
+        at = j * 2 * X
+        part = jnp.dot(mix, stack[:, at : at + 2 * X], preferred_element_type=jnp.float32)
         for a in range(3):
-            place = pl.ds(pl.multiple_of(at + (2 - a) * X, X), 2 * X)
+            place = slice(at + (2 - a) * X, at + (4 - a) * X)
             hidden[:, place] += part[a * C : (a + 1) * C]
-        return carry
-
-    lax.fori_loop(0, Y // 2, taps, 0)
-
-    def slopes(y, carry):
-        h = hidden[:, pl.ds(pl.multiple_of((y + 1) * X, X), X)]
+    for y in range(Y):
+        h = hidden[:, (y + 1) * X : (y + 2) * X]
         s = jax.nn.sigmoid(h)
         slope_ref[y] = s * (1.0 + h * (1.0 - s))
-        return carry
-
-    lax.fori_loop(0, Y, slopes, 0)
 
 
 def weight_kernel(g_ref, slope_ref, turned_ref, grad_ref, sums_ref, stack):
@@ -99,50 +123,43 @@
     )
 
 
-def input_kernel(grad_ref, g_ref, mix_ref, out_ref, stack, total):
+def input_kernel(grad_ref, g_ref, weight_ref, out_ref, stack, total):
     total[...] = jnp.zeros_like(total)
-
-    def spread(y, carry):
+    for y in range(Y):
         row = grad_ref[y].astype(jnp.float32)
-        at = pl.ds(pl.multiple_of(y * X, X), X)
         whole = jnp.concatenate([shifted(row, 1 - b) for b in range(3)], axis=0)
-        stack[:, at] = whole.astype(jnp.bfloat16)
-        return carry
-
-    lax.fori_loop(0, Y, spread, 0)
-
-    def taps(j, carry):
-        at = pl.multiple_of(j * 2 * X, 2 * X)
-        part = jnp.dot(
-            mix_ref[...], stack[:, pl.ds(at, 2 * X)], preferred_element_type=jnp.float32
-        )
+        stack[:, y * X : (y + 1) * X] = whole.astype(jnp.bfloat16)
+    mix = jnp.concatenate(
+        [
+            jnp.concatenate(
+                [weight_ref[3 * a + b].astype(jnp.float32).T for b in range(3)], axis=1
+            )
+            for a in range(3)
+        ],
+        axis=0,
+    ).astype(jnp.bfloat16)
+    for j in range(Y // 2):
+        at = j * 2 * X
+        part = jnp.dot(mix, stack[:, at : at + 2 * X], preferred_element_type=jnp.float32)
         for a in range(3):
-            place = pl.ds(pl.multiple_of(at + a * X, X), 2 * X)
+            place = slice(at + a * X, at + (a + 2) * X)
             total[:, place] += part[a * C : (a + 1) * C]
-        return carry
-
-    lax.fori_loop(0, Y // 2, taps, 0)
-
-    def finish(y, carry):
-        conv = total[:, pl.ds(pl.multiple_of((y + 1) * X, X), X)]
+    for y in range(Y):
+        conv = total[:, (y + 1) * X : (y + 2) * X]
         out_ref[y] = (g_ref[y].astype(jnp.float32) + conv).astype(jnp.bfloat16)
-        return carry
-
-    lax.fori_loop(0, Y, finish, 0)
 
 
 def blur_kernel(half_ref, taps_ref, own_ref, other_ref, halo_own_ref, halo_other_ref, out_ref):
     half = half_ref[0]
-    spill = jnp.where(half == 0, taps_ref[R], 0.0)
     sides = ((half, own_ref, halo_own_ref), (1 - half, other_ref, halo_other_ref))
     for slot, rows_ref, halo_ref in sides:
         before = halo_ref[0].astype(jnp.float32)
         for k in range(4):
             row = rows_ref[k].astype(jnp.float32)
             for pair in range(4):
-                value = taps_ref[2 * pair + half] * row
+                value = taps_ref[pair : pair + 1] * row
                 if pair == 0:
-                    value = value + spill * before
+                    value = value + taps_ref[4:5] * before
                 out_ref[4 * k + pair, slot] = value.astype(jnp.bfloat16)
             before = row
 
@@ -167,12 +184,13 @@
         out_ref[copy] = total
 
 
-def call(kernel, outs, scratch, flops, moved, *args, scalars=0):
+def call(kernel, outs, scratch, flops, moved, *args, scalars=0, far=0):
     return pl.pallas_call(
         kernel,
         out_shape=outs,
         in_specs=[pl.BlockSpec(memory_space=pltpu.SMEM)] * scalars
-        + [pl.BlockSpec(memory_space=pltpu.VMEM)] * (len(args) - scalars),
+        + [pl.BlockSpec(memory_space=pltpu.VMEM)] * (len(args) - scalars - far)
+        + [pl.BlockSpec(memory_space=pltpu.HBM)] * far,
         out_specs=jax.tree.map(lambda _: pl.BlockSpec(memory_space=pltpu.VMEM), outs),
         scratch_shapes=scratch,
         compiler_params=pltpu.CompilerParams(vmem_limit_bytes=VMEM_LIMIT),
@@ -184,46 +202,57 @@
     shape = jax.ShapeDtypeStruct
     bf16, f32 = jnp.bfloat16, jnp.float32
     coarse = cotangent[:, :, 0, :].transpose(1, 0, 2)
+    hops = [
+        [
+            ((group * N_CROSS + cross) * 2 + side, ((group + 1) * N_CROSS + cross) * 2)
+            for group in range(N_GROUP - 1)
+            for cross in range(N_CROSS)
+        ]
+        for side in range(2)
+    ]
+    halo_other = lax.ppermute(coarse[3:], AXES, hops[1])
     other = lax.ppermute(coarse, "zh", [(0, 1), (1, 0)])
-    halos = []
-    for side in range(2):
-        pairs = []
-        for group in range(N_GROUP - 1):
-            for cross in range(N_CROSS):
-                source = (group * N_CROSS + cross) * 2 + side
-                pairs.append((source, ((group + 1) * N_CROSS + cross) * 2))
-        halos.append(lax.ppermute(coarse[3:], AXES, pairs))
-    half = lax.axis_index("zh").astype(jnp.int32)
+    halo_own = lax.ppermute(coarse[3:], AXES, hops[0])
+    half = lax.axis_index("zh").astype(jnp.int32)[None]
+    flops = 2 * Y * X * 9 * C * C
+    slope, turned, coef = call(
+        forward_kernel,
+        (shape((Y, C, X), f32), shape((Y * X, WIDE), bf16), shape((8, X), f32)),
+        [
+            pltpu.VMEM((3 * C, Y * X), bf16),
+            pltpu.VMEM((C, (Y + 2) * X), f32),
+            pltpu.VMEM((C, Y, X), bf16),
+            pltpu.VMEM((9, C, C), bf16),
+            pltpu.SemaphoreType.DMA((2,)),
+        ],
+        64 * flops,
+        128 << 20,
+        half,
+        blur_taps,
+        conv_bias[None, :],
+        activations[:, 0],
+        weight,
+        scalars=2,
+        far=2,
+    )
+    slope, turned, coef, halo_other, halo_own, other = lax.optimization_barrier(
+        (slope, turned, coef, halo_other, halo_own, other)
+    )
     field = call(
         blur_kernel,
         shape((N_CROSS, 2, C, X), bf16),
         [],
         1 << 20,
         1 << 20,
-        half[None],
-        blur_taps,
+        half,
+        coef,
         coarse,
         other,
-        *halos,
-        scalars=2,
+        halo_own,
+        halo_other,
+        scalars=1,
     )
     g_out = lax.all_to_all(field, CROSS, 0, 0, tiled=True).reshape(Y, C, X)
-
-    taps = weight.reshape(3, 3, C, C)
-    forward_mix = taps.transpose(0, 2, 1, 3).reshape(3 * C, 3 * C)
-    backward_mix = taps.transpose(0, 3, 1, 2).reshape(3 * C, 3 * C)
-    act = activations[:, 0].transpose(1, 0, 2)
-    flops = 2 * Y * X * 9 * C * C
-    slope, turned = call(
-        forward_kernel,
-        (shape((Y, C, X), f32), shape((Y * X, WIDE), bf16)),
-        [pltpu.VMEM((3 * C, Y * X), bf16), pltpu.VMEM((C, (Y + 2) * X), f32)],
-        flops,
-        4 << 20,
-        act,
-        forward_mix,
-        conv_bias[:, None],
-    )
     grad, sums = call(
         weight_kernel,
         (shape((Y, C, X), bf16), shape((N_FLAT, PIECE, WIDE), f32)),
@@ -242,7 +271,7 @@
         2 << 20,
         grad,
         g_out,
-        backward_mix,
+        weight,
     )
     grad_input = out.transpose(1, 0, 2)[:, None]
 

time: 110 us -> 101 us (0.918)
  blocking collectives: 15.7 us -> 31.1 us
  Pallas kernels: 20.2 us -> 6.7 us
  waiting for transfers between devices: 27.2 us -> 20.1 us
  starting transfers between devices: 38.7 us -> 36.4 us
  local copies, waits for them, and re-layouts: 6.71 us -> 5.25 us
    all_to_all x0 -> x1, blocking collectives: none -> 15.6 us  [on_device(): g_out = lax.all_to_all(field, CROSS, 0, 0, tiled=True).reshape(Y, C, X)]
    pallas_call x7, Pallas kernels: 20.2 us -> 6.7 us  [call(): pl.pallas_call(kernel, out_shape=outs, in_specs=[pl.BlockSpec(memory_spac...]
    ppermute x2, waiting for transfers between devices: 12.5 us -> 0.01 us  [the longest x1 0.01 us: on_device(): halo_own = lax.ppermute(coarse[3:], AXES, hops[0])]
    all_to_all x1, starting transfers between devices: 4.39 us -> 11.6 us  [on_device(): parts = lax.all_to_all(sent, COLUMN, 0, 0, tiled=True)]
    all_to_all x1 -> x0, starting transfers between devices: 6.75 us -> none  [on_device(): g_out = lax.all_to_all(field, CROSS, 0, 0, tiled=True).reshape(Y, C, X)]
    all_to_all x1, waiting for transfers between devices: 7 us -> 12.4 us  [on_device(): parts = lax.all_to_all(sent, COLUMN, 0, 0, tiled=True)]
    ppermute x1, starting transfers between devices: 16.3 us -> 12 us  [on_device(): other = lax.ppermute(coarse, 'zh', [(0, 1), (1, 0)])]
    reshape x4 -> x0, local copies, waits for them, and re-layouts: 1.54 us -> none  [the longest x2 1.21 us: on_device(): taps = weight.reshape(3, 3, C, C)]
  transfers between devices with their start and end apart: 6 -> 5, of which waited for: 3 -> 2; matrix products, arithmetic and copies ran while one was open for 3% -> 1% of each run, Pallas kernels for 15% -> 4%
where the time goes in v3:
time: 101 us; the launch traced here: 100 us
  starting transfers between devices  36.4 us (36%)
  blocking collectives  31.1 us (31%)
  waiting for transfers between devices  20.1 us (20%)
  Pallas kernels  6.7 us (7%)
  local copies, waits for them, and re-layouts  5.25 us (5%)
    all_to_all x1, blocking collectives, on_device(): g_out = lax.all_to_all(field, CROSS, 0, 0, tiled=True).reshape(Y, C, X)  15.6 us
    all_to_all x1, blocking collectives, on_device(): parts = lax.all_to_all(sums, FLAT, 0, 0, tiled=True)  15.6 us
    all_to_all x1, waiting for transfers between devices, on_device(): parts = lax.all_to_all(sent, COLUMN, 0, 0, tiled=True)  12.4 us
    ppermute x1, starting transfers between devices, on_device(): other = lax.ppermute(coarse, 'zh', [(0, 1), (1, 0)])  12 us
    all_to_all x1, starting transfers between devices, on_device(): parts = lax.all_to_all(sent, COLUMN, 0, 0, tiled=True)  11.6 us
    all_to_all x1, waiting for transfers between devices, on_device(): lax.all_to_all(sent, FLAT, 0, 0, tiled=True).reshape(N_FLAT * PIECE, WIDE)  7.7 us
    pallas_call x7, Pallas kernels, call(): pl.pallas_call(kernel, out_shape=outs, in_specs=[pl.BlockSpec(memory_spac...  6.7 us
    all_to_all x1, starting transfers between devices, on_device(): lax.all_to_all(sent, FLAT, 0, 0, tiled=True).reshape(N_FLAT * PIECE, WIDE)  6.53 us
  transfers between devices with their start and end apart: 5, of which 2 were waited for; matrix products, arithmetic and copies ran while one was open for 1% of the time, Pallas kernels for 4%

profile of v3, /device:TPU:1, one launch (start us, length us, event | category | flops | bytes accessed | tf_op | source)
XLA Modules:
  0.0 100.4 jit_solution(9946077665021012671)
XLA Ops:
  0.6 0.9 copy.11
  1.5 4.9 %collective-permute-start.1 = (bf16[1,64,128]{2,1,0:T(8,128)(2,1)S(1)}, bf16[1,64,128]{2,1,0:T(8,128)(2,1)S(1)}, u32[]{:S(2)}, u32[]{:S(2)}) collective-permute-start(bf16[1,64,128]{2,1,0:T(8,128)(2,1)S(1)} %slice.5), channel_id=1, source_target_pairs={{0,32},{2,34},{4,36},{6,38},{8,40},{10,42},{12,44},{14,46},{16,48}... | collective-permute-start | bytes 49160 | tf_op jit(solution)/shard_map/ppermute | solution.py:215
  6.4 1.3 %collective-permute-start = (bf16[1,64,128]{2,1,0:T(8,128)(2,1)S(1)}, bf16[1,64,128]{2,1,0:T(8,128)(2,1)S(1)}, u32[]{:S(2)}, u32[]{:S(2)}) collective-permute-start(bf16[1,64,128]{2,1,0:T(8,128)(2,1)S(1)} %slice.5), channel_id=1, source_target_pairs={{1,32},{3,34},{5,36},{7,38},{9,40},{11,42},{13,44},{15,46},{17,48}... | collective-permute-start | bytes 49160 | tf_op jit(solution)/shard_map/ppermute | solution.py:213
  7.7 12.0 %collective-permute-start.2 = (bf16[4,64,128]{2,1,0:T(8,128)(2,1)S(1)}, bf16[4,64,128]{2,1,0:T(8,128)(2,1)S(1)}, u32[]{:S(2)}, u32[]{:S(2)}) collective-permute-start(bf16[4,64,128]{2,1,0:T(8,128)(2,1)S(1)} %bitcast.19), channel_id=1, source_target_pairs={{0,1},{1,0},{2,3},{3,2},{4,5},{5,4},{6,7},{7,6},{8,9},{9,8},{10,11... | collective-permute-start | bytes 196616 | tf_op jit(solution)/shard_map/ppermute | solution.py:214
  19.7 0.0 copy-start
  19.8 0.9 copy-done
  20.7 0.0 copy-start.2
  20.7 1.0 %copy-done.2 = bf16[64,1,32,128]{3,2,1,0:T(8,128)(2,1)S(1)} copy-done((bf16[64,1,32,128]{3,2,1,0:T(8,128)(2,1)S(1)}, bf16[64,1,32,128]{3,2,1,0:T(8,128)(2,1)}, u32[]{:S(2)}) %copy-start.2) | copy-done | bytes 524312
  21.7 0.0 copy-start.3
  21.7 0.7 copy-done.3
  22.4 0.0 copy-start.4
  22.4 0.7 copy-done.4
  23.0 2.8 %shard_map.76 = (f32[32,64,128]{2,1,0:T(8,128)S(1)}, bf16[4096,256]{1,0:T(8,128)(2,1)S(1)}, f32[8,128]{1,0:T(8,128)S(1)}) custom-call(s32[1]{0:T(128)} %bitcast.half_ref, f32[9]{0:T(128)S(1)} %copy-done.3, f32[1,64]{1,0:T(1,128)S(1)} %bitcast.22, bf16[64,32,128]{2,1,0:T(8,128)(2,1)S(1)} %bitcast.21, bf16[9,64,64]{2,1,0:T(8,128)(2,1)S(1)} %copy-done), custom_call_target="tpu_custom_call" | custom-call | flops 19327352832 | bytes 134217728 | tf_op jit(solution)/shard_map/pallas_call | solution.py:188
  25.8 0.0 collective-permute-done.1.halo_own_ref
  25.8 0.0 collective-permute-done.halo_other_ref
  25.9 0.0 collective-permute-done.2.other_ref
  25.9 0.1 shard_map.77
  26.0 15.6 %all_to_all.20 = bf16[16,2,64,128]{3,2,1,0:T(8,128)(2,1)S(1)} all-to-all(bf16[16,2,64,128]{3,2,1,0:T(8,128)(2,1)S(1)} %shard_map.77), channel_id=1, replica_groups=mesh['zl'=8,'core'=2,'x'=4,'y'=4,'zh'=2] {'x','y'}, dimensions={0} | all-to-all | bytes 1048576 | tf_op jit(solution)/shard_map/all_to_all | solution.py:255
  41.5 0.0 copy-start.1
  41.5 0.7 shard_map.78
  42.2 15.6 %all_to_all.21.parts_ref = f32[32,8,256]{2,1,0:T(8,128)S(1)} all-to-all(f32[32,8,256]{2,1,0:T(8,128)S(1)} %get-tuple-element.27), channel_id=1, replica_groups=mesh['zl'=8,'core'=2,'x'=4,'y'=4,'zh'=2] {'core','x','y'}, dimensions={0} | all-to-all | bytes 524288 | tf_op jit(solution)/shard_map/all_to_all | solution.py:278
  57.8 0.7 shard_map.79
  58.5 11.6 %all-to-all-start.2 = ((f32[16,8,256]{2,1,0:T(8,128)}), f32[16,8,256]{2,1,0:T(8,128)S(1)}, u32[]{:S(2)}, u32[]{:S(2)}) async-start(f32[16,8,256]{2,1,0:T(8,128)} %shard_map.79), calls=%async_computation.2 | async-start | bytes 262144 | tf_op jit(solution)/shard_map/all_to_all | solution.py:282
  70.1 0.0 copy-done.1
  70.1 0.9 shard_map.80
  71.0 12.4 %all-to-all-done.2.a = f32[16,8,256]{2,1,0:T(8,128)S(1)} async-done(((f32[16,8,256]{2,1,0:T(8,128)}), f32[16,8,256]{2,1,0:T(8,128)S(1)}, u32[]{:S(2)}, u32[]{:S(2)}) %all-to-all-start.2) | async-done | bytes 131104 | tf_op jit(solution)/shard_map/all_to_all | solution.py:282
  83.4 0.7 shard_map.81
  84.2 6.5 %all-to-all-start.3 = ((f32[32,8,256]{2,1,0:T(8,128)}), f32[32,8,256]{2,1,0:T(8,128)S(1)}, u32[]{:S(2)}, u32[]{:S(2)}) async-start(f32[32,8,256]{2,1,0:T(8,128)} %shard_map.81), calls=%async_computation.3 | async-start | bytes 524288 | tf_op jit(solution)/shard_map/all_to_all | solution.py:293
  90.7 1.1 %copy.9 = bf16[64,1,32,128]{3,2,1,0:T(8,128)(2,1)} copy(bf16[64,1,32,128]{3,0,2,1:T(8,128)(2,1)S(1)} %bitcast.16) | data formatting | bytes 1048576
  91.8 7.7 %all-to-all-done.3 = f32[32,8,256]{2,1,0:T(8,128)S(1)} async-done(((f32[32,8,256]{2,1,0:T(8,128)}), f32[32,8,256]{2,1,0:T(8,128)S(1)}, u32[]{:S(2)}, u32[]{:S(2)}) %all-to-all-start.3) | async-done | bytes 262176 | tf_op jit(solution)/shard_map/all_to_all | solution.py:293
  99.5 0.8 shard_map.82
  (1 shorter events, 0.0 us)
Async XLA Ops:
  1.5 24.3 %collective-permute-start.1 = (bf16[1,64,128]{2,1,0:T(8,128)(2,1)S(1)}, bf16[1,64,128]{2,1,0:T(8,128)(2,1)S(1)}, u32[]{:S(2)}, u32[]{:S(2)}) collective-permute-start(bf16[1,64,128]{2,1,0:T(8,128)(2,1)S(1)} %slice.5), channel_id=1, source_target_pairs={{0,32},{2,34},{4,36},{6,38},{8,40},{10,42},{12,44},{14,46},{16,48}... | collective-permute-start | bytes 49160 | tf_op jit(solution)/shard_map/ppermute | solution.py:215
  6.4 19.4 %collective-permute-start = (bf16[1,64,128]{2,1,0:T(8,128)(2,1)S(1)}, bf16[1,64,128]{2,1,0:T(8,128)(2,1)S(1)}, u32[]{:S(2)}, u32[]{:S(2)}) collective-permute-start(bf16[1,64,128]{2,1,0:T(8,128)(2,1)S(1)} %slice.5), channel_id=1, source_target_pairs={{1,32},{3,34},{5,36},{7,38},{9,40},{11,42},{13,44},{15,46},{17,48}... | collective-permute-start | bytes 49160 | tf_op jit(solution)/shard_map/ppermute | solution.py:213
  7.7 18.1 %collective-permute-start.2 = (bf16[4,64,128]{2,1,0:T(8,128)(2,1)S(1)}, bf16[4,64,128]{2,1,0:T(8,128)(2,1)S(1)}, u32[]{:S(2)}, u32[]{:S(2)}) collective-permute-start(bf16[4,64,128]{2,1,0:T(8,128)(2,1)S(1)} %bitcast.19), channel_id=1, source_target_pairs={{0,1},{1,0},{2,3},{3,2},{4,5},{5,4},{6,7},{7,6},{8,9},{9,8},{10,11... | collective-permute-start | bytes 196616 | tf_op jit(solution)/shard_map/ppermute | solution.py:214
  19.7 0.9 copy-start
  20.7 1.0 %copy-start.2 = (bf16[64,1,32,128]{3,2,1,0:T(8,128)(2,1)S(1)}, bf16[64,1,32,128]{3,2,1,0:T(8,128)(2,1)}, u32[]{:S(2)}) copy-start(bf16[64,1,32,128]{3,2,1,0:T(8,128)(2,1)} %param.5) | copy-start | bytes 1572868
  21.7 0.7 copy-start.3
  22.4 0.7 copy-start.4
  41.5 28.6 %copy-start.1 = (bf16[9,64,64]{2,1,0:T(8,128)(2,1)S(1)}, bf16[9,64,64]{2,1,0:T(8,128)(2,1)}, u32[]{:S(2)}) copy-start(bf16[9,64,64]{2,1,0:T(8,128)(2,1)} %weight_ref.1) | copy-start | bytes 221188
  58.5 24.9 %all-to-all-start.2 = ((f32[16,8,256]{2,1,0:T(8,128)}), f32[16,8,256]{2,1,0:T(8,128)S(1)}, u32[]{:S(2)}, u32[]{:S(2)}) async-start(f32[16,8,256]{2,1,0:T(8,128)} %shard_map.79), calls=%async_computation.2 | async-start | bytes 262144 | tf_op jit(solution)/shard_map/all_to_all | solution.py:282
  84.2 15.4 %all-to-all-start.3 = ((f32[32,8,256]{2,1,0:T(8,128)}), f32[32,8,256]{2,1,0:T(8,128)S(1)}, u32[]{:S(2)}, u32[]{:S(2)}) async-start(f32[32,8,256]{2,1,0:T(8,128)} %shard_map.81), calls=%async_computation.3 | async-start | bytes 524288 | tf_op jit(solution)/shard_map/all_to_all | solution.py:293

commit v4 on v3

--- a/solution.py
+++ b/solution.py
@@ -21,7 +21,8 @@
 N_FLAT = 32
 N_GROUP = 16
 N_COLUMN = 16
-PIECE = 8
+PIECE = 4
+LONG = 384
 WIDE = 256
 VMEM_LIMIT = 16 * 1024 * 1024
 
@@ -110,17 +111,23 @@
     for j in range(Y // 2):
         at = slice(j * 2 * X, (j + 1) * 2 * X)
         total += jnp.dot(stack[:, at], turned_ref[at, :], preferred_element_type=jnp.float32)
-    sums_ref[: 3 * C // PIECE] = total.reshape(3 * C // PIECE, PIECE, WIDE)
+    square = (C, C)
+    diagonal = lax.broadcasted_iota(jnp.int32, square, 0) == lax.broadcasted_iota(
+        jnp.int32, square, 1
+    )
     bias = total[C : 2 * C, 3 * C : 3 * C + 1]
-    diagonal = lax.broadcasted_iota(jnp.int32, (C, WIDE), 0) == lax.broadcasted_iota(
-        jnp.int32, (C, WIDE), 1
-    )
     row = jnp.sum(jnp.where(diagonal, bias, 0.0), axis=0, keepdims=True)
-    first = lax.broadcasted_iota(jnp.int32, (PIECE, WIDE), 0) == 0
-    sums_ref[3 * C // PIECE] = jnp.where(first, row, 0.0)
-    sums_ref[3 * C // PIECE + 1 :] = jnp.zeros(
-        (N_FLAT - 3 * C // PIECE - 1, PIECE, WIDE), jnp.float32
-    )
+    first = lax.broadcasted_iota(jnp.int32, square, 0) == 0
+    zero = jnp.zeros(square, jnp.float32)
+    sides = [total[a * C : (a + 1) * C, 2 * C : 3 * C] for a in range(3)]
+    low = jnp.concatenate([sides[0], sides[1]], axis=1)
+    high = jnp.concatenate([sides[2], zero], axis=1)
+    last = jnp.concatenate([jnp.where(first, row, 0.0), zero], axis=1)
+    top = jnp.concatenate([total[:C, : 2 * C], total[2 * C :, : 2 * C], high], axis=1)
+    bottom = jnp.concatenate([total[C : 2 * C, : 2 * C], low, last], axis=1)
+    for half, block in enumerate((top, bottom)):
+        for piece in range(C // PIECE):
+            sums_ref[half * C // PIECE + piece] = block[piece * PIECE : (piece + 1) * PIECE]
 
 
 def input_kernel(grad_ref, g_ref, weight_ref, out_ref, stack, total):
@@ -165,11 +172,26 @@
 
 
 def unpack_kernel(whole_ref, weight_ref, bias_ref):
-    for a in range(3):
-        rows = whole_ref[a * C : (a + 1) * C]
-        for b in range(3):
-            weight_ref[3 * a + b] = rows[:, b * C : (b + 1) * C]
-    bias_ref[...] = whole_ref[3 * C : 3 * C + 1, :C]
+    top, bottom = (
+        jnp.concatenate(
+            [whole_ref[half * C // PIECE + piece] for piece in range(C // PIECE)], axis=0
+        )
+        for half in range(2)
+    )
+    rows = (
+        (top, 0),
+        (top, 1),
+        (bottom, 2),
+        (bottom, 0),
+        (bottom, 1),
+        (bottom, 3),
+        (top, 2),
+        (top, 3),
+        (top, 4),
+    )
+    for tap, (block, place) in enumerate(rows):
+        weight_ref[tap] = block[:, place * C : (place + 1) * C]
+    bias_ref[...] = bottom[0:1, 4 * C : 5 * C]
 
 
 def spread_sum_kernel(parts_ref, out_ref):
@@ -235,8 +257,8 @@
         scalars=2,
         far=2,
     )
-    slope, turned, coef, halo_other, halo_own, other = lax.optimization_barrier(
-        (slope, turned, coef, halo_other, halo_own, other)
+    slope, turned, coef, halo_own, halo_other, other = lax.optimization_barrier(
+        (slope, turned, coef, halo_own, halo_other, other)
     )
     field = call(
         blur_kernel,
@@ -255,7 +277,7 @@
     g_out = lax.all_to_all(field, CROSS, 0, 0, tiled=True).reshape(Y, C, X)
     grad, sums = call(
         weight_kernel,
-        (shape((Y, C, X), bf16), shape((N_FLAT, PIECE, WIDE), f32)),
+        (shape((Y, C, X), bf16), shape((N_FLAT, PIECE, LONG), f32)),
         [pltpu.VMEM((3 * C, Y * X), bf16)],
         flops,
         4 << 20,
@@ -277,20 +299,20 @@
 
     parts = lax.all_to_all(sums, FLAT, 0, 0, tiled=True)
     sent = call(
-        spread_sum_kernel, shape((N_COLUMN, PIECE, WIDE), f32), [], 1 << 16, 1 << 18, parts
+        spread_sum_kernel, shape((N_COLUMN, PIECE, LONG), f32), [], 1 << 16, 1 << 18, parts
     )
     parts = lax.all_to_all(sent, COLUMN, 0, 0, tiled=True)
     parts, grad_input = lax.optimization_barrier((parts, grad_input))
     factor = float(512 * Y * X) ** -0.5
     sent = call(
         lambda a, b: scaled_sum_kernel(factor, a, b),
-        shape((N_FLAT, PIECE, WIDE), f32),
+        shape((N_FLAT, PIECE, LONG), f32),
         [],
         1 << 16,
         1 << 18,
         parts,
     )
-    whole = lax.all_to_all(sent, FLAT, 0, 0, tiled=True).reshape(N_FLAT * PIECE, WIDE)
+    whole = lax.all_to_all(sent, FLAT, 0, 0, tiled=True)
     grad_w, grad_b = call(
         unpack_kernel, (shape((9, C, C), f32), shape((1, C), f32)), [], 1, 1 << 18, whole
     )

time: 101 us -> 97.8 us (0.968)
  starting transfers between devices: 36.4 us -> 35.1 us
  waiting for transfers between devices: 20.1 us -> 18.9 us
    all_to_all x1, blocking collectives: 15.6 us -> 14.1 us  [on_device(): parts = lax.all_to_all(sums, FLAT, 0, 0, tiled=True)]
where the time goes in v4:
time: 97.8 us; the launch traced here: 97.3 us
  starting transfers between devices  35.1 us (36%)
  blocking collectives  30.6 us (31%)
  waiting for transfers between devices  18.9 us (19%)
  Pallas kernels  6.69 us (7%)
  local copies, waits for them, and re-layouts  5.25 us (5%)
    all_to_all x1, blocking collectives, on_device(): g_out = lax.all_to_all(field, CROSS, 0, 0, tiled=True).reshape(Y, C, X)  16.4 us
    all_to_all x1, blocking collectives, on_device(): parts = lax.all_to_all(sums, FLAT, 0, 0, tiled=True)  14.1 us
    ppermute x1, starting transfers between devices, on_device(): other = lax.ppermute(coarse, 'zh', [(0, 1), (1, 0)])  12 us
    all_to_all x1, waiting for transfers between devices, on_device(): parts = lax.all_to_all(sent, COLUMN, 0, 0, tiled=True)  11.8 us
    all_to_all x1, starting transfers between devices, on_device(): parts = lax.all_to_all(sent, COLUMN, 0, 0, tiled=True)  11.1 us
    all_to_all x1, waiting for transfers between devices, on_device(): whole = lax.all_to_all(sent, FLAT, 0, 0, tiled=True)  7.09 us
    pallas_call x7, Pallas kernels, call(): pl.pallas_call(kernel, out_shape=outs, in_specs=[pl.BlockSpec(memory_spac...  6.69 us
    all_to_all x1, starting transfers between devices, on_device(): whole = lax.all_to_all(sent, FLAT, 0, 0, tiled=True)  5.78 us
  transfers between devices with their start and end apart: 5, of which 2 were waited for; matrix products, arithmetic and copies ran while one was open for 1% of the time, Pallas kernels for 4%

profile of v4, /device:TPU:1, one launch (start us, length us, event | category | flops | bytes accessed | tf_op | source)
XLA Modules:
  0.0 97.3 jit_solution(10753983633216827188)
XLA Ops:
  0.6 0.9 copy.11
  1.5 1.3 %collective-permute-start.1 = (bf16[1,64,128]{2,1,0:T(8,128)(2,1)S(1)}, bf16[1,64,128]{2,1,0:T(8,128)(2,1)S(1)}, u32[]{:S(2)}, u32[]{:S(2)}) collective-permute-start(bf16[1,64,128]{2,1,0:T(8,128)(2,1)S(1)} %slice.5), channel_id=1, source_target_pairs={{1,32},{3,34},{5,36},{7,38},{9,40},{11,42},{13,44},{15,46},{17,48}... | collective-permute-start | bytes 49160 | tf_op jit(solution)/shard_map/ppermute | solution.py:235
  2.8 4.9 %collective-permute-start = (bf16[1,64,128]{2,1,0:T(8,128)(2,1)S(1)}, bf16[1,64,128]{2,1,0:T(8,128)(2,1)S(1)}, u32[]{:S(2)}, u32[]{:S(2)}) collective-permute-start(bf16[1,64,128]{2,1,0:T(8,128)(2,1)S(1)} %slice.5), channel_id=1, source_target_pairs={{0,32},{2,34},{4,36},{6,38},{8,40},{10,42},{12,44},{14,46},{16,48}... | collective-permute-start | bytes 49160 | tf_op jit(solution)/shard_map/ppermute | solution.py:237
  7.7 12.0 %collective-permute-start.2 = (bf16[4,64,128]{2,1,0:T(8,128)(2,1)S(1)}, bf16[4,64,128]{2,1,0:T(8,128)(2,1)S(1)}, u32[]{:S(2)}, u32[]{:S(2)}) collective-permute-start(bf16[4,64,128]{2,1,0:T(8,128)(2,1)S(1)} %bitcast.17), channel_id=1, source_target_pairs={{0,1},{1,0},{2,3},{3,2},{4,5},{5,4},{6,7},{7,6},{8,9},{9,8},{10,11... | collective-permute-start | bytes 196616 | tf_op jit(solution)/shard_map/ppermute | solution.py:236
  19.7 0.0 copy-start
  19.8 0.9 copy-done
  20.7 0.0 copy-start.2
  20.7 1.0 %copy-done.2 = bf16[64,1,32,128]{3,2,1,0:T(8,128)(2,1)S(1)} copy-done((bf16[64,1,32,128]{3,2,1,0:T(8,128)(2,1)S(1)}, bf16[64,1,32,128]{3,2,1,0:T(8,128)(2,1)}, u32[]{:S(2)}) %copy-start.2) | copy-done | bytes 524312
  21.7 0.0 copy-start.3
  21.7 0.7 copy-done.3
  22.4 0.0 copy-start.4
  22.4 0.7 copy-done.4
  23.0 2.8 %shard_map.76 = (f32[32,64,128]{2,1,0:T(8,128)S(1)}, bf16[4096,256]{1,0:T(8,128)(2,1)S(1)}, f32[8,128]{1,0:T(8,128)S(1)}) custom-call(s32[1]{0:T(128)} %bitcast.half_ref, f32[9]{0:T(128)S(1)} %copy-done.3, f32[1,64]{1,0:T(1,128)S(1)} %bitcast.20, bf16[64,32,128]{2,1,0:T(8,128)(2,1)S(1)} %bitcast.19, bf16[9,64,64]{2,1,0:T(8,128)(2,1)S(1)} %copy-done), custom_call_target="tpu_custom_call" | custom-call | flops 19327352832 | bytes 134217728 | tf_op jit(solution)/shard_map/pallas_call | solution.py:210
  25.8 0.0 collective-permute-done.1.halo_other_ref
  25.8 0.0 collective-permute-done.halo_own_ref
  25.9 0.0 collective-permute-done.2.other_ref
  25.9 0.1 shard_map.77
  26.0 16.4 %all_to_all.20 = bf16[16,2,64,128]{3,2,1,0:T(8,128)(2,1)S(1)} all-to-all(bf16[16,2,64,128]{3,2,1,0:T(8,128)(2,1)S(1)} %shard_map.77), channel_id=1, replica_groups=mesh['zl'=8,'core'=2,'x'=4,'y'=4,'zh'=2] {'x','y'}, dimensions={0} | all-to-all | bytes 1048576 | tf_op jit(solution)/shard_map/all_to_all | solution.py:277
  42.4 0.0 copy-start.1
  42.4 0.7 shard_map.78
  43.1 14.1 %all_to_all.21.parts_ref = f32[32,4,384]{2,1,0:T(4,128)S(1)} all-to-all(f32[32,4,384]{2,1,0:T(4,128)S(1)} %get-tuple-element.27), channel_id=1, replica_groups=mesh['zl'=8,'core'=2,'x'=4,'y'=4,'zh'=2] {'core','x','y'}, dimensions={0} | all-to-all | bytes 393216 | tf_op jit(solution)/shard_map/all_to_all | solution.py:300
  57.2 0.7 shard_map.79
  57.9 11.1 %all-to-all-start.2 = ((f32[16,4,384]{2,1,0:T(4,128)}), f32[16,4,384]{2,1,0:T(4,128)S(1)}, u32[]{:S(2)}, u32[]{:S(2)}) async-start(f32[16,4,384]{2,1,0:T(4,128)} %shard_map.79), calls=%async_computation.2 | async-start | bytes 196608 | tf_op jit(solution)/shard_map/all_to_all | solution.py:304
  69.0 0.0 copy-done.1
  69.0 0.9 shard_map.80
  69.9 11.8 %all-to-all-done.2.a = f32[16,4,384]{2,1,0:T(4,128)S(1)} async-done(((f32[16,4,384]{2,1,0:T(4,128)}), f32[16,4,384]{2,1,0:T(4,128)S(1)}, u32[]{:S(2)}, u32[]{:S(2)}) %all-to-all-start.2) | async-done | bytes 98336 | tf_op jit(solution)/shard_map/all_to_all | solution.py:304
  81.7 0.7 shard_map.81
  82.4 5.8 %all-to-all-start.3 = ((f32[32,4,384]{2,1,0:T(4,128)}), f32[32,4,384]{2,1,0:T(4,128)S(1)}, u32[]{:S(2)}, u32[]{:S(2)}) async-start(f32[32,4,384]{2,1,0:T(4,128)} %shard_map.81), calls=%async_computation.3 | async-start | bytes 393216 | tf_op jit(solution)/shard_map/all_to_all | solution.py:315
  88.2 1.1 %copy.9 = bf16[64,1,32,128]{3,2,1,0:T(8,128)(2,1)} copy(bf16[64,1,32,128]{3,0,2,1:T(8,128)(2,1)S(1)} %bitcast.15) | data formatting | bytes 1048576
  89.3 7.1 %all-to-all-done.3.whole_ref = f32[32,4,384]{2,1,0:T(4,128)S(1)} async-done(((f32[32,4,384]{2,1,0:T(4,128)}), f32[32,4,384]{2,1,0:T(4,128)S(1)}, u32[]{:S(2)}, u32[]{:S(2)}) %all-to-all-start.3) | async-done | bytes 196640 | tf_op jit(solution)/shard_map/all_to_all | solution.py:315
  96.4 0.8 shard_map.82
  (1 shorter events, 0.0 us)
Async XLA Ops:
  1.5 24.3 %collective-permute-start.1 = (bf16[1,64,128]{2,1,0:T(8,128)(2,1)S(1)}, bf16[1,64,128]{2,1,0:T(8,128)(2,1)S(1)}, u32[]{:S(2)}, u32[]{:S(2)}) collective-permute-start(bf16[1,64,128]{2,1,0:T(8,128)(2,1)S(1)} %slice.5), channel_id=1, source_target_pairs={{1,32},{3,34},{5,36},{7,38},{9,40},{11,42},{13,44},{15,46},{17,48}... | collective-permute-start | bytes 49160 | tf_op jit(solution)/shard_map/ppermute | solution.py:235
  2.8 23.1 %collective-permute-start = (bf16[1,64,128]{2,1,0:T(8,128)(2,1)S(1)}, bf16[1,64,128]{2,1,0:T(8,128)(2,1)S(1)}, u32[]{:S(2)}, u32[]{:S(2)}) collective-permute-start(bf16[1,64,128]{2,1,0:T(8,128)(2,1)S(1)} %slice.5), channel_id=1, source_target_pairs={{0,32},{2,34},{4,36},{6,38},{8,40},{10,42},{12,44},{14,46},{16,48}... | collective-permute-start | bytes 49160 | tf_op jit(solution)/shard_map/ppermute | solution.py:237
  7.7 18.1 %collective-permute-start.2 = (bf16[4,64,128]{2,1,0:T(8,128)(2,1)S(1)}, bf16[4,64,128]{2,1,0:T(8,128)(2,1)S(1)}, u32[]{:S(2)}, u32[]{:S(2)}) collective-permute-start(bf16[4,64,128]{2,1,0:T(8,128)(2,1)S(1)} %bitcast.17), channel_id=1, source_target_pairs={{0,1},{1,0},{2,3},{3,2},{4,5},{5,4},{6,7},{7,6},{8,9},{9,8},{10,11... | collective-permute-start | bytes 196616 | tf_op jit(solution)/shard_map/ppermute | solution.py:236
  19.7 0.9 copy-start
  20.7 1.0 %copy-start.2 = (bf16[64,1,32,128]{3,2,1,0:T(8,128)(2,1)S(1)}, bf16[64,1,32,128]{3,2,1,0:T(8,128)(2,1)}, u32[]{:S(2)}) copy-start(bf16[64,1,32,128]{3,2,1,0:T(8,128)(2,1)} %param.5) | copy-start | bytes 1572868
  21.7 0.7 copy-start.3
  22.4 0.7 copy-start.4
  42.4 26.6 %copy-start.1 = (bf16[9,64,64]{2,1,0:T(8,128)(2,1)S(1)}, bf16[9,64,64]{2,1,0:T(8,128)(2,1)}, u32[]{:S(2)}) copy-start(bf16[9,64,64]{2,1,0:T(8,128)(2,1)} %weight_ref.1) | copy-start | bytes 221188
  57.9 23.8 %all-to-all-start.2 = ((f32[16,4,384]{2,1,0:T(4,128)}), f32[16,4,384]{2,1,0:T(4,128)S(1)}, u32[]{:S(2)}, u32[]{:S(2)}) async-start(f32[16,4,384]{2,1,0:T(4,128)} %shard_map.79), calls=%async_computation.2 | async-start | bytes 196608 | tf_op jit(solution)/shard_map/all_to_all | solution.py:304
  82.4 14.0 %all-to-all-start.3 = ((f32[32,4,384]{2,1,0:T(4,128)}), f32[32,4,384]{2,1,0:T(4,128)S(1)}, u32[]{:S(2)}, u32[]{:S(2)}) async-start(f32[32,4,384]{2,1,0:T(4,128)} %shard_map.81), calls=%async_computation.3 | async-start | bytes 393216 | tf_op jit(solution)/shard_map/all_to_all | solution.py:315

commit v5 on v4

--- a/solution.py
+++ b/solution.py
@@ -21,6 +21,7 @@
 N_FLAT = 32
 N_GROUP = 16
 N_COLUMN = 16
+FIRST = 6
 PIECE = 4
 LONG = 384
 WIDE = 256
@@ -156,18 +157,24 @@
         out_ref[y] = (g_ref[y].astype(jnp.float32) + conv).astype(jnp.bfloat16)
 
 
-def blur_kernel(half_ref, taps_ref, own_ref, other_ref, halo_own_ref, halo_other_ref, out_ref):
+def turn_kernel(own_ref, other_ref, rows_ref, last_ref):
+    for slot, raw_ref in enumerate((own_ref, other_ref)):
+        rows = jnp.swapaxes(raw_ref[...].astype(jnp.float32), 0, 1).astype(jnp.bfloat16)
+        rows_ref[slot] = rows
+        last_ref[slot] = rows[3]
+
+
+def blur_kernel(half_ref, taps_ref, rows_ref, halo_ref, out_ref):
     half = half_ref[0]
-    sides = ((half, own_ref, halo_own_ref), (1 - half, other_ref, halo_other_ref))
-    for slot, rows_ref, halo_ref in sides:
-        before = halo_ref[0].astype(jnp.float32)
+    for slot, place in enumerate((half, 1 - half)):
+        before = halo_ref[slot].astype(jnp.float32)
         for k in range(4):
-            row = rows_ref[k].astype(jnp.float32)
+            row = rows_ref[slot, k].astype(jnp.float32)
             for pair in range(4):
                 value = taps_ref[pair : pair + 1] * row
                 if pair == 0:
                     value = value + taps_ref[4:5] * before
-                out_ref[4 * k + pair, slot] = value.astype(jnp.bfloat16)
+                out_ref[4 * k + pair, place] = value.astype(jnp.bfloat16)
             before = row
 
 
@@ -223,18 +230,8 @@
 def on_device(activations, cotangent, weight, conv_bias, blur_taps):
     shape = jax.ShapeDtypeStruct
     bf16, f32 = jnp.bfloat16, jnp.float32
-    coarse = cotangent[:, :, 0, :].transpose(1, 0, 2)
-    hops = [
-        [
-            ((group * N_CROSS + cross) * 2 + side, ((group + 1) * N_CROSS + cross) * 2)
-            for group in range(N_GROUP - 1)
-            for cross in range(N_CROSS)
-        ]
-        for side in range(2)
-    ]
-    halo_other = lax.ppermute(coarse[3:], AXES, hops[1])
-    other = lax.ppermute(coarse, "zh", [(0, 1), (1, 0)])
-    halo_own = lax.ppermute(coarse[3:], AXES, hops[0])
+    raw = cotangent[:, :, 0, :]
+    other = lax.ppermute(raw, "zh", [(0, 1), (1, 0)])
     half = lax.axis_index("zh").astype(jnp.int32)[None]
     flops = 2 * Y * X * 9 * C * C
     slope, turned, coef = call(
@@ -257,9 +254,22 @@
         scalars=2,
         far=2,
     )
-    slope, turned, coef, halo_own, halo_other, other = lax.optimization_barrier(
-        (slope, turned, coef, halo_own, halo_other, other)
-    )
+    slope, turned, coef, raw = lax.optimization_barrier((slope, turned, coef, raw))
+    rows, last = call(
+        turn_kernel,
+        (shape((2, 4, C, X), bf16), shape((2, C, X), bf16)),
+        [],
+        1 << 16,
+        1 << 18,
+        raw,
+        other,
+    )
+    hops = [
+        ((group * N_CROSS + cross) * 2, ((group + 1) * N_CROSS + cross) * 2)
+        for group in range(N_GROUP - 1)
+        for cross in range(N_CROSS)
+    ]
+    halo = lax.ppermute(last, AXES, hops)
     field = call(
         blur_kernel,
         shape((N_CROSS, 2, C, X), bf16),
@@ -268,10 +278,8 @@
         1 << 20,
         half,
         coef,
-        coarse,
-        other,
-        halo_own,
-        halo_other,
+        rows,
+        halo,
         scalars=1,
     )
     g_out = lax.all_to_all(field, CROSS, 0, 0, tiled=True).reshape(Y, C, X)
@@ -301,7 +309,15 @@
     sent = call(
         spread_sum_kernel, shape((N_COLUMN, PIECE, LONG), f32), [], 1 << 16, 1 << 18, parts
     )
-    parts = lax.all_to_all(sent, COLUMN, 0, 0, tiled=True)
+    columns = [
+        [
+            (((z % 8) * 2 + core) * N_CROSS + cross) * 2 + z // 8
+            for z in [(FIRST + step) % N_COLUMN for step in range(N_COLUMN)]
+        ]
+        for core in range(2)
+        for cross in range(N_CROSS)
+    ]
+    parts = lax.all_to_all(sent, AXES, 0, 0, axis_index_groups=columns, tiled=True)
     parts, grad_input = lax.optimization_barrier((parts, grad_input))
     factor = float(512 * Y * X) ** -0.5
     sent = call(

time: 97.8 us -> 91.7 us (0.938)
  waiting for transfers between devices: 18.9 us -> 14.8 us
    all_to_all x1, waiting for transfers between devices: 11.8 us -> 6.73 us  [on_device(): lax.all_to_all(sent, AXES, 0, 0, axis_index_groups=columns, tiled=True)]
    all_to_all x1, blocking collectives: 14.1 us -> 11.9 us  [on_device(): parts = lax.all_to_all(sums, FLAT, 0, 0, tiled=True)]
    ppermute x3 -> x2, starting transfers between devices: 18.2 us -> 19.8 us  [the longest x1 16.3 us: on_device(): other = lax.ppermute(raw, 'zh', [(0, 1), (1, 0)])]
    all_to_all x1, starting transfers between devices: 11.1 us -> 9.67 us  [on_device(): lax.all_to_all(sent, AXES, 0, 0, axis_index_groups=columns, tiled=True)]
    all_to_all x1, blocking collectives: 16.4 us -> 17.8 us  [on_device(): g_out = lax.all_to_all(field, CROSS, 0, 0, tiled=True).reshape(Y, C, X)]
    ppermute x3 -> x2, waiting for transfers between devices: 0.01 us -> 1 us  [the longest x1 1 us: on_device(): halo = lax.ppermute(last, AXES, hops)]
    unnamed x12 -> x13, local copies, waits for them, and re-layouts: 5.25 us -> 4.4 us
    pallas_call x7 -> x8, Pallas kernels: 6.69 us -> 6.77 us  [call(): pl.pallas_call(kernel, out_shape=outs, in_specs=[pl.BlockSpec(memory_spac...]
  transfers between devices with their start and end apart: 5 -> 4, of which waited for: 2 -> 3; matrix products, arithmetic and copies ran while one was open for 1% -> 1% of each run, Pallas kernels for 4% -> 4%
where the time goes in v5:
time: 91.7 us; the launch traced here: 91.3 us
  starting transfers between devices  34.8 us (38%)
  blocking collectives  29.8 us (32%)
  waiting for transfers between devices  14.8 us (16%)
  Pallas kernels  6.77 us (7%)
  local copies, waits for them, and re-layouts  4.4 us (5%)
    all_to_all x1, blocking collectives, on_device(): g_out = lax.all_to_all(field, CROSS, 0, 0, tiled=True).reshape(Y, C, X)  17.8 us
    ppermute x1, starting transfers between devices, on_device(): other = lax.ppermute(raw, 'zh', [(0, 1), (1, 0)])  16.3 us
    all_to_all x1, blocking collectives, on_device(): parts = lax.all_to_all(sums, FLAT, 0, 0, tiled=True)  11.9 us
    all_to_all x1, starting transfers between devices, on_device(): lax.all_to_all(sent, AXES, 0, 0, axis_index_groups=columns, tiled=True)  9.67 us
    all_to_all x1, waiting for transfers between devices, on_device(): whole = lax.all_to_all(sent, FLAT, 0, 0, tiled=True)  7.09 us
    pallas_call x8, Pallas kernels, call(): pl.pallas_call(kernel, out_shape=outs, in_specs=[pl.BlockSpec(memory_spac...  6.77 us
    all_to_all x1, waiting for transfers between devices, on_device(): lax.all_to_all(sent, AXES, 0, 0, axis_index_groups=columns, tiled=True)  6.73 us
    all_to_all x1, starting transfers between devices, on_device(): whole = lax.all_to_all(sent, FLAT, 0, 0, tiled=True)  5.36 us
  transfers between devices with their start and end apart: 4, of which 3 were waited for; matrix products, arithmetic and copies ran while one was open for 1% of the time, Pallas kernels for 4%

profile of v5, /device:TPU:1, one launch (start us, length us, event | category | flops | bytes accessed | tf_op | source)
XLA Modules:
  0.0 91.3 jit_solution(2792489961826229823)
XLA Ops:
  0.6 16.3 %collective-permute-start = (bf16[64,4,128]{2,1,0:T(4,128)(2,1)}, bf16[64,4,128]{2,1,0:T(4,128)(2,1)S(1)}, u32[]{:S(2)}, u32[]{:S(2)}) collective-permute-start(bf16[64,4,128]{2,1,0:T(4,128)(2,1)} %bitcast.12), channel_id=1, source_target_pairs={{0,1},{1,0},{2,3},{3,2},{4,5},{5,4},{6,7},{7,6},{8,9},{9,8},{10,11... | collective-permute-start | bytes 196616 | tf_op jit(solution)/shard_map/ppermute | solution.py:234
  16.9 0.0 copy-start
  16.9 0.9 copy-done
  17.8 0.0 copy-start.3
  17.8 1.0 %copy-done.3 = bf16[64,1,32,128]{3,2,1,0:T(8,128)(2,1)S(1)} copy-done((bf16[64,1,32,128]{3,2,1,0:T(8,128)(2,1)S(1)}, bf16[64,1,32,128]{3,2,1,0:T(8,128)(2,1)}, u32[]{:S(2)}) %copy-start.3) | copy-done | bytes 524312
  18.9 0.0 copy-start.4
  18.9 0.7 copy-done.4
  19.5 0.0 copy-start.5
  19.5 0.7 copy-done.5
  20.2 0.0 copy-start.2
  20.2 2.8 %shard_map.76 = (f32[32,64,128]{2,1,0:T(8,128)S(1)}, bf16[4096,256]{1,0:T(8,128)(2,1)S(1)}, f32[8,128]{1,0:T(8,128)S(1)}) custom-call(s32[1]{0:T(128)} %bitcast.half_ref, f32[9]{0:T(128)S(1)} %copy-done.4, f32[1,64]{1,0:T(1,128)S(1)} %bitcast.15, bf16[64,32,128]{2,1,0:T(8,128)(2,1)S(1)} %bitcast.14, bf16[9,64,64]{2,1,0:T(8,128)(2,1)S(1)} %copy-done), custom_call_target="tpu_custom_call" | custom-call | flops 19327352832 | bytes 134217728 | tf_op jit(solution)/shard_map/pallas_call | solution.py:217
  23.0 0.0 collective-permute-done.other_ref
  23.0 0.0 copy-done.2
  23.0 0.1 shard_map.77
  23.1 3.5 %collective-permute-start.1 = (bf16[2,64,128]{2,1,0:T(8,128)(2,1)S(1)}, bf16[2,64,128]{2,1,0:T(8,128)(2,1)S(1)}, u32[]{:S(2)}, u32[]{:S(2)}) collective-permute-start(bf16[2,64,128]{2,1,0:T(8,128)(2,1)S(1)} %get-tuple-element.24), channel_id=1, source_target_pairs={{0,32},{2,34},{4,36},{6,38},{8,40},{10,42},{12,44},{14,46},{16,48}... | collective-permute-start | bytes 98312 | tf_op jit(solution)/shard_map/ppermute | solution.py:272
  26.6 1.0 %collective-permute-done.1.halo_ref = bf16[2,64,128]{2,1,0:T(8,128)(2,1)S(1)} collective-permute-done((bf16[2,64,128]{2,1,0:T(8,128)(2,1)S(1)}, bf16[2,64,128]{2,1,0:T(8,128)(2,1)S(1)}, u32[]{:S(2)}, u32[]{:S(2)}) %collective-permute-start.1) | collective-permute-done | bytes 32800 | tf_op jit(solution)/shard_map/ppermute | solution.py:272
  27.6 0.1 shard_map.78
  27.7 17.8 %all_to_all.20 = bf16[16,2,64,128]{3,2,1,0:T(8,128)(2,1)S(1)} all-to-all(bf16[16,2,64,128]{3,2,1,0:T(8,128)(2,1)S(1)} %shard_map.78), channel_id=1, replica_groups=mesh['zl'=8,'core'=2,'x'=4,'y'=4,'zh'=2] {'x','y'}, dimensions={0} | all-to-all | bytes 1048576 | tf_op jit(solution)/shard_map/all_to_all | solution.py:285
  45.5 0.0 copy-start.1
  45.5 0.7 shard_map.79
  46.2 11.9 %all_to_all.21.parts_ref = f32[32,4,384]{2,1,0:T(4,128)S(1)} all-to-all(f32[32,4,384]{2,1,0:T(4,128)S(1)} %get-tuple-element.27), channel_id=1, replica_groups=mesh['zl'=8,'core'=2,'x'=4,'y'=4,'zh'=2] {'core','x','y'}, dimensions={0} | all-to-all | bytes 393216 | tf_op jit(solution)/shard_map/all_to_all | solution.py:308
  58.2 0.7 shard_map.80
  58.9 9.7 %all-to-all-start.2 = ((f32[16,4,384]{2,1,0:T(4,128)}), f32[16,4,384]{2,1,0:T(4,128)S(1)}, u32[]{:S(2)}, u32[]{:S(2)}) async-start(f32[16,4,384]{2,1,0:T(4,128)} %shard_map.80), calls=%async_computation.2 | async-start | bytes 196608 | tf_op jit(solution)/shard_map/all_to_all | solution.py:320
  68.5 0.0 copy-done.1
  68.6 0.9 shard_map.81
  69.4 6.7 %all-to-all-done.2.a = f32[16,4,384]{2,1,0:T(4,128)S(1)} async-done(((f32[16,4,384]{2,1,0:T(4,128)}), f32[16,4,384]{2,1,0:T(4,128)S(1)}, u32[]{:S(2)}, u32[]{:S(2)}) %all-to-all-start.2) | async-done | bytes 98336 | tf_op jit(solution)/shard_map/all_to_all | solution.py:320
  76.1 0.7 shard_map.82
  76.9 5.4 %all-to-all-start.3 = ((f32[32,4,384]{2,1,0:T(4,128)}), f32[32,4,384]{2,1,0:T(4,128)S(1)}, u32[]{:S(2)}, u32[]{:S(2)}) async-start(f32[32,4,384]{2,1,0:T(4,128)} %shard_map.82), calls=%async_computation.3 | async-start | bytes 393216 | tf_op jit(solution)/shard_map/all_to_all | solution.py:331
  82.2 1.1 %copy.8 = bf16[64,1,32,128]{3,2,1,0:T(8,128)(2,1)} copy(bf16[64,1,32,128]{3,0,2,1:T(8,128)(2,1)S(1)} %bitcast.11) | data formatting | bytes 1048576
  83.4 7.1 %all-to-all-done.3.whole_ref = f32[32,4,384]{2,1,0:T(4,128)S(1)} async-done(((f32[32,4,384]{2,1,0:T(4,128)}), f32[32,4,384]{2,1,0:T(4,128)S(1)}, u32[]{:S(2)}, u32[]{:S(2)}) %all-to-all-start.3) | async-done | bytes 196640 | tf_op jit(solution)/shard_map/all_to_all | solution.py:331
  90.5 0.8 shard_map.83
Async XLA Ops:
  0.6 22.4 %collective-permute-start = (bf16[64,4,128]{2,1,0:T(4,128)(2,1)}, bf16[64,4,128]{2,1,0:T(4,128)(2,1)S(1)}, u32[]{:S(2)}, u32[]{:S(2)}) collective-permute-start(bf16[64,4,128]{2,1,0:T(4,128)(2,1)} %bitcast.12), channel_id=1, source_target_pairs={{0,1},{1,0},{2,3},{3,2},{4,5},{5,4},{6,7},{7,6},{8,9},{9,8},{10,11... | collective-permute-start | bytes 196616 | tf_op jit(solution)/shard_map/ppermute | solution.py:234
  16.9 0.9 %copy-start = (bf16[9,64,64]{2,1,0:T(8,128)(2,1)S(1)}, bf16[9,64,64]{2,1,0:T(8,128)(2,1)}, u32[]{:S(2)}) copy-start(bf16[9,64,64]{2,1,0:T(8,128)(2,1)} %weight_ref.1) | copy-start | bytes 221188
  17.8 1.0 %copy-start.3 = (bf16[64,1,32,128]{3,2,1,0:T(8,128)(2,1)S(1)}, bf16[64,1,32,128]{3,2,1,0:T(8,128)(2,1)}, u32[]{:S(2)}) copy-start(bf16[64,1,32,128]{3,2,1,0:T(8,128)(2,1)} %param.5) | copy-start | bytes 1572868
  18.9 0.7 copy-start.4
  19.5 0.7 copy-start.5
  20.2 2.8 %copy-start.2 = (bf16[64,4,1,128]{3,1,2,0:T(4,128)(2,1)S(1)}, bf16[64,4,1,128]{3,1,2,0:T(4,128)(2,1)}, u32[]{:S(2)}) copy-start(bf16[64,4,1,128]{3,1,2,0:T(4,128)(2,1)} %param.6) | copy-start | bytes 196612
  23.1 4.5 %collective-permute-start.1 = (bf16[2,64,128]{2,1,0:T(8,128)(2,1)S(1)}, bf16[2,64,128]{2,1,0:T(8,128)(2,1)S(1)}, u32[]{:S(2)}, u32[]{:S(2)}) collective-permute-start(bf16[2,64,128]{2,1,0:T(8,128)(2,1)S(1)} %get-tuple-element.24), channel_id=1, source_target_pairs={{0,32},{2,34},{4,36},{6,38},{8,40},{10,42},{12,44},{14,46},{16,48}... | collective-permute-start | bytes 98312 | tf_op jit(solution)/shard_map/ppermute | solution.py:272
  45.5 23.0 %copy-start.1 = (bf16[9,64,64]{2,1,0:T(8,128)(2,1)S(1)}, bf16[9,64,64]{2,1,0:T(8,128)(2,1)}, u32[]{:S(2)}) copy-start(bf16[9,64,64]{2,1,0:T(8,128)(2,1)} %weight_ref.1) | copy-start | bytes 221188
  58.9 17.3 %all-to-all-start.2 = ((f32[16,4,384]{2,1,0:T(4,128)}), f32[16,4,384]{2,1,0:T(4,128)S(1)}, u32[]{:S(2)}, u32[]{:S(2)}) async-start(f32[16,4,384]{2,1,0:T(4,128)} %shard_map.80), calls=%async_computation.2 | async-start | bytes 196608 | tf_op jit(solution)/shard_map/all_to_all | solution.py:320
  76.9 13.6 %all-to-all-start.3 = ((f32[32,4,384]{2,1,0:T(4,128)}), f32[32,4,384]{2,1,0:T(4,128)S(1)}, u32[]{:S(2)}, u32[]{:S(2)}) async-start(f32[32,4,384]{2,1,0:T(4,128)} %shard_map.82), calls=%async_computation.3 | async-start | bytes 393216 | tf_op jit(solution)/shard_map/all_to_all | solution.py:331

commit v6 on v5

--- a/solution.py
+++ b/solution.py
@@ -14,10 +14,7 @@
 SIZES = (8, 2, 4, 4, 2)
 GROUP = ("zl", "core")
 PLANE = ("x", "y", "zh")
-CROSS = ("x", "y")
 N_CROSS = 16
-FLAT = ("core", "x", "y")
-COLUMN = ("zl", "zh")
 N_FLAT = 32
 N_GROUP = 16
 N_COLUMN = 16
@@ -26,6 +23,11 @@
 LONG = 384
 WIDE = 256
 VMEM_LIMIT = 16 * 1024 * 1024
+CORNER = 3
+CROSS_ORDER = [
+    ((CORNER + a) % 4, (CORNER + b) % 4) for a in range(4) for b in range(4)
+]
+PLACE = [CROSS_ORDER.index((y // 8, y // 2 % 4)) * 2 + y % 2 for y in range(Y)]
 
 
 def shifted(row, step):
@@ -102,7 +104,7 @@
     stack[0:C, (Y - 1) * X :] = zero
     stack[2 * C :, 0:X] = zero
     for y in range(Y):
-        grad = (g_ref[y].astype(jnp.float32) * slope_ref[y]).astype(jnp.bfloat16)
+        grad = (g_ref[PLACE[y]].astype(jnp.float32) * slope_ref[y]).astype(jnp.bfloat16)
         grad_ref[y] = grad
         for a in range(3):
             row = y + a - 1
@@ -152,9 +154,13 @@
         for a in range(3):
             place = slice(at + a * X, at + (a + 2) * X)
             total[:, place] += part[a * C : (a + 1) * C]
-    for y in range(Y):
-        conv = total[:, (y + 1) * X : (y + 2) * X]
-        out_ref[y] = (g_ref[y].astype(jnp.float32) + conv).astype(jnp.bfloat16)
+    for y in range(0, Y, 16):
+        rows = []
+        for row in range(y, y + 16):
+            conv = total[:, (row + 1) * X : (row + 2) * X]
+            rows.append(g_ref[PLACE[row]].astype(jnp.float32) + conv)
+        turned = jnp.swapaxes(jnp.stack(rows), 0, 1)
+        out_ref[:, y : y + 16] = turned.astype(jnp.bfloat16)
 
 
 def turn_kernel(own_ref, other_ref, rows_ref, last_ref):
@@ -174,7 +180,7 @@
                 value = taps_ref[pair : pair + 1] * row
                 if pair == 0:
                     value = value + taps_ref[4:5] * before
-                out_ref[4 * k + pair, place] = value.astype(jnp.bfloat16)
+                out_ref[CROSS_ORDER.index((k, pair)), place] = value.astype(jnp.bfloat16)
             before = row
 
 
@@ -282,7 +288,13 @@
         halo,
         scalars=1,
     )
-    g_out = lax.all_to_all(field, CROSS, 0, 0, tiled=True).reshape(Y, C, X)
+    crosses = [
+        [(group * 4 + x) * 8 + y * 2 + zh for x, y in CROSS_ORDER]
+        for group in range(N_GROUP)
+        for zh in range(2)
+    ]
+    g_out = lax.all_to_all(field, AXES, 0, 0, axis_index_groups=crosses, tiled=True)
+    g_out = g_out.reshape(Y, C, X)
     grad, sums = call(
         weight_kernel,
         (shape((Y, C, X), bf16), shape((N_FLAT, PIECE, LONG), f32)),
@@ -293,9 +305,9 @@
         slope,
         turned,
     )
-    out = call(
+    grad_input = call(
         input_kernel,
-        shape((Y, C, X), bf16),
+        shape((C, Y, X), bf16),
         [pltpu.VMEM((3 * C, Y * X), bf16), pltpu.VMEM((C, (Y + 2) * X), f32)],
         flops,
         2 << 20,
@@ -303,9 +315,13 @@
         g_out,
         weight,
     )
-    grad_input = out.transpose(1, 0, 2)[:, None]
-
-    parts = lax.all_to_all(sums, FLAT, 0, 0, tiled=True)
+
+    flats = [
+        [((zl * 2 + core) * 4 + x) * 8 + y * 2 + zh for core in range(2) for x, y in CROSS_ORDER]
+        for zl in range(8)
+        for zh in range(2)
+    ]
+    parts = lax.all_to_all(sums, AXES, 0, 0, axis_index_groups=flats, tiled=True)
     sent = call(
         spread_sum_kernel, shape((N_COLUMN, PIECE, LONG), f32), [], 1 << 16, 1 << 18, parts
     )
@@ -328,11 +344,11 @@
         1 << 18,
         parts,
     )
-    whole = lax.all_to_all(sent, FLAT, 0, 0, tiled=True)
+    whole = lax.all_to_all(sent, AXES, 0, 0, axis_index_groups=flats, tiled=True)
     grad_w, grad_b = call(
         unpack_kernel, (shape((9, C, C), f32), shape((1, C), f32)), [], 1, 1 << 18, whole
     )
-    return grad_input, grad_w, grad_b.reshape(C)
+    return grad_input[:, None], grad_w, grad_b.reshape(C)
 
 
 def solution(mesh):

time: 91.7 us -> 88.3 us (0.963)
  blocking collectives: 29.8 us -> 40.6 us
  waiting for transfers between devices: 14.8 us -> 6.75 us
  starting transfers between devices: 34.8 us -> 29.5 us
  local copies, waits for them, and re-layouts: 4.4 us -> 3.26 us
    all_to_all x2 -> x3, blocking collectives: 29.8 us -> 40.6 us  [the longest x1 14.9 us: on_device(): lax.all_to_all(field, AXES, 0, 0, axis_index_groups=crosses, tiled=True)]
    all_to_all x1 -> x0, waiting for transfers between devices: 7.09 us -> none  [on_device(): whole = lax.all_to_all(sent, FLAT, 0, 0, tiled=True)]
    all_to_all x1 -> x0, starting transfers between devices: 5.36 us -> none  [on_device(): whole = lax.all_to_all(sent, FLAT, 0, 0, tiled=True)]
    unnamed x13 -> x12, local copies, waits for them, and re-layouts: 4.4 us -> 3.26 us
    all_to_all x1, waiting for transfers between devices: 6.73 us -> 5.74 us  [on_device(): lax.all_to_all(sent, AXES, 0, 0, axis_index_groups=columns, tiled=True)]
  transfers between devices with their start and end apart: 4 -> 3, of which waited for: 3 -> 2; matrix products, arithmetic and copies ran while one was open for 1% -> 0% of each run, Pallas kernels for 4% -> 5%
where the time goes in v6:
time: 88.3 us; the launch traced here: 87.9 us
  blocking collectives  40.6 us (46%)
  starting transfers between devices  29.5 us (33%)
  Pallas kernels  7.09 us (8%)
  waiting for transfers between devices  6.75 us (8%)
  local copies, waits for them, and re-layouts  3.26 us (4%)
    ppermute x1, starting transfers between devices, on_device(): other = lax.ppermute(raw, 'zh', [(0, 1), (1, 0)])  16.3 us
    all_to_all x1, blocking collectives, on_device(): lax.all_to_all(field, AXES, 0, 0, axis_index_groups=crosses, tiled=True)  14.9 us
    all_to_all x1, blocking collectives, on_device(): lax.all_to_all(sent, AXES, 0, 0, axis_index_groups=flats, tiled=True)  13.2 us
    all_to_all x1, blocking collectives, on_device(): lax.all_to_all(sums, AXES, 0, 0, axis_index_groups=flats, tiled=True)  12.5 us
    all_to_all x1, starting transfers between devices, on_device(): lax.all_to_all(sent, AXES, 0, 0, axis_index_groups=columns, tiled=True)  9.72 us
    pallas_call x8, Pallas kernels, call(): pl.pallas_call(kernel, out_shape=outs, in_specs=[pl.BlockSpec(memory_spac...  7.09 us
    all_to_all x1, waiting for transfers between devices, on_device(): lax.all_to_all(sent, AXES, 0, 0, axis_index_groups=columns, tiled=True)  5.74 us
    ppermute x1, starting transfers between devices, on_device(): halo = lax.ppermute(last, AXES, hops)  3.49 us
  transfers between devices with their start and end apart: 3, of which 2 were waited for; matrix products, arithmetic and copies ran while one was open for 0% of the time, Pallas kernels for 5%

profile of v6, /device:TPU:1, one launch (start us, length us, event | category | flops | bytes accessed | tf_op | source)
XLA Modules:
  0.0 87.9 jit_solution(5196842824257997124)
XLA Ops:
  0.6 16.3 %collective-permute-start = (bf16[64,4,128]{2,1,0:T(4,128)(2,1)}, bf16[64,4,128]{2,1,0:T(4,128)(2,1)S(1)}, u32[]{:S(2)}, u32[]{:S(2)}) collective-permute-start(bf16[64,4,128]{2,1,0:T(4,128)(2,1)} %bitcast.11), channel_id=1, source_target_pairs={{0,1},{1,0},{2,3},{3,2},{4,5},{5,4},{6,7},{7,6},{8,9},{9,8},{10,11... | collective-permute-start | bytes 196616 | tf_op jit(solution)/shard_map/ppermute | solution.py:240
  16.9 0.0 copy-start
  16.9 0.9 %copy-done = bf16[9,64,64]{2,1,0:T(8,128)(2,1)S(1)} copy-done((bf16[9,64,64]{2,1,0:T(8,128)(2,1)S(1)}, bf16[9,64,64]{2,1,0:T(8,128)(2,1)}, u32[]{:S(2)}) %copy-start) | copy-done | bytes 73752
  17.8 0.0 copy-start.3
  17.8 1.0 %copy-done.3 = bf16[64,1,32,128]{3,2,1,0:T(8,128)(2,1)S(1)} copy-done((bf16[64,1,32,128]{3,2,1,0:T(8,128)(2,1)S(1)}, bf16[64,1,32,128]{3,2,1,0:T(8,128)(2,1)}, u32[]{:S(2)}) %copy-start.3) | copy-done | bytes 524312
  18.9 0.0 copy-start.4
  18.9 0.7 copy-done.4
  19.5 0.0 copy-start.5
  19.5 0.7 copy-done.5
  20.2 0.0 copy-start.2
  20.2 2.8 %shard_map.76 = (f32[32,64,128]{2,1,0:T(8,128)S(1)}, bf16[4096,256]{1,0:T(8,128)(2,1)S(1)}, f32[8,128]{1,0:T(8,128)S(1)}) custom-call(s32[1]{0:T(128)} %bitcast.half_ref, f32[9]{0:T(128)S(1)} %copy-done.4, f32[1,64]{1,0:T(1,128)S(1)} %bitcast.14, bf16[64,32,128]{2,1,0:T(8,128)(2,1)S(1)} %bitcast.13, bf16[9,64,64]{2,1,0:T(8,128)(2,1)S(1)} %copy-done), custom_call_target="tpu_custom_call" | custom-call | flops 19327352832 | bytes 134217728 | tf_op jit(solution)/shard_map/pallas_call | solution.py:223
  23.0 0.0 collective-permute-done.other_ref
  23.0 0.0 copy-done.2
  23.0 0.1 shard_map.77
  23.1 3.5 %collective-permute-start.1 = (bf16[2,64,128]{2,1,0:T(8,128)(2,1)S(1)}, bf16[2,64,128]{2,1,0:T(8,128)(2,1)S(1)}, u32[]{:S(2)}, u32[]{:S(2)}) collective-permute-start(bf16[2,64,128]{2,1,0:T(8,128)(2,1)S(1)} %get-tuple-element.24), channel_id=1, source_target_pairs={{0,32},{2,34},{4,36},{6,38},{8,40},{10,42},{12,44},{14,46},{16,48}... | collective-permute-start | bytes 98312 | tf_op jit(solution)/shard_map/ppermute | solution.py:278
  26.6 1.0 %collective-permute-done.1.halo_ref = bf16[2,64,128]{2,1,0:T(8,128)(2,1)S(1)} collective-permute-done((bf16[2,64,128]{2,1,0:T(8,128)(2,1)S(1)}, bf16[2,64,128]{2,1,0:T(8,128)(2,1)S(1)}, u32[]{:S(2)}, u32[]{:S(2)}) %collective-permute-start.1) | collective-permute-done | bytes 32800 | tf_op jit(solution)/shard_map/ppermute | solution.py:278
  27.6 0.1 shard_map.78
  27.7 14.9 %all_to_all.20 = bf16[16,2,64,128]{3,2,1,0:T(8,128)(2,1)S(1)} all-to-all(bf16[16,2,64,128]{3,2,1,0:T(8,128)(2,1)S(1)} %shard_map.78), channel_id=1, replica_groups={{30,24,26,28,6,0,2,4,14,8,10,12,22,16,18,20},{31,25,27,29,7,1,3,5,15,9,..., dimensions={0} | all-to-all | bytes 1048576 | tf_op jit(solution)/shard_map/all_to_all | solution.py:296
  42.6 0.0 copy-start.1
  42.6 0.7 shard_map.79
  43.3 12.5 %all_to_all.21.parts_ref = f32[32,4,384]{2,1,0:T(4,128)S(1)} all-to-all(f32[32,4,384]{2,1,0:T(4,128)S(1)} %get-tuple-element.27), channel_id=1, replica_groups={{30,24,26,28,6,0,2,4,14,8,10,12,22,16,18,20,62,56,58,60,38,32,34,36,46,..., dimensions={0} | all-to-all | bytes 393216 | tf_op jit(solution)/shard_map/all_to_all | solution.py:324
  55.8 0.7 shard_map.80
  56.5 9.7 %all-to-all-start.2 = ((f32[16,4,384]{2,1,0:T(4,128)}), f32[16,4,384]{2,1,0:T(4,128)S(1)}, u32[]{:S(2)}, u32[]{:S(2)}) async-start(f32[16,4,384]{2,1,0:T(4,128)} %shard_map.80), calls=%async_computation.2 | async-start | bytes 196608 | tf_op jit(solution)/shard_map/all_to_all | solution.py:336
  66.2 0.0 copy-done.1
  66.2 1.8 %shard_map.81 = bf16[64,32,128]{2,1,0:T(8,128)(2,1)} custom-call(bf16[32,64,128]{2,1,0:T(8,128)(2,1)S(1)} %get-tuple-element.28.grad_ref, bf16[32,64,128]{2,1,0:T(8,128)(2,1)S(1)} %bitcast.10, bf16[9,64,64]{2,1,0:T(8,128)(2,1)S(1)} %copy-done.1), custom_call_target="tpu_custom_call" | custom-call | flops 301989888 | bytes 2097152 | tf_op jit(solution)/shard_map/pallas_call | solution.py:223
  68.1 5.7 %all-to-all-done.2.a = f32[16,4,384]{2,1,0:T(4,128)S(1)} async-done(((f32[16,4,384]{2,1,0:T(4,128)}), f32[16,4,384]{2,1,0:T(4,128)S(1)}, u32[]{:S(2)}, u32[]{:S(2)}) %all-to-all-start.2) | async-done | bytes 98336 | tf_op jit(solution)/shard_map/all_to_all | solution.py:336
  73.9 13.2 %all_to_all.22.whole_ref = f32[32,4,384]{2,1,0:T(4,128)S(1)} all-to-all(f32[32,4,384]{2,1,0:T(4,128)S(1)} %shard_map.82), channel_id=1, replica_groups={{30,24,26,28,6,0,2,4,14,8,10,12,22,16,18,20,62,56,58,60,38,32,34,36,46,..., dimensions={0} | all-to-all | bytes 393216 | tf_op jit(solution)/shard_map/all_to_all | solution.py:347
  87.1 0.8 shard_map.83
  (1 shorter events, 0.0 us)
Async XLA Ops:
  0.6 22.4 %collective-permute-start = (bf16[64,4,128]{2,1,0:T(4,128)(2,1)}, bf16[64,4,128]{2,1,0:T(4,128)(2,1)S(1)}, u32[]{:S(2)}, u32[]{:S(2)}) collective-permute-start(bf16[64,4,128]{2,1,0:T(4,128)(2,1)} %bitcast.11), channel_id=1, source_target_pairs={{0,1},{1,0},{2,3},{3,2},{4,5},{5,4},{6,7},{7,6},{8,9},{9,8},{10,11... | collective-permute-start | bytes 196616 | tf_op jit(solution)/shard_map/ppermute | solution.py:240
  16.9 0.9 %copy-start = (bf16[9,64,64]{2,1,0:T(8,128)(2,1)S(1)}, bf16[9,64,64]{2,1,0:T(8,128)(2,1)}, u32[]{:S(2)}) copy-start(bf16[9,64,64]{2,1,0:T(8,128)(2,1)} %weight_ref.1) | copy-start | bytes 221188
  17.8 1.0 %copy-start.3 = (bf16[64,1,32,128]{3,2,1,0:T(8,128)(2,1)S(1)}, bf16[64,1,32,128]{3,2,1,0:T(8,128)(2,1)}, u32[]{:S(2)}) copy-start(bf16[64,1,32,128]{3,2,1,0:T(8,128)(2,1)} %param.5) | copy-start | bytes 1572868
  18.9 0.7 copy-start.4
  19.5 0.7 copy-start.5
  20.2 2.8 %copy-start.2 = (bf16[64,4,1,128]{3,1,2,0:T(4,128)(2,1)S(1)}, bf16[64,4,1,128]{3,1,2,0:T(4,128)(2,1)}, u32[]{:S(2)}) copy-start(bf16[64,4,1,128]{3,1,2,0:T(4,128)(2,1)} %param.6) | copy-start | bytes 196612
  23.1 4.5 %collective-permute-start.1 = (bf16[2,64,128]{2,1,0:T(8,128)(2,1)S(1)}, bf16[2,64,128]{2,1,0:T(8,128)(2,1)S(1)}, u32[]{:S(2)}, u32[]{:S(2)}) collective-permute-start(bf16[2,64,128]{2,1,0:T(8,128)(2,1)S(1)} %get-tuple-element.24), channel_id=1, source_target_pairs={{0,32},{2,34},{4,36},{6,38},{8,40},{10,42},{12,44},{14,46},{16,48}... | collective-permute-start | bytes 98312 | tf_op jit(solution)/shard_map/ppermute | solution.py:278
  42.6 23.6 %copy-start.1 = (bf16[9,64,64]{2,1,0:T(8,128)(2,1)S(1)}, bf16[9,64,64]{2,1,0:T(8,128)(2,1)}, u32[]{:S(2)}) copy-start(bf16[9,64,64]{2,1,0:T(8,128)(2,1)} %weight_ref.1) | copy-start | bytes 221188
  56.5 17.3 %all-to-all-start.2 = ((f32[16,4,384]{2,1,0:T(4,128)}), f32[16,4,384]{2,1,0:T(4,128)S(1)}, u32[]{:S(2)}, u32[]{:S(2)}) async-start(f32[16,4,384]{2,1,0:T(4,128)} %shard_map.80), calls=%async_computation.2 | async-start | bytes 196608 | tf_op jit(solution)/shard_map/all_to_all | solution.py:336

commit v7 on v6

--- a/solution.py
+++ b/solution.py
@@ -19,8 +19,8 @@
 N_GROUP = 16
 N_COLUMN = 16
 FIRST = 6
-PIECE = 4
-LONG = 384
+PIECE = 2
+LONG = 640
 WIDE = 256
 VMEM_LIMIT = 16 * 1024 * 1024
 CORNER = 3
@@ -121,16 +121,13 @@
     bias = total[C : 2 * C, 3 * C : 3 * C + 1]
     row = jnp.sum(jnp.where(diagonal, bias, 0.0), axis=0, keepdims=True)
     first = lax.broadcasted_iota(jnp.int32, square, 0) == 0
-    zero = jnp.zeros(square, jnp.float32)
-    sides = [total[a * C : (a + 1) * C, 2 * C : 3 * C] for a in range(3)]
-    low = jnp.concatenate([sides[0], sides[1]], axis=1)
-    high = jnp.concatenate([sides[2], zero], axis=1)
-    last = jnp.concatenate([jnp.where(first, row, 0.0), zero], axis=1)
-    top = jnp.concatenate([total[:C, : 2 * C], total[2 * C :, : 2 * C], high], axis=1)
-    bottom = jnp.concatenate([total[C : 2 * C, : 2 * C], low, last], axis=1)
-    for half, block in enumerate((top, bottom)):
-        for piece in range(C // PIECE):
-            sums_ref[half * C // PIECE + piece] = block[piece * PIECE : (piece + 1) * PIECE]
+    last = jnp.where(first, row, 0.0)
+    blocks = [
+        total[a * C : (a + 1) * C, b * C : (b + 1) * C] for a in range(3) for b in range(3)
+    ]
+    whole = jnp.concatenate(blocks + [last], axis=1)
+    for piece in range(N_FLAT):
+        sums_ref[piece] = whole[piece * PIECE : (piece + 1) * PIECE]
 
 
 def input_kernel(grad_ref, g_ref, weight_ref, out_ref, stack, total):
@@ -185,26 +182,10 @@
 
 
 def unpack_kernel(whole_ref, weight_ref, bias_ref):
-    top, bottom = (
-        jnp.concatenate(
-            [whole_ref[half * C // PIECE + piece] for piece in range(C // PIECE)], axis=0
-        )
-        for half in range(2)
-    )
-    rows = (
-        (top, 0),
-        (top, 1),
-        (bottom, 2),
-        (bottom, 0),
-        (bottom, 1),
-        (bottom, 3),
-        (top, 2),
-        (top, 3),
-        (top, 4),
-    )
-    for tap, (block, place) in enumerate(rows):
-        weight_ref[tap] = block[:, place * C : (place + 1) * C]
-    bias_ref[...] = bottom[0:1, 4 * C : 5 * C]
+    whole = jnp.concatenate([whole_ref[piece] for piece in range(N_FLAT)], axis=0)
+    for tap in range(9):
+        weight_ref[tap] = whole[:, tap * C : (tap + 1) * C]
+    bias_ref[...] = whole[0:1, 9 * C :]
 
 
 def spread_sum_kernel(parts_ref, out_ref):

time: 88.3 us -> 87.1 us (0.986)
  no operation moved by 1% of the time
where the time goes in v7:
time: 87.1 us; the launch traced here: 86.7 us
  blocking collectives  39.8 us (46%)
  starting transfers between devices  29.5 us (34%)
  Pallas kernels  7.21 us (8%)
  waiting for transfers between devices  6.24 us (7%)
  local copies, waits for them, and re-layouts  3.26 us (4%)
    ppermute x1, starting transfers between devices, on_device(): other = lax.ppermute(raw, 'zh', [(0, 1), (1, 0)])  16.3 us
    all_to_all x1, blocking collectives, on_device(): lax.all_to_all(field, AXES, 0, 0, axis_index_groups=crosses, tiled=True)  14.9 us
    all_to_all x1, blocking collectives, on_device(): lax.all_to_all(sent, AXES, 0, 0, axis_index_groups=flats, tiled=True)  12.7 us
    all_to_all x1, blocking collectives, on_device(): lax.all_to_all(sums, AXES, 0, 0, axis_index_groups=flats, tiled=True)  12.2 us
    all_to_all x1, starting transfers between devices, on_device(): lax.all_to_all(sent, AXES, 0, 0, axis_index_groups=columns, tiled=True)  9.72 us
    pallas_call x8, Pallas kernels, call(): pl.pallas_call(kernel, out_shape=outs, in_specs=[pl.BlockSpec(memory_spac...  7.21 us
    all_to_all x1, waiting for transfers between devices, on_device(): lax.all_to_all(sent, AXES, 0, 0, axis_index_groups=columns, tiled=True)  5.23 us
    ppermute x1, starting transfers between devices, on_device(): halo = lax.ppermute(last, AXES, hops)  3.49 us
  transfers between devices with their start and end apart: 3, of which 2 were waited for; matrix products, arithmetic and copies ran while one was open for 0% of the time, Pallas kernels for 5%

profile of v7, /device:TPU:1, one launch (start us, length us, event | category | flops | bytes accessed | tf_op | source)
XLA Modules:
  0.0 86.7 jit_solution(18417425032710021171)
XLA Ops:
  0.6 16.3 %collective-permute-start = (bf16[64,4,128]{2,1,0:T(4,128)(2,1)}, bf16[64,4,128]{2,1,0:T(4,128)(2,1)S(1)}, u32[]{:S(2)}, u32[]{:S(2)}) collective-permute-start(bf16[64,4,128]{2,1,0:T(4,128)(2,1)} %bitcast.11), channel_id=1, source_target_pairs={{0,1},{1,0},{2,3},{3,2},{4,5},{5,4},{6,7},{7,6},{8,9},{9,8},{10,11... | collective-permute-start | bytes 196616 | tf_op jit(solution)/shard_map/ppermute | solution.py:221
  16.9 0.0 copy-start
  16.9 0.9 %copy-done = bf16[9,64,64]{2,1,0:T(8,128)(2,1)S(1)} copy-done((bf16[9,64,64]{2,1,0:T(8,128)(2,1)S(1)}, bf16[9,64,64]{2,1,0:T(8,128)(2,1)}, u32[]{:S(2)}) %copy-start) | copy-done | bytes 73752
  17.8 0.0 copy-start.3
  17.8 1.0 %copy-done.3 = bf16[64,1,32,128]{3,2,1,0:T(8,128)(2,1)S(1)} copy-done((bf16[64,1,32,128]{3,2,1,0:T(8,128)(2,1)S(1)}, bf16[64,1,32,128]{3,2,1,0:T(8,128)(2,1)}, u32[]{:S(2)}) %copy-start.3) | copy-done | bytes 524312
  18.9 0.0 copy-start.4
  18.9 0.7 copy-done.4
  19.5 0.0 copy-start.5
  19.5 0.7 copy-done.5
  20.2 0.0 copy-start.2
  20.2 2.8 %shard_map.76 = (f32[32,64,128]{2,1,0:T(8,128)S(1)}, bf16[4096,256]{1,0:T(8,128)(2,1)S(1)}, f32[8,128]{1,0:T(8,128)S(1)}) custom-call(s32[1]{0:T(128)} %bitcast.half_ref, f32[9]{0:T(128)S(1)} %copy-done.4, f32[1,64]{1,0:T(1,128)S(1)} %bitcast.14, bf16[64,32,128]{2,1,0:T(8,128)(2,1)S(1)} %bitcast.13, bf16[9,64,64]{2,1,0:T(8,128)(2,1)S(1)} %copy-done), custom_call_target="tpu_custom_call" | custom-call | flops 19327352832 | bytes 134217728 | tf_op jit(solution)/shard_map/pallas_call | solution.py:204
  23.0 0.0 collective-permute-done.other_ref
  23.0 0.0 copy-done.2
  23.0 0.1 shard_map.77
  23.1 3.5 %collective-permute-start.1 = (bf16[2,64,128]{2,1,0:T(8,128)(2,1)S(1)}, bf16[2,64,128]{2,1,0:T(8,128)(2,1)S(1)}, u32[]{:S(2)}, u32[]{:S(2)}) collective-permute-start(bf16[2,64,128]{2,1,0:T(8,128)(2,1)S(1)} %get-tuple-element.24), channel_id=1, source_target_pairs={{0,32},{2,34},{4,36},{6,38},{8,40},{10,42},{12,44},{14,46},{16,48}... | collective-permute-start | bytes 98312 | tf_op jit(solution)/shard_map/ppermute | solution.py:259
  26.6 1.0 %collective-permute-done.1.halo_ref = bf16[2,64,128]{2,1,0:T(8,128)(2,1)S(1)} collective-permute-done((bf16[2,64,128]{2,1,0:T(8,128)(2,1)S(1)}, bf16[2,64,128]{2,1,0:T(8,128)(2,1)S(1)}, u32[]{:S(2)}, u32[]{:S(2)}) %collective-permute-start.1) | collective-permute-done | bytes 32800 | tf_op jit(solution)/shard_map/ppermute | solution.py:259
  27.6 0.1 shard_map.78
  27.7 14.9 %all_to_all.20 = bf16[16,2,64,128]{3,2,1,0:T(8,128)(2,1)S(1)} all-to-all(bf16[16,2,64,128]{3,2,1,0:T(8,128)(2,1)S(1)} %shard_map.78), channel_id=1, replica_groups={{30,24,26,28,6,0,2,4,14,8,10,12,22,16,18,20},{31,25,27,29,7,1,3,5,15,9,..., dimensions={0} | all-to-all | bytes 1048576 | tf_op jit(solution)/shard_map/all_to_all | solution.py:277
  42.6 0.0 copy-start.1
  42.6 0.8 shard_map.79
  43.4 12.2 %all_to_all.21.parts_ref = f32[32,2,640]{2,1,0:T(2,128)S(1)} all-to-all(f32[32,2,640]{2,1,0:T(2,128)S(1)} %get-tuple-element.27), channel_id=1, replica_groups={{30,24,26,28,6,0,2,4,14,8,10,12,22,16,18,20,62,56,58,60,38,32,34,36,46,..., dimensions={0} | all-to-all | bytes 327680 | tf_op jit(solution)/shard_map/all_to_all | solution.py:305
  55.6 0.7 shard_map.80
  56.3 9.7 %all-to-all-start.2 = ((f32[16,2,640]{2,1,0:T(2,128)}), f32[16,2,640]{2,1,0:T(2,128)S(1)}, u32[]{:S(2)}, u32[]{:S(2)}) async-start(f32[16,2,640]{2,1,0:T(2,128)} %shard_map.80), calls=%async_computation.2 | async-start | bytes 163840 | tf_op jit(solution)/shard_map/all_to_all | solution.py:317
  66.0 0.0 copy-done.1
  66.0 1.8 %shard_map.81 = bf16[64,32,128]{2,1,0:T(8,128)(2,1)} custom-call(bf16[32,64,128]{2,1,0:T(8,128)(2,1)S(1)} %get-tuple-element.28.grad_ref, bf16[32,64,128]{2,1,0:T(8,128)(2,1)S(1)} %bitcast.10, bf16[9,64,64]{2,1,0:T(8,128)(2,1)S(1)} %copy-done.1), custom_call_target="tpu_custom_call" | custom-call | flops 301989888 | bytes 2097152 | tf_op jit(solution)/shard_map/pallas_call | solution.py:204
  67.9 5.2 %all-to-all-done.2.a = f32[16,2,640]{2,1,0:T(2,128)S(1)} async-done(((f32[16,2,640]{2,1,0:T(2,128)}), f32[16,2,640]{2,1,0:T(2,128)S(1)}, u32[]{:S(2)}, u32[]{:S(2)}) %all-to-all-start.2) | async-done | bytes 81952 | tf_op jit(solution)/shard_map/all_to_all | solution.py:317
  73.1 0.1 shard_map.82
  73.2 12.7 %all_to_all.22.whole_ref = f32[32,2,640]{2,1,0:T(2,128)S(1)} all-to-all(f32[32,2,640]{2,1,0:T(2,128)S(1)} %shard_map.82), channel_id=1, replica_groups={{30,24,26,28,6,0,2,4,14,8,10,12,22,16,18,20,62,56,58,60,38,32,34,36,46,..., dimensions={0} | all-to-all | bytes 327680 | tf_op jit(solution)/shard_map/all_to_all | solution.py:328
  85.9 0.8 shard_map.83
Async XLA Ops:
  0.6 22.4 %collective-permute-start = (bf16[64,4,128]{2,1,0:T(4,128)(2,1)}, bf16[64,4,128]{2,1,0:T(4,128)(2,1)S(1)}, u32[]{:S(2)}, u32[]{:S(2)}) collective-permute-start(bf16[64,4,128]{2,1,0:T(4,128)(2,1)} %bitcast.11), channel_id=1, source_target_pairs={{0,1},{1,0},{2,3},{3,2},{4,5},{5,4},{6,7},{7,6},{8,9},{9,8},{10,11... | collective-permute-start | bytes 196616 | tf_op jit(solution)/shard_map/ppermute | solution.py:221
  16.9 0.9 %copy-start = (bf16[9,64,64]{2,1,0:T(8,128)(2,1)S(1)}, bf16[9,64,64]{2,1,0:T(8,128)(2,1)}, u32[]{:S(2)}) copy-start(bf16[9,64,64]{2,1,0:T(8,128)(2,1)} %weight_ref.1) | copy-start | bytes 221188
  17.8 1.0 %copy-start.3 = (bf16[64,1,32,128]{3,2,1,0:T(8,128)(2,1)S(1)}, bf16[64,1,32,128]{3,2,1,0:T(8,128)(2,1)}, u32[]{:S(2)}) copy-start(bf16[64,1,32,128]{3,2,1,0:T(8,128)(2,1)} %param.5) | copy-start | bytes 1572868
  18.9 0.7 copy-start.4
  19.5 0.7 copy-start.5
  20.2 2.8 %copy-start.2 = (bf16[64,4,1,128]{3,1,2,0:T(4,128)(2,1)S(1)}, bf16[64,4,1,128]{3,1,2,0:T(4,128)(2,1)}, u32[]{:S(2)}) copy-start(bf16[64,4,1,128]{3,1,2,0:T(4,128)(2,1)} %param.6) | copy-start | bytes 196612
  23.1 4.5 %collective-permute-start.1 = (bf16[2,64,128]{2,1,0:T(8,128)(2,1)S(1)}, bf16[2,64,128]{2,1,0:T(8,128)(2,1)S(1)}, u32[]{:S(2)}, u32[]{:S(2)}) collective-permute-start(bf16[2,64,128]{2,1,0:T(8,128)(2,1)S(1)} %get-tuple-element.24), channel_id=1, source_target_pairs={{0,32},{2,34},{4,36},{6,38},{8,40},{10,42},{12,44},{14,46},{16,48}... | collective-permute-start | bytes 98312 | tf_op jit(solution)/shard_map/ppermute | solution.py:259
  42.6 23.4 %copy-start.1 = (bf16[9,64,64]{2,1,0:T(8,128)(2,1)S(1)}, bf16[9,64,64]{2,1,0:T(8,128)(2,1)}, u32[]{:S(2)}) copy-start(bf16[9,64,64]{2,1,0:T(8,128)(2,1)} %weight_ref.1) | copy-start | bytes 221188
  56.3 16.8 %all-to-all-start.2 = ((f32[16,2,640]{2,1,0:T(2,128)}), f32[16,2,640]{2,1,0:T(2,128)S(1)}, u32[]{:S(2)}, u32[]{:S(2)}) async-start(f32[16,2,640]{2,1,0:T(2,128)} %shard_map.80), calls=%async_computation.2 | async-start | bytes 163840 | tf_op jit(solution)/shard_map/all_to_all | solution.py:317

commit v8 on v7

--- a/solution.py
+++ b/solution.py
@@ -18,7 +18,7 @@
 N_FLAT = 32
 N_GROUP = 16
 N_COLUMN = 16
-FIRST = 6
+FIRST = 7
 PIECE = 2
 LONG = 640
 WIDE = 256
@@ -40,8 +40,8 @@
 
 def forward_kernel(
     half_ref,
-    taps_ref,
-    bias_ref,
+    taps_far,
+    bias_far,
     act_far,
     weight_far,
     slope_ref,
@@ -49,25 +49,30 @@
     coef_ref,
     stack,
     hidden,
+    taps_ref,
+    bias_ref,
     act_ref,
     weight_ref,
     sems,
 ):
+    fars = (taps_far, bias_far, act_far, weight_far)
+    nears = (taps_ref, bias_ref, act_ref, weight_ref)
     copies = [
-        pltpu.make_async_copy(act_far, act_ref, sems.at[0]),
-        pltpu.make_async_copy(weight_far, weight_ref, sems.at[1]),
+        pltpu.make_async_copy(far, near, sems.at[i])
+        for i, (far, near) in enumerate(zip(fars, nears))
     ]
     for copy in copies:
         copy.start()
-    half = half_ref[0]
+    for copy in copies:
+        copy.wait()
+    low = half_ref[0] == 0
     for pair in range(4):
-        coef_ref[pair : pair + 1] = jnp.full((1, X), taps_ref[2 * pair + half], jnp.float32)
-    spill = jnp.where(half == 0, taps_ref[R], 0.0)
-    coef_ref[4:] = jnp.full((4, X), spill, jnp.float32)
+        even, odd = (taps_ref[:, 2 * pair + i : 2 * pair + i + 1] for i in range(2))
+        coef_ref[pair : pair + 1] = jnp.broadcast_to(jnp.where(low, even, odd), (1, X))
+    spill = jnp.where(low, taps_ref[:, R : R + 1], 0.0)
+    coef_ref[4:] = jnp.broadcast_to(spill, (4, X))
     column = lax.broadcasted_iota(jnp.int32, (X, WIDE - 3 * C), 1)
     ones = jnp.where(column == 0, 1.0, 0.0).astype(jnp.bfloat16)
-    for copy in copies:
-        copy.wait()
     for y in range(Y):
         if y % 16 == 0:
             rows = jnp.swapaxes(act_ref[:, y : y + 16].astype(jnp.float32), 0, 1)
@@ -227,19 +232,21 @@
         [
             pltpu.VMEM((3 * C, Y * X), bf16),
             pltpu.VMEM((C, (Y + 2) * X), f32),
+            pltpu.VMEM((1, 9), f32),
+            pltpu.VMEM((1, C), f32),
             pltpu.VMEM((C, Y, X), bf16),
             pltpu.VMEM((9, C, C), bf16),
-            pltpu.SemaphoreType.DMA((2,)),
+            pltpu.SemaphoreType.DMA((4,)),
         ],
         64 * flops,
         128 << 20,
         half,
-        blur_taps,
-        conv_bias[None, :],
-        activations[:, 0],
-        weight,
-        scalars=2,
-        far=2,
+        *[
+            pltpu.with_memory_space_constraint(array, pltpu.HBM)
+            for array in (blur_taps[None], conv_bias[None], activations[:, 0], weight)
+        ],
+        scalars=1,
+        far=4,
     )
     slope, turned, coef, raw = lax.optimization_barrier((slope, turned, coef, raw))
     rows, last = call(

time: 87.1 us -> 86.1 us (0.989)
  local copies, waits for them, and re-layouts: 3.26 us -> 0.01 us
  starting transfers between devices: 29.5 us -> 31.5 us
  waiting for transfers between devices: 6.24 us -> 4.52 us
  blocking collectives: 39.8 us -> 41.4 us
    unnamed x12 -> x4, local copies, waits for them, and re-layouts: 3.26 us -> 0.01 us
    all_to_all x1, waiting for transfers between devices: 5.23 us -> 3.52 us  [on_device(): lax.all_to_all(sent, AXES, 0, 0, axis_index_groups=columns, tiled=True)]
    all_to_all x1, starting transfers between devices: 9.72 us -> 11.1 us  [on_device(): lax.all_to_all(sent, AXES, 0, 0, axis_index_groups=columns, tiled=True)]
  transfers between devices with their start and end apart: 3 -> 3, of which waited for: 2 -> 2; matrix products, arithmetic and copies ran while one was open for 0% -> 0% of each run, Pallas kernels for 5% -> 6%
where the time goes in v8:
time: 86.1 us; the launch traced here: 85.8 us
  blocking collectives  41.4 us (48%)
  starting transfers between devices  31.5 us (37%)
  Pallas kernels  7.65 us (9%)
  waiting for transfers between devices  4.52 us (5%)
    ppermute x1, starting transfers between devices, on_device(): other = lax.ppermute(raw, 'zh', [(0, 1), (1, 0)])  16.3 us
    all_to_all x1, blocking collectives, on_device(): lax.all_to_all(field, AXES, 0, 0, axis_index_groups=crosses, tiled=True)  15.7 us
    all_to_all x1, blocking collectives, on_device(): lax.all_to_all(sent, AXES, 0, 0, axis_index_groups=flats, tiled=True)  13.5 us
    all_to_all x1, blocking collectives, on_device(): lax.all_to_all(sums, AXES, 0, 0, axis_index_groups=flats, tiled=True)  12.2 us
    all_to_all x1, starting transfers between devices, on_device(): lax.all_to_all(sent, AXES, 0, 0, axis_index_groups=columns, tiled=True)  11.1 us
    pallas_call x8, Pallas kernels, call(): pl.pallas_call(kernel, out_shape=outs, in_specs=[pl.BlockSpec(memory_spac...  7.65 us
    ppermute x1, starting transfers between devices, on_device(): halo = lax.ppermute(last, AXES, hops)  4.13 us
    all_to_all x1, waiting for transfers between devices, on_device(): lax.all_to_all(sent, AXES, 0, 0, axis_index_groups=columns, tiled=True)  3.52 us
  transfers between devices with their start and end apart: 3, of which 2 were waited for; matrix products, arithmetic and copies ran while one was open for 0% of the time, Pallas kernels for 6%

profile of v8, /device:TPU:1, one launch (start us, length us, event | category | flops | bytes accessed | tf_op | source)
XLA Modules:
  0.0 85.8 jit_solution(15280829675810217674)
XLA Ops:
  0.6 16.3 %collective-permute-start = (bf16[64,4,128]{2,1,0:T(4,128)(2,1)}, bf16[64,4,128]{2,1,0:T(4,128)(2,1)S(1)}, u32[]{:S(2)}, u32[]{:S(2)}) collective-permute-start(bf16[64,4,128]{2,1,0:T(4,128)(2,1)} %bitcast.12), channel_id=1, source_target_pairs={{0,1},{1,0},{2,3},{3,2},{4,5},{5,4},{6,7},{7,6},{8,9},{9,8},{10,11... | collective-permute-start | bytes 196616 | tf_op jit(solution)/shard_map/ppermute | solution.py:226
  16.9 0.0 copy-start.1
  16.9 3.3 %shard_map.76 = (f32[32,64,128]{2,1,0:T(8,128)S(1)}, bf16[4096,256]{1,0:T(8,128)(2,1)S(1)}, f32[8,128]{1,0:T(8,128)S(1)}) custom-call(s32[1]{0:T(128)} %bitcast.half_ref, f32[1,9]{1,0:T(1,128)} %bitcast.16, f32[1,64]{1,0:T(1,128)} %bitcast.17, bf16[64,32,128]{2,1,0:T(8,128)(2,1)} %bitcast.15, bf16[9,64,64]{2,1,0:T(8,128)(2,1)} %weight_ref.1), custom_call_target="tpu_custom_call" | custom-call | flops 19327352832 | bytes 134217728 | tf_op jit(solution)/shard_map/pallas_call | solution.py:209
  20.2 0.0 collective-permute-done.other_ref
  20.2 0.0 copy-done.1
  20.2 0.1 shard_map.77
  20.3 4.1 %collective-permute-start.1 = (bf16[2,64,128]{2,1,0:T(8,128)(2,1)S(1)}, bf16[2,64,128]{2,1,0:T(8,128)(2,1)S(1)}, u32[]{:S(2)}, u32[]{:S(2)}) collective-permute-start(bf16[2,64,128]{2,1,0:T(8,128)(2,1)S(1)} %get-tuple-element.24), channel_id=1, source_target_pairs={{0,32},{2,34},{4,36},{6,38},{8,40},{10,42},{12,44},{14,46},{16,48}... | collective-permute-start | bytes 98312 | tf_op jit(solution)/shard_map/ppermute | solution.py:266
  24.4 1.0 %collective-permute-done.1.halo_ref = bf16[2,64,128]{2,1,0:T(8,128)(2,1)S(1)} collective-permute-done((bf16[2,64,128]{2,1,0:T(8,128)(2,1)S(1)}, bf16[2,64,128]{2,1,0:T(8,128)(2,1)S(1)}, u32[]{:S(2)}, u32[]{:S(2)}) %collective-permute-start.1) | collective-permute-done | bytes 32800 | tf_op jit(solution)/shard_map/ppermute | solution.py:266
  25.4 0.1 shard_map.78
  25.5 15.7 %all_to_all.20 = bf16[16,2,64,128]{3,2,1,0:T(8,128)(2,1)S(1)} all-to-all(bf16[16,2,64,128]{3,2,1,0:T(8,128)(2,1)S(1)} %shard_map.78), channel_id=1, replica_groups={{30,24,26,28,6,0,2,4,14,8,10,12,22,16,18,20},{31,25,27,29,7,1,3,5,15,9,..., dimensions={0} | all-to-all | bytes 1048576 | tf_op jit(solution)/shard_map/all_to_all | solution.py:284
  41.2 0.0 copy-start
  41.2 0.8 shard_map.79
  42.0 12.2 %all_to_all.21.parts_ref = f32[32,2,640]{2,1,0:T(2,128)S(1)} all-to-all(f32[32,2,640]{2,1,0:T(2,128)S(1)} %get-tuple-element.27), channel_id=1, replica_groups={{30,24,26,28,6,0,2,4,14,8,10,12,22,16,18,20,62,56,58,60,38,32,34,36,46,..., dimensions={0} | all-to-all | bytes 327680 | tf_op jit(solution)/shard_map/all_to_all | solution.py:312
  54.2 0.7 shard_map.80
  54.9 11.1 %all-to-all-start.2 = ((f32[16,2,640]{2,1,0:T(2,128)}), f32[16,2,640]{2,1,0:T(2,128)S(1)}, u32[]{:S(2)}, u32[]{:S(2)}) async-start(f32[16,2,640]{2,1,0:T(2,128)} %shard_map.80), calls=%async_computation.2 | async-start | bytes 163840 | tf_op jit(solution)/shard_map/all_to_all | solution.py:324
  66.0 0.0 copy-done
  66.0 1.8 %shard_map.81 = bf16[64,32,128]{2,1,0:T(8,128)(2,1)} custom-call(bf16[32,64,128]{2,1,0:T(8,128)(2,1)S(1)} %get-tuple-element.28.grad_ref, bf16[32,64,128]{2,1,0:T(8,128)(2,1)S(1)} %bitcast.11, bf16[9,64,64]{2,1,0:T(8,128)(2,1)S(1)} %copy-done), custom_call_target="tpu_custom_call" | custom-call | flops 301989888 | bytes 2097152 | tf_op jit(solution)/shard_map/pallas_call | solution.py:209
  67.8 3.5 %all-to-all-done.2.a = f32[16,2,640]{2,1,0:T(2,128)S(1)} async-done(((f32[16,2,640]{2,1,0:T(2,128)}), f32[16,2,640]{2,1,0:T(2,128)S(1)}, u32[]{:S(2)}, u32[]{:S(2)}) %all-to-all-start.2) | async-done | bytes 81952 | tf_op jit(solution)/shard_map/all_to_all | solution.py:324
  71.4 0.1 shard_map.82
  71.4 13.5 %all_to_all.22.whole_ref = f32[32,2,640]{2,1,0:T(2,128)S(1)} all-to-all(f32[32,2,640]{2,1,0:T(2,128)S(1)} %shard_map.82), channel_id=1, replica_groups={{30,24,26,28,6,0,2,4,14,8,10,12,22,16,18,20,62,56,58,60,38,32,34,36,46,..., dimensions={0} | all-to-all | bytes 327680 | tf_op jit(solution)/shard_map/all_to_all | solution.py:335
  84.9 0.8 shard_map.83
Async XLA Ops:
  0.6 19.6 %collective-permute-start = (bf16[64,4,128]{2,1,0:T(4,128)(2,1)}, bf16[64,4,128]{2,1,0:T(4,128)(2,1)S(1)}, u32[]{:S(2)}, u32[]{:S(2)}) collective-permute-start(bf16[64,4,128]{2,1,0:T(4,128)(2,1)} %bitcast.12), channel_id=1, source_target_pairs={{0,1},{1,0},{2,3},{3,2},{4,5},{5,4},{6,7},{7,6},{8,9},{9,8},{10,11... | collective-permute-start | bytes 196616 | tf_op jit(solution)/shard_map/ppermute | solution.py:226
  16.9 3.3 %copy-start.1 = (bf16[64,4,1,128]{3,1,2,0:T(4,128)(2,1)S(1)}, bf16[64,4,1,128]{3,1,2,0:T(4,128)(2,1)}, u32[]{:S(2)}) copy-start(bf16[64,4,1,128]{3,1,2,0:T(4,128)(2,1)} %param.6) | copy-start | bytes 196612
  20.3 5.1 %collective-permute-start.1 = (bf16[2,64,128]{2,1,0:T(8,128)(2,1)S(1)}, bf16[2,64,128]{2,1,0:T(8,128)(2,1)S(1)}, u32[]{:S(2)}, u32[]{:S(2)}) collective-permute-start(bf16[2,64,128]{2,1,0:T(8,128)(2,1)S(1)} %get-tuple-element.24), channel_id=1, source_target_pairs={{0,32},{2,34},{4,36},{6,38},{8,40},{10,42},{12,44},{14,46},{16,48}... | collective-permute-start | bytes 98312 | tf_op jit(solution)/shard_map/ppermute | solution.py:266
  41.2 24.8 %copy-start = (bf16[9,64,64]{2,1,0:T(8,128)(2,1)S(1)}, bf16[9,64,64]{2,1,0:T(8,128)(2,1)}, u32[]{:S(2)}) copy-start(bf16[9,64,64]{2,1,0:T(8,128)(2,1)} %weight_ref.1) | copy-start | bytes 221188
  54.9 16.4 %all-to-all-start.2 = ((f32[16,2,640]{2,1,0:T(2,128)}), f32[16,2,640]{2,1,0:T(2,128)S(1)}, u32[]{:S(2)}, u32[]{:S(2)}) async-start(f32[16,2,640]{2,1,0:T(2,128)} %shard_map.80), calls=%async_computation.2 | async-start | bytes 163840 | tf_op jit(solution)/shard_map/all_to_all | solution.py:324

commit v9 on v8

--- a/solution.py
+++ b/solution.py
@@ -187,20 +187,22 @@
 
 
 def unpack_kernel(whole_ref, weight_ref, bias_ref):
-    whole = jnp.concatenate([whole_ref[piece] for piece in range(N_FLAT)], axis=0)
+    whole = whole_ref[...].astype(jnp.float32)
+    whole = jnp.concatenate([whole[piece] for piece in range(N_FLAT)], axis=0)
     for tap in range(9):
         weight_ref[tap] = whole[:, tap * C : (tap + 1) * C]
     bias_ref[...] = whole[0:1, 9 * C :]
 
 
 def spread_sum_kernel(parts_ref, out_ref):
-    total = jnp.sum(parts_ref[...], axis=0)
+    total = jnp.sum(parts_ref[...].astype(jnp.float32), axis=0).astype(out_ref.dtype)
     for copy in range(out_ref.shape[0]):
         out_ref[copy] = total
 
 
 def scaled_sum_kernel(factor, parts_ref, out_ref):
-    total = jnp.sum(parts_ref[...], axis=0) * factor
+    total = jnp.sum(parts_ref[...].astype(jnp.float32), axis=0) * factor
+    total = total.astype(out_ref.dtype)
     for copy in range(out_ref.shape[0]):
         out_ref[copy] = total
 
@@ -311,7 +313,7 @@
     ]
     parts = lax.all_to_all(sums, AXES, 0, 0, axis_index_groups=flats, tiled=True)
     sent = call(
-        spread_sum_kernel, shape((N_COLUMN, PIECE, LONG), f32), [], 1 << 16, 1 << 18, parts
+        spread_sum_kernel, shape((N_COLUMN, PIECE, LONG), bf16), [], 1 << 16, 1 << 18, parts
     )
     columns = [
         [
@@ -326,7 +328,7 @@
     factor = float(512 * Y * X) ** -0.5
     sent = call(
         lambda a, b: scaled_sum_kernel(factor, a, b),
-        shape((N_FLAT, PIECE, LONG), f32),
+        shape((N_FLAT, PIECE, LONG), bf16),
         [],
         1 << 16,
         1 << 18,

time: 86.1 us -> 84 us (0.976)
  blocking collectives: 41.4 us -> 40 us
    all_to_all x1, blocking collectives: 13.5 us -> 12.1 us  [on_device(): lax.all_to_all(sent, AXES, 0, 0, axis_index_groups=flats, tiled=True)]
where the time goes in v9:
time: 84 us; the launch traced here: 83.7 us
  blocking collectives  40 us (48%)
  starting transfers between devices  31.5 us (38%)
  Pallas kernels  7.64 us (9%)
  waiting for transfers between devices  3.87 us (5%)
    ppermute x1, starting transfers between devices, on_device(): other = lax.ppermute(raw, 'zh', [(0, 1), (1, 0)])  16.3 us
    all_to_all x1, blocking collectives, on_device(): lax.all_to_all(field, AXES, 0, 0, axis_index_groups=crosses, tiled=True)  15.7 us
    all_to_all x1, blocking collectives, on_device(): lax.all_to_all(sums, AXES, 0, 0, axis_index_groups=flats, tiled=True)  12.2 us
    all_to_all x1, blocking collectives, on_device(): lax.all_to_all(sent, AXES, 0, 0, axis_index_groups=flats, tiled=True)  12.1 us
    all_to_all x1, starting transfers between devices, on_device(): lax.all_to_all(sent, AXES, 0, 0, axis_index_groups=columns, tiled=True)  11.1 us
    pallas_call x8, Pallas kernels, call(): pl.pallas_call(kernel, out_shape=outs, in_specs=[pl.BlockSpec(memory_spac...  7.64 us
    ppermute x1, starting transfers between devices, on_device(): halo = lax.ppermute(last, AXES, hops)  4.13 us
    all_to_all x1, waiting for transfers between devices, on_device(): lax.all_to_all(sent, AXES, 0, 0, axis_index_groups=columns, tiled=True)  2.86 us
  transfers between devices with their start and end apart: 3, of which 2 were waited for; matrix products, arithmetic and copies ran while one was open for 0% of the time, Pallas kernels for 6%

profile of v9, /device:TPU:1, one launch (start us, length us, event | category | flops | bytes accessed | tf_op | source)
XLA Modules:
  0.0 83.7 jit_solution(12719233735610635376)
XLA Ops:
  0.6 16.3 %collective-permute-start = (bf16[64,4,128]{2,1,0:T(4,128)(2,1)}, bf16[64,4,128]{2,1,0:T(4,128)(2,1)S(1)}, u32[]{:S(2)}, u32[]{:S(2)}) collective-permute-start(bf16[64,4,128]{2,1,0:T(4,128)(2,1)} %bitcast.12), channel_id=1, source_target_pairs={{0,1},{1,0},{2,3},{3,2},{4,5},{5,4},{6,7},{7,6},{8,9},{9,8},{10,11... | collective-permute-start | bytes 196616 | tf_op jit(solution)/shard_map/ppermute | solution.py:228
  16.9 0.0 copy-start.1
  16.9 3.3 %shard_map.76 = (f32[32,64,128]{2,1,0:T(8,128)S(1)}, bf16[4096,256]{1,0:T(8,128)(2,1)S(1)}, f32[8,128]{1,0:T(8,128)S(1)}) custom-call(s32[1]{0:T(128)} %bitcast.half_ref, f32[1,9]{1,0:T(1,128)} %bitcast.16, f32[1,64]{1,0:T(1,128)} %bitcast.17, bf16[64,32,128]{2,1,0:T(8,128)(2,1)} %bitcast.15, bf16[9,64,64]{2,1,0:T(8,128)(2,1)} %weight_ref.1), custom_call_target="tpu_custom_call" | custom-call | flops 19327352832 | bytes 134217728 | tf_op jit(solution)/shard_map/pallas_call | solution.py:211
  20.2 0.0 collective-permute-done.other_ref
  20.2 0.0 copy-done.1
  20.2 0.1 shard_map.77
  20.3 4.1 %collective-permute-start.1 = (bf16[2,64,128]{2,1,0:T(8,128)(2,1)S(1)}, bf16[2,64,128]{2,1,0:T(8,128)(2,1)S(1)}, u32[]{:S(2)}, u32[]{:S(2)}) collective-permute-start(bf16[2,64,128]{2,1,0:T(8,128)(2,1)S(1)} %get-tuple-element.24), channel_id=1, source_target_pairs={{0,32},{2,34},{4,36},{6,38},{8,40},{10,42},{12,44},{14,46},{16,48}... | collective-permute-start | bytes 98312 | tf_op jit(solution)/shard_map/ppermute | solution.py:268
  24.4 1.0 %collective-permute-done.1.halo_ref = bf16[2,64,128]{2,1,0:T(8,128)(2,1)S(1)} collective-permute-done((bf16[2,64,128]{2,1,0:T(8,128)(2,1)S(1)}, bf16[2,64,128]{2,1,0:T(8,128)(2,1)S(1)}, u32[]{:S(2)}, u32[]{:S(2)}) %collective-permute-start.1) | collective-permute-done | bytes 32800 | tf_op jit(solution)/shard_map/ppermute | solution.py:268
  25.4 0.1 shard_map.78
  25.5 15.7 %all_to_all.20 = bf16[16,2,64,128]{3,2,1,0:T(8,128)(2,1)S(1)} all-to-all(bf16[16,2,64,128]{3,2,1,0:T(8,128)(2,1)S(1)} %shard_map.78), channel_id=1, replica_groups={{30,24,26,28,6,0,2,4,14,8,10,12,22,16,18,20},{31,25,27,29,7,1,3,5,15,9,..., dimensions={0} | all-to-all | bytes 1048576 | tf_op jit(solution)/shard_map/all_to_all | solution.py:286
  41.2 0.0 copy-start
  41.2 0.8 shard_map.79
  42.0 12.2 %all_to_all.21.parts_ref = f32[32,2,640]{2,1,0:T(2,128)S(1)} all-to-all(f32[32,2,640]{2,1,0:T(2,128)S(1)} %get-tuple-element.27), channel_id=1, replica_groups={{30,24,26,28,6,0,2,4,14,8,10,12,22,16,18,20,62,56,58,60,38,32,34,36,46,..., dimensions={0} | all-to-all | bytes 327680 | tf_op jit(solution)/shard_map/all_to_all | solution.py:314
  54.2 0.7 shard_map.80
  54.9 11.1 %all-to-all-start.2 = ((bf16[16,2,640]{2,1,0:T(2,128)(2,1)}), bf16[16,2,640]{2,1,0:T(2,128)(2,1)S(1)}, u32[]{:S(2)}, u32[]{:S(2)}) async-start(bf16[16,2,640]{2,1,0:T(2,128)(2,1)} %shard_map.80), calls=%async_computation.2 | async-start | bytes 81920 | tf_op jit(solution)/shard_map/all_to_all | solution.py:326
  66.0 0.0 copy-done
  66.0 1.8 %shard_map.81 = bf16[64,32,128]{2,1,0:T(8,128)(2,1)} custom-call(bf16[32,64,128]{2,1,0:T(8,128)(2,1)S(1)} %get-tuple-element.28.grad_ref, bf16[32,64,128]{2,1,0:T(8,128)(2,1)S(1)} %bitcast.11, bf16[9,64,64]{2,1,0:T(8,128)(2,1)S(1)} %copy-done), custom_call_target="tpu_custom_call" | custom-call | flops 301989888 | bytes 2097152 | tf_op jit(solution)/shard_map/pallas_call | solution.py:211
  67.8 2.9 %all-to-all-done.2.a = bf16[16,2,640]{2,1,0:T(2,128)(2,1)S(1)} async-done(((bf16[16,2,640]{2,1,0:T(2,128)(2,1)}), bf16[16,2,640]{2,1,0:T(2,128)(2,1)S(1)}, u32[]{:S(2)}, u32[]{:S(2)}) %all-to-all-start.2) | async-done | bytes 40992 | tf_op jit(solution)/shard_map/all_to_all | solution.py:326
  70.7 0.1 shard_map.82
  70.8 12.1 %all_to_all.22.whole_ref = bf16[32,2,640]{2,1,0:T(2,128)(2,1)S(1)} all-to-all(bf16[32,2,640]{2,1,0:T(2,128)(2,1)S(1)} %shard_map.82), channel_id=1, replica_groups={{30,24,26,28,6,0,2,4,14,8,10,12,22,16,18,20,62,56,58,60,38,32,34,36,46,..., dimensions={0} | all-to-all | bytes 163840 | tf_op jit(solution)/shard_map/all_to_all | solution.py:337
  82.9 0.8 %shard_map.83 = (f32[9,64,64]{2,1,0:T(8,128)}, f32[1,64]{1,0:T(1,128)}) custom-call(bf16[32,2,640]{2,1,0:T(2,128)(2,1)S(1)} %all_to_all.22.whole_ref), custom_call_target="tpu_custom_call" | custom-call | flops 1 | bytes 262144 | tf_op jit(solution)/shard_map/pallas_call | solution.py:211
Async XLA Ops:
  0.6 19.6 %collective-permute-start = (bf16[64,4,128]{2,1,0:T(4,128)(2,1)}, bf16[64,4,128]{2,1,0:T(4,128)(2,1)S(1)}, u32[]{:S(2)}, u32[]{:S(2)}) collective-permute-start(bf16[64,4,128]{2,1,0:T(4,128)(2,1)} %bitcast.12), channel_id=1, source_target_pairs={{0,1},{1,0},{2,3},{3,2},{4,5},{5,4},{6,7},{7,6},{8,9},{9,8},{10,11... | collective-permute-start | bytes 196616 | tf_op jit(solution)/shard_map/ppermute | solution.py:228
  16.9 3.3 %copy-start.1 = (bf16[64,4,1,128]{3,1,2,0:T(4,128)(2,1)S(1)}, bf16[64,4,1,128]{3,1,2,0:T(4,128)(2,1)}, u32[]{:S(2)}) copy-start(bf16[64,4,1,128]{3,1,2,0:T(4,128)(2,1)} %param.6) | copy-start | bytes 196612
  20.3 5.1 %collective-permute-start.1 = (bf16[2,64,128]{2,1,0:T(8,128)(2,1)S(1)}, bf16[2,64,128]{2,1,0:T(8,128)(2,1)S(1)}, u32[]{:S(2)}, u32[]{:S(2)}) collective-permute-start(bf16[2,64,128]{2,1,0:T(8,128)(2,1)S(1)} %get-tuple-element.24), channel_id=1, source_target_pairs={{0,32},{2,34},{4,36},{6,38},{8,40},{10,42},{12,44},{14,46},{16,48}... | collective-permute-start | bytes 98312 | tf_op jit(solution)/shard_map/ppermute | solution.py:268
  41.2 24.8 %copy-start = (bf16[9,64,64]{2,1,0:T(8,128)(2,1)S(1)}, bf16[9,64,64]{2,1,0:T(8,128)(2,1)}, u32[]{:S(2)}) copy-start(bf16[9,64,64]{2,1,0:T(8,128)(2,1)} %weight_ref.1) | copy-start | bytes 221188
  54.9 15.8 %all-to-all-start.2 = ((bf16[16,2,640]{2,1,0:T(2,128)(2,1)}), bf16[16,2,640]{2,1,0:T(2,128)(2,1)S(1)}, u32[]{:S(2)}, u32[]{:S(2)}) async-start(bf16[16,2,640]{2,1,0:T(2,128)(2,1)} %shard_map.80), calls=%async_computation.2 | async-start | bytes 81920 | tf_op jit(solution)/shard_map/all_to_all | solution.py:326

commit v10 on v9

--- a/solution.py
+++ b/solution.py
@@ -18,15 +18,17 @@
 N_FLAT = 32
 N_GROUP = 16
 N_COLUMN = 16
-FIRST = 7
+FIRST = 8
 PIECE = 2
 LONG = 640
 WIDE = 256
 VMEM_LIMIT = 16 * 1024 * 1024
-CORNER = 3
-CROSS_ORDER = [
-    ((CORNER + a) % 4, (CORNER + b) % 4) for a in range(4) for b in range(4)
-]
+def ranks(corner):
+    return [((corner[0] + a) % 4, (corner[1] + b) % 4) for a in range(4) for b in range(4)]
+
+
+CROSS_ORDER = ranks((2, 2))
+FLAT_ORDER = ranks((2, 2))
 PLACE = [CROSS_ORDER.index((y // 8, y // 2 % 4)) * 2 + y % 2 for y in range(Y)]
 
 
@@ -307,7 +309,7 @@
     )
 
     flats = [
-        [((zl * 2 + core) * 4 + x) * 8 + y * 2 + zh for core in range(2) for x, y in CROSS_ORDER]
+        [((zl * 2 + core) * 4 + x) * 8 + y * 2 + zh for core in range(2) for x, y in FLAT_ORDER]
         for zl in range(8)
         for zh in range(2)
     ]

time: 84 us -> 81.6 us (0.971)
  waiting for transfers between devices: 3.87 us -> 1.76 us
  blocking collectives: 40 us -> 37.9 us
  starting transfers between devices: 31.5 us -> 33.3 us
    all_to_all x1, waiting for transfers between devices: 2.86 us -> 0.76 us  [on_device(): lax.all_to_all(sent, AXES, 0, 0, axis_index_groups=columns, tiled=True)]
    all_to_all x1, starting transfers between devices: 11.1 us -> 12.9 us  [on_device(): lax.all_to_all(sent, AXES, 0, 0, axis_index_groups=columns, tiled=True)]
    all_to_all x1, blocking collectives: 12.2 us -> 10.8 us  [on_device(): lax.all_to_all(sums, AXES, 0, 0, axis_index_groups=flats, tiled=True)]
where the time goes in v10:
time: 81.6 us; the launch traced here: 81.3 us
  blocking collectives  37.9 us (46%)
  starting transfers between devices  33.3 us (41%)
  Pallas kernels  7.64 us (9%)
  waiting for transfers between devices  1.76 us (2%)
    ppermute x1, starting transfers between devices, on_device(): other = lax.ppermute(raw, 'zh', [(0, 1), (1, 0)])  16.3 us
    all_to_all x1, blocking collectives, on_device(): lax.all_to_all(field, AXES, 0, 0, axis_index_groups=crosses, tiled=True)  15.5 us
    all_to_all x1, starting transfers between devices, on_device(): lax.all_to_all(sent, AXES, 0, 0, axis_index_groups=columns, tiled=True)  12.9 us
    all_to_all x1, blocking collectives, on_device(): lax.all_to_all(sent, AXES, 0, 0, axis_index_groups=flats, tiled=True)  11.7 us
    all_to_all x1, blocking collectives, on_device(): lax.all_to_all(sums, AXES, 0, 0, axis_index_groups=flats, tiled=True)  10.8 us
    pallas_call x8, Pallas kernels, call(): pl.pallas_call(kernel, out_shape=outs, in_specs=[pl.BlockSpec(memory_spac...  7.64 us
    ppermute x1, starting transfers between devices, on_device(): halo = lax.ppermute(last, AXES, hops)  4.13 us
  transfers between devices with their start and end apart: 3, of which 2 were waited for; matrix products, arithmetic and copies ran while one was open for 0% of the time, Pallas kernels for 6%

profile of v10, /device:TPU:1, one launch (start us, length us, event | category | flops | bytes accessed | tf_op | source)
XLA Modules:
  0.0 81.3 jit_solution(13514264369691636274)
XLA Ops:
  0.6 16.3 %collective-permute-start = (bf16[64,4,128]{2,1,0:T(4,128)(2,1)}, bf16[64,4,128]{2,1,0:T(4,128)(2,1)S(1)}, u32[]{:S(2)}, u32[]{:S(2)}) collective-permute-start(bf16[64,4,128]{2,1,0:T(4,128)(2,1)} %bitcast.12), channel_id=1, source_target_pairs={{0,1},{1,0},{2,3},{3,2},{4,5},{5,4},{6,7},{7,6},{8,9},{9,8},{10,11... | collective-permute-start | bytes 196616 | tf_op jit(solution)/shard_map/ppermute | solution.py:230
  16.9 0.0 copy-start.1
  16.9 3.3 %shard_map.76 = (f32[32,64,128]{2,1,0:T(8,128)S(1)}, bf16[4096,256]{1,0:T(8,128)(2,1)S(1)}, f32[8,128]{1,0:T(8,128)S(1)}) custom-call(s32[1]{0:T(128)} %bitcast.half_ref, f32[1,9]{1,0:T(1,128)} %bitcast.16, f32[1,64]{1,0:T(1,128)} %bitcast.17, bf16[64,32,128]{2,1,0:T(8,128)(2,1)} %bitcast.15, bf16[9,64,64]{2,1,0:T(8,128)(2,1)} %weight_ref.1), custom_call_target="tpu_custom_call" | custom-call | flops 19327352832 | bytes 134217728 | tf_op jit(solution)/shard_map/pallas_call | solution.py:213
  20.2 0.0 collective-permute-done.other_ref
  20.2 0.0 copy-done.1
  20.2 0.1 shard_map.77
  20.3 4.1 %collective-permute-start.1 = (bf16[2,64,128]{2,1,0:T(8,128)(2,1)S(1)}, bf16[2,64,128]{2,1,0:T(8,128)(2,1)S(1)}, u32[]{:S(2)}, u32[]{:S(2)}) collective-permute-start(bf16[2,64,128]{2,1,0:T(8,128)(2,1)S(1)} %get-tuple-element.24), channel_id=1, source_target_pairs={{0,32},{2,34},{4,36},{6,38},{8,40},{10,42},{12,44},{14,46},{16,48}... | collective-permute-start | bytes 98312 | tf_op jit(solution)/shard_map/ppermute | solution.py:270
  24.4 1.0 %collective-permute-done.1.halo_ref = bf16[2,64,128]{2,1,0:T(8,128)(2,1)S(1)} collective-permute-done((bf16[2,64,128]{2,1,0:T(8,128)(2,1)S(1)}, bf16[2,64,128]{2,1,0:T(8,128)(2,1)S(1)}, u32[]{:S(2)}, u32[]{:S(2)}) %collective-permute-start.1) | collective-permute-done | bytes 32800 | tf_op jit(solution)/shard_map/ppermute | solution.py:270
  25.4 0.1 shard_map.78
  25.5 15.5 %all_to_all.20 = bf16[16,2,64,128]{3,2,1,0:T(8,128)(2,1)S(1)} all-to-all(bf16[16,2,64,128]{3,2,1,0:T(8,128)(2,1)S(1)} %shard_map.78), channel_id=1, replica_groups={{20,22,16,18,28,30,24,26,4,6,0,2,12,14,8,10},{21,23,17,19,29,31,25,27,5..., dimensions={0} | all-to-all | bytes 1048576 | tf_op jit(solution)/shard_map/all_to_all | solution.py:288
  41.0 0.0 copy-start
  41.0 0.8 shard_map.79
  41.8 10.8 %all_to_all.21.parts_ref = f32[32,2,640]{2,1,0:T(2,128)S(1)} all-to-all(f32[32,2,640]{2,1,0:T(2,128)S(1)} %get-tuple-element.27), channel_id=1, replica_groups={{20,22,16,18,28,30,24,26,4,6,0,2,12,14,8,10,52,54,48,50,60,62,56,58,36,..., dimensions={0} | all-to-all | bytes 327680 | tf_op jit(solution)/shard_map/all_to_all | solution.py:316
  52.6 0.7 shard_map.80
  53.2 12.9 %all-to-all-start.2 = ((bf16[16,2,640]{2,1,0:T(2,128)(2,1)}), bf16[16,2,640]{2,1,0:T(2,128)(2,1)S(1)}, u32[]{:S(2)}, u32[]{:S(2)}) async-start(bf16[16,2,640]{2,1,0:T(2,128)(2,1)} %shard_map.80), calls=%async_computation.2 | async-start | bytes 81920 | tf_op jit(solution)/shard_map/all_to_all | solution.py:328
  66.1 0.0 copy-done
  66.1 1.8 %shard_map.81 = bf16[64,32,128]{2,1,0:T(8,128)(2,1)} custom-call(bf16[32,64,128]{2,1,0:T(8,128)(2,1)S(1)} %get-tuple-element.28.grad_ref, bf16[32,64,128]{2,1,0:T(8,128)(2,1)S(1)} %bitcast.11, bf16[9,64,64]{2,1,0:T(8,128)(2,1)S(1)} %copy-done), custom_call_target="tpu_custom_call" | custom-call | flops 301989888 | bytes 2097152 | tf_op jit(solution)/shard_map/pallas_call | solution.py:213
  68.0 0.8 all-to-all-done.2.a
  68.7 0.1 shard_map.82
  68.8 11.7 %all_to_all.22.whole_ref = bf16[32,2,640]{2,1,0:T(2,128)(2,1)S(1)} all-to-all(bf16[32,2,640]{2,1,0:T(2,128)(2,1)S(1)} %shard_map.82), channel_id=1, replica_groups={{20,22,16,18,28,30,24,26,4,6,0,2,12,14,8,10,52,54,48,50,60,62,56,58,36,..., dimensions={0} | all-to-all | bytes 163840 | tf_op jit(solution)/shard_map/all_to_all | solution.py:339
  80.5 0.8 %shard_map.83 = (f32[9,64,64]{2,1,0:T(8,128)}, f32[1,64]{1,0:T(1,128)}) custom-call(bf16[32,2,640]{2,1,0:T(2,128)(2,1)S(1)} %all_to_all.22.whole_ref), custom_call_target="tpu_custom_call" | custom-call | flops 1 | bytes 262144 | tf_op jit(solution)/shard_map/pallas_call | solution.py:213
Async XLA Ops:
  0.6 19.6 %collective-permute-start = (bf16[64,4,128]{2,1,0:T(4,128)(2,1)}, bf16[64,4,128]{2,1,0:T(4,128)(2,1)S(1)}, u32[]{:S(2)}, u32[]{:S(2)}) collective-permute-start(bf16[64,4,128]{2,1,0:T(4,128)(2,1)} %bitcast.12), channel_id=1, source_target_pairs={{0,1},{1,0},{2,3},{3,2},{4,5},{5,4},{6,7},{7,6},{8,9},{9,8},{10,11... | collective-permute-start | bytes 196616 | tf_op jit(solution)/shard_map/ppermute | solution.py:230
  16.9 3.3 %copy-start.1 = (bf16[64,4,1,128]{3,1,2,0:T(4,128)(2,1)S(1)}, bf16[64,4,1,128]{3,1,2,0:T(4,128)(2,1)}, u32[]{:S(2)}) copy-start(bf16[64,4,1,128]{3,1,2,0:T(4,128)(2,1)} %param.6) | copy-start | bytes 196612
  20.3 5.1 %collective-permute-start.1 = (bf16[2,64,128]{2,1,0:T(8,128)(2,1)S(1)}, bf16[2,64,128]{2,1,0:T(8,128)(2,1)S(1)}, u32[]{:S(2)}, u32[]{:S(2)}) collective-permute-start(bf16[2,64,128]{2,1,0:T(8,128)(2,1)S(1)} %get-tuple-element.24), channel_id=1, source_target_pairs={{0,32},{2,34},{4,36},{6,38},{8,40},{10,42},{12,44},{14,46},{16,48}... | collective-permute-start | bytes 98312 | tf_op jit(solution)/shard_map/ppermute | solution.py:270
  41.0 25.1 %copy-start = (bf16[9,64,64]{2,1,0:T(8,128)(2,1)S(1)}, bf16[9,64,64]{2,1,0:T(8,128)(2,1)}, u32[]{:S(2)}) copy-start(bf16[9,64,64]{2,1,0:T(8,128)(2,1)} %weight_ref.1) | copy-start | bytes 221188
  53.2 15.5 %all-to-all-start.2 = ((bf16[16,2,640]{2,1,0:T(2,128)(2,1)}), bf16[16,2,640]{2,1,0:T(2,128)(2,1)S(1)}, u32[]{:S(2)}, u32[]{:S(2)}) async-start(bf16[16,2,640]{2,1,0:T(2,128)(2,1)} %shard_map.80), calls=%async_computation.2 | async-start | bytes 81920 | tf_op jit(solution)/shard_map/all_to_all | solution.py:328

commit v11 on v10

--- a/solution.py
+++ b/solution.py
@@ -309,7 +309,7 @@
     )
 
     flats = [
-        [((zl * 2 + core) * 4 + x) * 8 + y * 2 + zh for core in range(2) for x, y in FLAT_ORDER]
+        [((zl * 2 + core) * 4 + x) * 8 + y * 2 + zh for core in (1, 0) for x, y in FLAT_ORDER]
         for zl in range(8)
         for zh in range(2)
     ]

time: 81.6 us -> 81.1 us (level)
  no operation moved by 1% of the time
where the time goes in v11:
time: 81.1 us; the launch traced here: 80.7 us
  blocking collectives  37.3 us (46%)
  starting transfers between devices  33.3 us (41%)
  Pallas kernels  7.64 us (9%)
  waiting for transfers between devices  1.76 us (2%)
    ppermute x1, starting transfers between devices, on_device(): other = lax.ppermute(raw, 'zh', [(0, 1), (1, 0)])  16.3 us
    all_to_all x1, blocking collectives, on_device(): lax.all_to_all(field, AXES, 0, 0, axis_index_groups=crosses, tiled=True)  15.5 us
    all_to_all x1, starting transfers between devices, on_device(): lax.all_to_all(sent, AXES, 0, 0, axis_index_groups=columns, tiled=True)  12.9 us
    all_to_all x1, blocking collectives, on_device(): lax.all_to_all(sent, AXES, 0, 0, axis_index_groups=flats, tiled=True)  11.4 us
    all_to_all x1, blocking collectives, on_device(): lax.all_to_all(sums, AXES, 0, 0, axis_index_groups=flats, tiled=True)  10.5 us
    pallas_call x8, Pallas kernels, call(): pl.pallas_call(kernel, out_shape=outs, in_specs=[pl.BlockSpec(memory_spac...  7.64 us
    ppermute x1, starting transfers between devices, on_device(): halo = lax.ppermute(last, AXES, hops)  4.13 us
  transfers between devices with their start and end apart: 3, of which 2 were waited for; matrix products, arithmetic and copies ran while one was open for 0% of the time, Pallas kernels for 6%

profile of v11, /device:TPU:1, one launch (start us, length us, event | category | flops | bytes accessed | tf_op | source)
XLA Modules:
  0.0 80.7 jit_solution(9352644570014667293)
XLA Ops:
  0.6 16.3 %collective-permute-start = (bf16[64,4,128]{2,1,0:T(4,128)(2,1)}, bf16[64,4,128]{2,1,0:T(4,128)(2,1)S(1)}, u32[]{:S(2)}, u32[]{:S(2)}) collective-permute-start(bf16[64,4,128]{2,1,0:T(4,128)(2,1)} %bitcast.12), channel_id=1, source_target_pairs={{0,1},{1,0},{2,3},{3,2},{4,5},{5,4},{6,7},{7,6},{8,9},{9,8},{10,11... | collective-permute-start | bytes 196616 | tf_op jit(solution)/shard_map/ppermute | solution.py:230
  16.9 0.0 copy-start.1
  16.9 3.3 %shard_map.76 = (f32[32,64,128]{2,1,0:T(8,128)S(1)}, bf16[4096,256]{1,0:T(8,128)(2,1)S(1)}, f32[8,128]{1,0:T(8,128)S(1)}) custom-call(s32[1]{0:T(128)} %bitcast.half_ref, f32[1,9]{1,0:T(1,128)} %bitcast.16, f32[1,64]{1,0:T(1,128)} %bitcast.17, bf16[64,32,128]{2,1,0:T(8,128)(2,1)} %bitcast.15, bf16[9,64,64]{2,1,0:T(8,128)(2,1)} %weight_ref.1), custom_call_target="tpu_custom_call" | custom-call | flops 19327352832 | bytes 134217728 | tf_op jit(solution)/shard_map/pallas_call | solution.py:213
  20.2 0.0 collective-permute-done.other_ref
  20.2 0.0 copy-done.1
  20.2 0.1 shard_map.77
  20.3 4.1 %collective-permute-start.1 = (bf16[2,64,128]{2,1,0:T(8,128)(2,1)S(1)}, bf16[2,64,128]{2,1,0:T(8,128)(2,1)S(1)}, u32[]{:S(2)}, u32[]{:S(2)}) collective-permute-start(bf16[2,64,128]{2,1,0:T(8,128)(2,1)S(1)} %get-tuple-element.24), channel_id=1, source_target_pairs={{0,32},{2,34},{4,36},{6,38},{8,40},{10,42},{12,44},{14,46},{16,48}... | collective-permute-start | bytes 98312 | tf_op jit(solution)/shard_map/ppermute | solution.py:270
  24.4 1.0 %collective-permute-done.1.halo_ref = bf16[2,64,128]{2,1,0:T(8,128)(2,1)S(1)} collective-permute-done((bf16[2,64,128]{2,1,0:T(8,128)(2,1)S(1)}, bf16[2,64,128]{2,1,0:T(8,128)(2,1)S(1)}, u32[]{:S(2)}, u32[]{:S(2)}) %collective-permute-start.1) | collective-permute-done | bytes 32800 | tf_op jit(solution)/shard_map/ppermute | solution.py:270
  25.4 0.1 shard_map.78
  25.5 15.5 %all_to_all.20 = bf16[16,2,64,128]{3,2,1,0:T(8,128)(2,1)S(1)} all-to-all(bf16[16,2,64,128]{3,2,1,0:T(8,128)(2,1)S(1)} %shard_map.78), channel_id=1, replica_groups={{20,22,16,18,28,30,24,26,4,6,0,2,12,14,8,10},{21,23,17,19,29,31,25,27,5..., dimensions={0} | all-to-all | bytes 1048576 | tf_op jit(solution)/shard_map/all_to_all | solution.py:288
  41.0 0.0 copy-start
  41.0 0.8 shard_map.79
  41.8 10.5 %all_to_all.21.parts_ref = f32[32,2,640]{2,1,0:T(2,128)S(1)} all-to-all(f32[32,2,640]{2,1,0:T(2,128)S(1)} %get-tuple-element.27), channel_id=1, replica_groups={{52,54,48,50,60,62,56,58,36,38,32,34,44,46,40,42,20,22,16,18,28,30,24,2..., dimensions={0} | all-to-all | bytes 327680 | tf_op jit(solution)/shard_map/all_to_all | solution.py:316
  52.2 0.7 shard_map.80
  52.9 12.9 %all-to-all-start.2 = ((bf16[16,2,640]{2,1,0:T(2,128)(2,1)}), bf16[16,2,640]{2,1,0:T(2,128)(2,1)S(1)}, u32[]{:S(2)}, u32[]{:S(2)}) async-start(bf16[16,2,640]{2,1,0:T(2,128)(2,1)} %shard_map.80), calls=%async_computation.2 | async-start | bytes 81920 | tf_op jit(solution)/shard_map/all_to_all | solution.py:328
  65.8 0.0 copy-done
  65.8 1.8 %shard_map.81 = bf16[64,32,128]{2,1,0:T(8,128)(2,1)} custom-call(bf16[32,64,128]{2,1,0:T(8,128)(2,1)S(1)} %get-tuple-element.28.grad_ref, bf16[32,64,128]{2,1,0:T(8,128)(2,1)S(1)} %bitcast.11, bf16[9,64,64]{2,1,0:T(8,128)(2,1)S(1)} %copy-done), custom_call_target="tpu_custom_call" | custom-call | flops 301989888 | bytes 2097152 | tf_op jit(solution)/shard_map/pallas_call | solution.py:213
  67.6 0.8 all-to-all-done.2.a
  68.4 0.1 shard_map.82
  68.5 11.4 %all_to_all.22.whole_ref = bf16[32,2,640]{2,1,0:T(2,128)(2,1)S(1)} all-to-all(bf16[32,2,640]{2,1,0:T(2,128)(2,1)S(1)} %shard_map.82), channel_id=1, replica_groups={{52,54,48,50,60,62,56,58,36,38,32,34,44,46,40,42,20,22,16,18,28,30,24,2..., dimensions={0} | all-to-all | bytes 163840 | tf_op jit(solution)/shard_map/all_to_all | solution.py:339
  79.9 0.8 %shard_map.83 = (f32[9,64,64]{2,1,0:T(8,128)}, f32[1,64]{1,0:T(1,128)}) custom-call(bf16[32,2,640]{2,1,0:T(2,128)(2,1)S(1)} %all_to_all.22.whole_ref), custom_call_target="tpu_custom_call" | custom-call | flops 1 | bytes 262144 | tf_op jit(solution)/shard_map/pallas_call | solution.py:213
Async XLA Ops:
  0.6 19.6 %collective-permute-start = (bf16[64,4,128]{2,1,0:T(4,128)(2,1)}, bf16[64,4,128]{2,1,0:T(4,128)(2,1)S(1)}, u32[]{:S(2)}, u32[]{:S(2)}) collective-permute-start(bf16[64,4,128]{2,1,0:T(4,128)(2,1)} %bitcast.12), channel_id=1, source_target_pairs={{0,1},{1,0},{2,3},{3,2},{4,5},{5,4},{6,7},{7,6},{8,9},{9,8},{10,11... | collective-permute-start | bytes 196616 | tf_op jit(solution)/shard_map/ppermute | solution.py:230
  16.9 3.3 %copy-start.1 = (bf16[64,4,1,128]{3,1,2,0:T(4,128)(2,1)S(1)}, bf16[64,4,1,128]{3,1,2,0:T(4,128)(2,1)}, u32[]{:S(2)}) copy-start(bf16[64,4,1,128]{3,1,2,0:T(4,128)(2,1)} %param.6) | copy-start | bytes 196612
  20.3 5.1 %collective-permute-start.1 = (bf16[2,64,128]{2,1,0:T(8,128)(2,1)S(1)}, bf16[2,64,128]{2,1,0:T(8,128)(2,1)S(1)}, u32[]{:S(2)}, u32[]{:S(2)}) collective-permute-start(bf16[2,64,128]{2,1,0:T(8,128)(2,1)S(1)} %get-tuple-element.24), channel_id=1, source_target_pairs={{0,32},{2,34},{4,36},{6,38},{8,40},{10,42},{12,44},{14,46},{16,48}... | collective-permute-start | bytes 98312 | tf_op jit(solution)/shard_map/ppermute | solution.py:270
  41.0 24.8 %copy-start = (bf16[9,64,64]{2,1,0:T(8,128)(2,1)S(1)}, bf16[9,64,64]{2,1,0:T(8,128)(2,1)}, u32[]{:S(2)}) copy-start(bf16[9,64,64]{2,1,0:T(8,128)(2,1)} %weight_ref.1) | copy-start | bytes 221188
  52.9 15.5 %all-to-all-start.2 = ((bf16[16,2,640]{2,1,0:T(2,128)(2,1)}), bf16[16,2,640]{2,1,0:T(2,128)(2,1)S(1)}, u32[]{:S(2)}, u32[]{:S(2)}) async-start(bf16[16,2,640]{2,1,0:T(2,128)(2,1)} %shard_map.80), calls=%async_computation.2 | async-start | bytes 81920 | tf_op jit(solution)/shard_map/all_to_all | solution.py:328

commit v12 on v11

--- a/solution.py
+++ b/solution.py
@@ -320,7 +320,7 @@
     columns = [
         [
             (((z % 8) * 2 + core) * N_CROSS + cross) * 2 + z // 8
-            for z in [(FIRST + step) % N_COLUMN for step in range(N_COLUMN)]
+            for z in [(FIRST + 5 * step) % N_COLUMN for step in range(N_COLUMN)]
         ]
         for core in range(2)
         for cross in range(N_CROSS)

time: 81.1 us -> 81 us (level)
  no operation moved by 1% of the time
where the time goes in v12:
time: 81 us; the launch traced here: 80.7 us
  blocking collectives  37.3 us (46%)
  starting transfers between devices  33.3 us (41%)
  Pallas kernels  7.64 us (9%)
  waiting for transfers between devices  1.76 us (2%)
    ppermute x1, starting transfers between devices, on_device(): other = lax.ppermute(raw, 'zh', [(0, 1), (1, 0)])  16.3 us
    all_to_all x1, blocking collectives, on_device(): lax.all_to_all(field, AXES, 0, 0, axis_index_groups=crosses, tiled=True)  15.5 us
    all_to_all x1, starting transfers between devices, on_device(): lax.all_to_all(sent, AXES, 0, 0, axis_index_groups=columns, tiled=True)  12.9 us
    all_to_all x1, blocking collectives, on_device(): lax.all_to_all(sent, AXES, 0, 0, axis_index_groups=flats, tiled=True)  11.4 us
    all_to_all x1, blocking collectives, on_device(): lax.all_to_all(sums, AXES, 0, 0, axis_index_groups=flats, tiled=True)  10.5 us
    pallas_call x8, Pallas kernels, call(): pl.pallas_call(kernel, out_shape=outs, in_specs=[pl.BlockSpec(memory_spac...  7.64 us
    ppermute x1, starting transfers between devices, on_device(): halo = lax.ppermute(last, AXES, hops)  4.13 us
  transfers between devices with their start and end apart: 3, of which 2 were waited for; matrix products, arithmetic and copies ran while one was open for 0% of the time, Pallas kernels for 6%

profile of v12, /device:TPU:1, one launch (start us, length us, event | category | flops | bytes accessed | tf_op | source)
XLA Modules:
  0.0 80.7 jit_solution(4305528018020468730)
XLA Ops:
  0.6 16.3 %collective-permute-start = (bf16[64,4,128]{2,1,0:T(4,128)(2,1)}, bf16[64,4,128]{2,1,0:T(4,128)(2,1)S(1)}, u32[]{:S(2)}, u32[]{:S(2)}) collective-permute-start(bf16[64,4,128]{2,1,0:T(4,128)(2,1)} %bitcast.12), channel_id=1, source_target_pairs={{0,1},{1,0},{2,3},{3,2},{4,5},{5,4},{6,7},{7,6},{8,9},{9,8},{10,11... | collective-permute-start | bytes 196616 | tf_op jit(solution)/shard_map/ppermute | solution.py:230
  16.9 0.0 copy-start.1
  16.9 3.3 %shard_map.76 = (f32[32,64,128]{2,1,0:T(8,128)S(1)}, bf16[4096,256]{1,0:T(8,128)(2,1)S(1)}, f32[8,128]{1,0:T(8,128)S(1)}) custom-call(s32[1]{0:T(128)} %bitcast.half_ref, f32[1,9]{1,0:T(1,128)} %bitcast.16, f32[1,64]{1,0:T(1,128)} %bitcast.17, bf16[64,32,128]{2,1,0:T(8,128)(2,1)} %bitcast.15, bf16[9,64,64]{2,1,0:T(8,128)(2,1)} %weight_ref.1), custom_call_target="tpu_custom_call" | custom-call | flops 19327352832 | bytes 134217728 | tf_op jit(solution)/shard_map/pallas_call | solution.py:213
  20.2 0.0 collective-permute-done.other_ref
  20.2 0.0 copy-done.1
  20.2 0.1 shard_map.77
  20.3 4.1 %collective-permute-start.1 = (bf16[2,64,128]{2,1,0:T(8,128)(2,1)S(1)}, bf16[2,64,128]{2,1,0:T(8,128)(2,1)S(1)}, u32[]{:S(2)}, u32[]{:S(2)}) collective-permute-start(bf16[2,64,128]{2,1,0:T(8,128)(2,1)S(1)} %get-tuple-element.24), channel_id=1, source_target_pairs={{0,32},{2,34},{4,36},{6,38},{8,40},{10,42},{12,44},{14,46},{16,48}... | collective-permute-start | bytes 98312 | tf_op jit(solution)/shard_map/ppermute | solution.py:270
  24.4 1.0 %collective-permute-done.1.halo_ref = bf16[2,64,128]{2,1,0:T(8,128)(2,1)S(1)} collective-permute-done((bf16[2,64,128]{2,1,0:T(8,128)(2,1)S(1)}, bf16[2,64,128]{2,1,0:T(8,128)(2,1)S(1)}, u32[]{:S(2)}, u32[]{:S(2)}) %collective-permute-start.1) | collective-permute-done | bytes 32800 | tf_op jit(solution)/shard_map/ppermute | solution.py:270
  25.4 0.1 shard_map.78
  25.5 15.5 %all_to_all.20 = bf16[16,2,64,128]{3,2,1,0:T(8,128)(2,1)S(1)} all-to-all(bf16[16,2,64,128]{3,2,1,0:T(8,128)(2,1)S(1)} %shard_map.78), channel_id=1, replica_groups={{20,22,16,18,28,30,24,26,4,6,0,2,12,14,8,10},{21,23,17,19,29,31,25,27,5..., dimensions={0} | all-to-all | bytes 1048576 | tf_op jit(solution)/shard_map/all_to_all | solution.py:288
  41.0 0.0 copy-start
  41.0 0.8 shard_map.79
  41.8 10.5 %all_to_all.21.parts_ref = f32[32,2,640]{2,1,0:T(2,128)S(1)} all-to-all(f32[32,2,640]{2,1,0:T(2,128)S(1)} %get-tuple-element.27), channel_id=1, replica_groups={{52,54,48,50,60,62,56,58,36,38,32,34,44,46,40,42,20,22,16,18,28,30,24,2..., dimensions={0} | all-to-all | bytes 327680 | tf_op jit(solution)/shard_map/all_to_all | solution.py:316
  52.2 0.7 shard_map.80
  52.9 12.9 %all-to-all-start.2 = ((bf16[16,2,640]{2,1,0:T(2,128)(2,1)}), bf16[16,2,640]{2,1,0:T(2,128)(2,1)S(1)}, u32[]{:S(2)}, u32[]{:S(2)}) async-start(bf16[16,2,640]{2,1,0:T(2,128)(2,1)} %shard_map.80), calls=%async_computation.2 | async-start | bytes 81920 | tf_op jit(solution)/shard_map/all_to_all | solution.py:328
  65.8 0.0 copy-done
  65.8 1.8 %shard_map.81 = bf16[64,32,128]{2,1,0:T(8,128)(2,1)} custom-call(bf16[32,64,128]{2,1,0:T(8,128)(2,1)S(1)} %get-tuple-element.28.grad_ref, bf16[32,64,128]{2,1,0:T(8,128)(2,1)S(1)} %bitcast.11, bf16[9,64,64]{2,1,0:T(8,128)(2,1)S(1)} %copy-done), custom_call_target="tpu_custom_call" | custom-call | flops 301989888 | bytes 2097152 | tf_op jit(solution)/shard_map/pallas_call | solution.py:213
  67.6 0.8 all-to-all-done.2.a
  68.4 0.1 shard_map.82
  68.5 11.4 %all_to_all.22.whole_ref = bf16[32,2,640]{2,1,0:T(2,128)(2,1)S(1)} all-to-all(bf16[32,2,640]{2,1,0:T(2,128)(2,1)S(1)} %shard_map.82), channel_id=1, replica_groups={{52,54,48,50,60,62,56,58,36,38,32,34,44,46,40,42,20,22,16,18,28,30,24,2..., dimensions={0} | all-to-all | bytes 163840 | tf_op jit(solution)/shard_map/all_to_all | solution.py:339
  79.8 0.8 %shard_map.83 = (f32[9,64,64]{2,1,0:T(8,128)}, f32[1,64]{1,0:T(1,128)}) custom-call(bf16[32,2,640]{2,1,0:T(2,128)(2,1)S(1)} %all_to_all.22.whole_ref), custom_call_target="tpu_custom_call" | custom-call | flops 1 | bytes 262144 | tf_op jit(solution)/shard_map/pallas_call | solution.py:213
Async XLA Ops:
  0.6 19.6 %collective-permute-start = (bf16[64,4,128]{2,1,0:T(4,128)(2,1)}, bf16[64,4,128]{2,1,0:T(4,128)(2,1)S(1)}, u32[]{:S(2)}, u32[]{:S(2)}) collective-permute-start(bf16[64,4,128]{2,1,0:T(4,128)(2,1)} %bitcast.12), channel_id=1, source_target_pairs={{0,1},{1,0},{2,3},{3,2},{4,5},{5,4},{6,7},{7,6},{8,9},{9,8},{10,11... | collective-permute-start | bytes 196616 | tf_op jit(solution)/shard_map/ppermute | solution.py:230
  16.9 3.3 %copy-start.1 = (bf16[64,4,1,128]{3,1,2,0:T(4,128)(2,1)S(1)}, bf16[64,4,1,128]{3,1,2,0:T(4,128)(2,1)}, u32[]{:S(2)}) copy-start(bf16[64,4,1,128]{3,1,2,0:T(4,128)(2,1)} %param.6) | copy-start | bytes 196612
  20.3 5.1 %collective-permute-start.1 = (bf16[2,64,128]{2,1,0:T(8,128)(2,1)S(1)}, bf16[2,64,128]{2,1,0:T(8,128)(2,1)S(1)}, u32[]{:S(2)}, u32[]{:S(2)}) collective-permute-start(bf16[2,64,128]{2,1,0:T(8,128)(2,1)S(1)} %get-tuple-element.24), channel_id=1, source_target_pairs={{0,32},{2,34},{4,36},{6,38},{8,40},{10,42},{12,44},{14,46},{16,48}... | collective-permute-start | bytes 98312 | tf_op jit(solution)/shard_map/ppermute | solution.py:270
  41.0 24.8 %copy-start = (bf16[9,64,64]{2,1,0:T(8,128)(2,1)S(1)}, bf16[9,64,64]{2,1,0:T(8,128)(2,1)}, u32[]{:S(2)}) copy-start(bf16[9,64,64]{2,1,0:T(8,128)(2,1)} %weight_ref.1) | copy-start | bytes 221188
  52.9 15.5 %all-to-all-start.2 = ((bf16[16,2,640]{2,1,0:T(2,128)(2,1)}), bf16[16,2,640]{2,1,0:T(2,128)(2,1)S(1)}, u32[]{:S(2)}, u32[]{:S(2)}) async-start(bf16[16,2,640]{2,1,0:T(2,128)(2,1)} %shard_map.80), calls=%async_computation.2 | async-start | bytes 81920 | tf_op jit(solution)/shard_map/all_to_all | solution.py:328

commit v13 on v11

--- a/solution.py
+++ b/solution.py
@@ -188,12 +188,18 @@
             before = row
 
 
-def unpack_kernel(whole_ref, weight_ref, bias_ref):
+def unpack_kernel(whole_ref, weight_far, bias_ref, weight_ref, sems):
     whole = whole_ref[...].astype(jnp.float32)
     whole = jnp.concatenate([whole[piece] for piece in range(N_FLAT)], axis=0)
+    copies = []
     for tap in range(9):
         weight_ref[tap] = whole[:, tap * C : (tap + 1) * C]
+        copy = pltpu.make_async_copy(weight_ref.at[tap], weight_far.at[tap], sems.at[tap])
+        copy.start()
+        copies.append(copy)
     bias_ref[...] = whole[0:1, 9 * C :]
+    for copy in copies:
+        copy.wait()
 
 
 def spread_sum_kernel(parts_ref, out_ref):
@@ -337,9 +343,17 @@
         parts,
     )
     whole = lax.all_to_all(sent, AXES, 0, 0, axis_index_groups=flats, tiled=True)
-    grad_w, grad_b = call(
-        unpack_kernel, (shape((9, C, C), f32), shape((1, C), f32)), [], 1, 1 << 18, whole
-    )
+    grad_w, grad_b = pl.pallas_call(
+        unpack_kernel,
+        out_shape=(shape((9, C, C), f32), shape((1, C), f32)),
+        in_specs=[pl.BlockSpec(memory_space=pltpu.VMEM)],
+        out_specs=(
+            pl.BlockSpec(memory_space=pltpu.HBM),
+            pl.BlockSpec(memory_space=pltpu.VMEM),
+        ),
+        scratch_shapes=[pltpu.VMEM((9, C, C), f32), pltpu.SemaphoreType.DMA((9,))],
+        compiler_params=pltpu.CompilerParams(vmem_limit_bytes=VMEM_LIMIT),
+    )(whole)
     return grad_input[:, None], grad_w, grad_b.reshape(C)
 
 

time: 81.1 us -> 81.6 us (level)
    pallas_call x0 -> x1, Pallas kernels: none -> 1.38 us  [on_device(): pl.pallas_call(unpack_kernel, out_shape=(shape((9, C, C), f32), shape((1,...]
    pallas_call x8 -> x7, Pallas kernels: 7.64 us -> 6.79 us  [call(): pl.pallas_call(kernel, out_shape=outs, in_specs=[pl.BlockSpec(memory_spac...]
where the time goes in v13:
time: 81.6 us; the launch traced here: 81.3 us
  blocking collectives  37.3 us (46%)
  starting transfers between devices  33.3 us (41%)
  Pallas kernels  8.17 us (10%)
  waiting for transfers between devices  1.76 us (2%)
    ppermute x1, starting transfers between devices, on_device(): other = lax.ppermute(raw, 'zh', [(0, 1), (1, 0)])  16.3 us
    all_to_all x1, blocking collectives, on_device(): lax.all_to_all(field, AXES, 0, 0, axis_index_groups=crosses, tiled=True)  15.5 us
    all_to_all x1, starting transfers between devices, on_device(): lax.all_to_all(sent, AXES, 0, 0, axis_index_groups=columns, tiled=True)  12.9 us
    all_to_all x1, blocking collectives, on_device(): lax.all_to_all(sent, AXES, 0, 0, axis_index_groups=flats, tiled=True)  11.4 us
    all_to_all x1, blocking collectives, on_device(): lax.all_to_all(sums, AXES, 0, 0, axis_index_groups=flats, tiled=True)  10.5 us
    pallas_call x7, Pallas kernels, call(): pl.pallas_call(kernel, out_shape=outs, in_specs=[pl.BlockSpec(memory_spac...  6.79 us
    ppermute x1, starting transfers between devices, on_device(): halo = lax.ppermute(last, AXES, hops)  4.13 us
  transfers between devices with their start and end apart: 3, of which 2 were waited for; matrix products, arithmetic and copies ran while one was open for 0% of the time, Pallas kernels for 6%

profile of v13, /device:TPU:1, one launch (start us, length us, event | category | flops | bytes accessed | tf_op | source)
XLA Modules:
  0.0 81.3 jit_solution(6662847150704067403)
XLA Ops:
  0.6 16.3 %collective-permute-start = (bf16[64,4,128]{2,1,0:T(4,128)(2,1)}, bf16[64,4,128]{2,1,0:T(4,128)(2,1)S(1)}, u32[]{:S(2)}, u32[]{:S(2)}) collective-permute-start(bf16[64,4,128]{2,1,0:T(4,128)(2,1)} %bitcast.12), channel_id=1, source_target_pairs={{0,1},{1,0},{2,3},{3,2},{4,5},{5,4},{6,7},{7,6},{8,9},{9,8},{10,11... | collective-permute-start | bytes 196616 | tf_op jit(solution)/shard_map/ppermute | solution.py:236
  16.9 0.0 copy-start.1
  16.9 3.3 %shard_map.76 = (f32[32,64,128]{2,1,0:T(8,128)S(1)}, bf16[4096,256]{1,0:T(8,128)(2,1)S(1)}, f32[8,128]{1,0:T(8,128)S(1)}) custom-call(s32[1]{0:T(128)} %bitcast.half_ref, f32[1,9]{1,0:T(1,128)} %bitcast.16, f32[1,64]{1,0:T(1,128)} %bitcast.17, bf16[64,32,128]{2,1,0:T(8,128)(2,1)} %bitcast.15, bf16[9,64,64]{2,1,0:T(8,128)(2,1)} %weight_ref.1), custom_call_target="tpu_custom_call" | custom-call | flops 19327352832 | bytes 134217728 | tf_op jit(solution)/shard_map/pallas_call | solution.py:219
  20.2 0.0 collective-permute-done.other_ref
  20.2 0.0 copy-done.1
  20.2 0.1 shard_map.77
  20.3 4.1 %collective-permute-start.1 = (bf16[2,64,128]{2,1,0:T(8,128)(2,1)S(1)}, bf16[2,64,128]{2,1,0:T(8,128)(2,1)S(1)}, u32[]{:S(2)}, u32[]{:S(2)}) collective-permute-start(bf16[2,64,128]{2,1,0:T(8,128)(2,1)S(1)} %get-tuple-element.24), channel_id=1, source_target_pairs={{0,32},{2,34},{4,36},{6,38},{8,40},{10,42},{12,44},{14,46},{16,48}... | collective-permute-start | bytes 98312 | tf_op jit(solution)/shard_map/ppermute | solution.py:276
  24.4 1.0 %collective-permute-done.1.halo_ref = bf16[2,64,128]{2,1,0:T(8,128)(2,1)S(1)} collective-permute-done((bf16[2,64,128]{2,1,0:T(8,128)(2,1)S(1)}, bf16[2,64,128]{2,1,0:T(8,128)(2,1)S(1)}, u32[]{:S(2)}, u32[]{:S(2)}) %collective-permute-start.1) | collective-permute-done | bytes 32800 | tf_op jit(solution)/shard_map/ppermute | solution.py:276
  25.4 0.1 shard_map.78
  25.5 15.5 %all_to_all.20 = bf16[16,2,64,128]{3,2,1,0:T(8,128)(2,1)S(1)} all-to-all(bf16[16,2,64,128]{3,2,1,0:T(8,128)(2,1)S(1)} %shard_map.78), channel_id=1, replica_groups={{20,22,16,18,28,30,24,26,4,6,0,2,12,14,8,10},{21,23,17,19,29,31,25,27,5..., dimensions={0} | all-to-all | bytes 1048576 | tf_op jit(solution)/shard_map/all_to_all | solution.py:294
  41.0 0.0 copy-start
  41.0 0.8 shard_map.79
  41.8 10.5 %all_to_all.21.parts_ref = f32[32,2,640]{2,1,0:T(2,128)S(1)} all-to-all(f32[32,2,640]{2,1,0:T(2,128)S(1)} %get-tuple-element.27), channel_id=1, replica_groups={{52,54,48,50,60,62,56,58,36,38,32,34,44,46,40,42,20,22,16,18,28,30,24,2..., dimensions={0} | all-to-all | bytes 327680 | tf_op jit(solution)/shard_map/all_to_all | solution.py:322
  52.2 0.7 shard_map.80
  52.9 12.9 %all-to-all-start.2 = ((bf16[16,2,640]{2,1,0:T(2,128)(2,1)}), bf16[16,2,640]{2,1,0:T(2,128)(2,1)S(1)}, u32[]{:S(2)}, u32[]{:S(2)}) async-start(bf16[16,2,640]{2,1,0:T(2,128)(2,1)} %shard_map.80), calls=%async_computation.2 | async-start | bytes 81920 | tf_op jit(solution)/shard_map/all_to_all | solution.py:334
  65.8 0.0 copy-done
  65.8 1.8 %shard_map.81 = bf16[64,32,128]{2,1,0:T(8,128)(2,1)} custom-call(bf16[32,64,128]{2,1,0:T(8,128)(2,1)S(1)} %get-tuple-element.28.grad_ref, bf16[32,64,128]{2,1,0:T(8,128)(2,1)S(1)} %bitcast.11, bf16[9,64,64]{2,1,0:T(8,128)(2,1)S(1)} %copy-done), custom_call_target="tpu_custom_call" | custom-call | flops 301989888 | bytes 2097152 | tf_op jit(solution)/shard_map/pallas_call | solution.py:219
  67.6 0.8 all-to-all-done.2.a
  68.4 0.1 shard_map.82
  68.5 11.4 %all_to_all.22.whole_ref = bf16[32,2,640]{2,1,0:T(2,128)(2,1)S(1)} all-to-all(bf16[32,2,640]{2,1,0:T(2,128)(2,1)S(1)} %shard_map.82), channel_id=1, replica_groups={{52,54,48,50,60,62,56,58,36,38,32,34,44,46,40,42,20,22,16,18,28,30,24,2..., dimensions={0} | all-to-all | bytes 163840 | tf_op jit(solution)/shard_map/all_to_all | solution.py:345
  79.9 1.4 %shard_map.83 = (f32[9,64,64]{2,1,0:T(8,128)}, f32[1,64]{1,0:T(1,128)}) custom-call(bf16[32,2,640]{2,1,0:T(2,128)(2,1)S(1)} %all_to_all.22.whole_ref), custom_call_target="tpu_custom_call" | custom-call | tf_op jit(solution)/shard_map/pallas_call | solution.py:346
Async XLA Ops:
  0.6 19.6 %collective-permute-start = (bf16[64,4,128]{2,1,0:T(4,128)(2,1)}, bf16[64,4,128]{2,1,0:T(4,128)(2,1)S(1)}, u32[]{:S(2)}, u32[]{:S(2)}) collective-permute-start(bf16[64,4,128]{2,1,0:T(4,128)(2,1)} %bitcast.12), channel_id=1, source_target_pairs={{0,1},{1,0},{2,3},{3,2},{4,5},{5,4},{6,7},{7,6},{8,9},{9,8},{10,11... | collective-permute-start | bytes 196616 | tf_op jit(solution)/shard_map/ppermute | solution.py:236
  16.9 3.3 %copy-start.1 = (bf16[64,4,1,128]{3,1,2,0:T(4,128)(2,1)S(1)}, bf16[64,4,1,128]{3,1,2,0:T(4,128)(2,1)}, u32[]{:S(2)}) copy-start(bf16[64,4,1,128]{3,1,2,0:T(4,128)(2,1)} %param.6) | copy-start | bytes 196612
  20.3 5.1 %collective-permute-start.1 = (bf16[2,64,128]{2,1,0:T(8,128)(2,1)S(1)}, bf16[2,64,128]{2,1,0:T(8,128)(2,1)S(1)}, u32[]{:S(2)}, u32[]{:S(2)}) collective-permute-start(bf16[2,64,128]{2,1,0:T(8,128)(2,1)S(1)} %get-tuple-element.24), channel_id=1, source_target_pairs={{0,32},{2,34},{4,36},{6,38},{8,40},{10,42},{12,44},{14,46},{16,48}... | collective-permute-start | bytes 98312 | tf_op jit(solution)/shard_map/ppermute | solution.py:276
  41.0 24.8 %copy-start = (bf16[9,64,64]{2,1,0:T(8,128)(2,1)S(1)}, bf16[9,64,64]{2,1,0:T(8,128)(2,1)}, u32[]{:S(2)}) copy-start(bf16[9,64,64]{2,1,0:T(8,128)(2,1)} %weight_ref.1) | copy-start | bytes 221188
  52.9 15.5 %all-to-all-start.2 = ((bf16[16,2,640]{2,1,0:T(2,128)(2,1)}), bf16[16,2,640]{2,1,0:T(2,128)(2,1)S(1)}, u32[]{:S(2)}, u32[]{:S(2)}) async-start(bf16[16,2,640]{2,1,0:T(2,128)(2,1)} %shard_map.80), calls=%async_computation.2 | async-start | bytes 81920 | tf_op jit(solution)/shard_map/all_to_all | solution.py:334
